TPU v7x, 32 devices: a whole 2x2x4 slice. The times are simulated.
32 devices in a mesh: gx: 8 (over z, x), yz: 4 (over y, core).
Axes of the slice: x: 2, y: 2, z: 4, core: 2. Of those that a mesh axis runs over, the one named last changes fastest.
Arguments:
- coarse_state: float32 [21, 48, 24, 384], P(None, 'gx', 'yz')
- fine_state: bfloat16 [128, 21, 512], P(('gx', 'yz')), may hold values from -6 to 6
- diffusion: float32 [21], replicated, may hold values from 0.005 to 0.04
- rate: float32 [21, 21], replicated, may hold values from -0.625 to 0.625
- box_pos: int32 [8, 4, 2], P('gx', 'yz'), may hold values from 0 to 63, as said below
- box_owner: int32 [8, 4, 2], P('gx', 'yz'), may hold values from 0 to 3, as said below
Outputs:
- coarse_next: float32 [21, 48, 24, 384], P(None, 'gx', 'yz')
- fine_next: bfloat16 [128, 21, 512], P(('gx', 'yz'))
Inputs may be any that keep to these rules, and one draw needn't show every extreme that they name: `box_pos`: the 2 positions of one device are distinct. `box_owner`: the 2 boxes of one device go to distinct owners of its slab; in every slab some owner receives a box from every device of the slab.
All inputs are finite; a program needn't handle non-finite values.
Results may differ from a plain program's by a relative error of at most 0.0025.
Values may be sent and summed in bfloat16 or wider, within the bound.
No kernel may reach another device: no remote copies, remote signals or barrier semaphores. Data moves between devices by JAX's collectives and lax.ppermute only.
A program may use at most 64 MiB of HBM per device.

v0:
```python
import jax
import jax.numpy as jnp
from jax import lax
from jax.sharding import PartitionSpec as P


def with_halo(array, sides, width):
    for axis, dim in sides:
        count, length = (lax.axis_size(axis), array.shape[dim])
        up = [(i, (i + 1) % count) for i in range(count)]
        down = [(j, i) for i, j in up]
        last = lax.slice_in_dim(array, length - width, length, axis=dim)
        initial = lax.slice_in_dim(array, 0, width, axis=dim)
        before = lax.ppermute(last, axis, up)
        after = lax.ppermute(initial, axis, down)
        array = jnp.concatenate([before, array, after], axis=dim)
    return array


def react(rate, field):
    return jnp.einsum("st,txyz->sxyz", rate, field, precision=lax.Precision.HIGHEST)


def cycle_faces(patch):
    return jnp.stack(
        [
            patch[:, 0, 1:-1, 1:-1],
            patch[:, -1, 1:-1, 1:-1],
            patch[:, 1:-1, 0, 1:-1],
            patch[:, 1:-1, -1, 1:-1],
            patch[:, 1:-1, 1:-1, 0],
            patch[:, 1:-1, 1:-1, -1],
        ],
        axis=1,
    )


def inner_faces(patch):
    return jnp.stack(
        [
            patch[:, 1, 1:-1, 1:-1],
            patch[:, -2, 1:-1, 1:-1],
            patch[:, 1:-1, 1, 1:-1],
            patch[:, 1:-1, -2, 1:-1],
            patch[:, 1:-1, 1:-1, 1],
            patch[:, 1:-1, 1:-1, -2],
        ],
        axis=1,
    )


def widen(face):
    return jnp.repeat(jnp.repeat(face, 2, axis=1), 2, axis=2)


def fine_box(fine, ghost_old, ghost_new, diffusion, rate):
    species = fine.shape[0]
    half = ghost_old.shape[2]
    edge = 2 * half
    plane = edge * edge
    cells = plane * edge
    field = fine
    coef = diffusion[:, None]
    index = jnp.arange(cells, dtype=jnp.int32)[None, :]
    xpos = index // plane
    ypos = index // edge % edge
    zpos = index % edge
    shapes = [
        (species, 1, edge, edge),
        (species, 1, edge, edge),
        (species, edge, 1, edge),
        (species, edge, 1, edge),
        (species, edge, edge, 1),
        (species, edge, edge, 1),
    ]
    flux_sum = jnp.zeros_like(ghost_old)
    for sub in range(2):
        ghost = ghost_old if sub == 0 else 0.5 * (ghost_old + ghost_new)

        def spread(face):
            wide = widen(ghost[:, face]).reshape(shapes[face])
            return jnp.broadcast_to(wide, (species, edge, edge, edge)).reshape(species, cells)

        lap = jnp.where(xpos == 0, spread(0), jnp.roll(field, plane, 1))
        lap = lap + jnp.where(xpos == edge - 1, spread(1), jnp.roll(field, -plane, 1))
        lap = lap + jnp.where(ypos == 0, spread(2), jnp.roll(field, edge, 1))
        lap = lap + jnp.where(ypos == edge - 1, spread(3), jnp.roll(field, -edge, 1))
        lap = lap + jnp.where(zpos == 0, spread(4), jnp.roll(field, 1, 1))
        lap = lap + jnp.where(zpos == edge - 1, spread(5), jnp.roll(field, -1, 1))
        lap = lap - 6.0 * field
        cube = field.reshape(species, edge, edge, edge)
        bounds = jnp.stack(
            [
                cube[:, 0],
                cube[:, -1],
                cube[:, :, 0],
                cube[:, :, -1],
                cube[:, :, :, 0],
                cube[:, :, :, -1],
            ],
            axis=1,
        )
        pooled = bounds.reshape(species, 6, half, 2, half, 2).sum(axis=(3, 5))
        flux_sum = flux_sum + diffusion[:, None, None, None] * (ghost - 0.25 * pooled)
        field = (
            field + 2.0 * coef * lap + 0.5 * jnp.dot(rate, field, precision=lax.Precision.HIGHEST)
        )
    average = field.reshape(species, half, 2, half, 2, half, 2).mean(axis=(2, 4, 6))
    return (field, flux_sum, average)


def correct(patch_new, patch_old, flux_sum, average, diffusion):
    fix = (
        diffusion[:, None, None, None] * (cycle_faces(patch_old) - inner_faces(patch_old))
        - flux_sum
    )
    out = patch_new.at[:, 0, 1:-1, 1:-1].add(fix[:, 0])
    out = out.at[:, -1, 1:-1, 1:-1].add(fix[:, 1])
    out = out.at[:, 1:-1, 0, 1:-1].add(fix[:, 2])
    out = out.at[:, 1:-1, -1, 1:-1].add(fix[:, 3])
    out = out.at[:, 1:-1, 1:-1, 0].add(fix[:, 4])
    out = out.at[:, 1:-1, 1:-1, -1].add(fix[:, 5])
    return out.at[:, 1:-1, 1:-1, 1:-1].set(average)


def local(coarse_state, fine_state, diffusion, rate, box_pos, box_owner):
    species = coarse_state.shape[0]
    width = coarse_state.shape[1]
    half = width - 2
    facets = 6 * half * half
    count = lax.axis_size("yz")
    coef = diffusion[:, None, None, None]
    padded = with_halo(coarse_state.astype(jnp.bfloat16), (("gx", 1), ("yz", 2)), 1).astype(
        coarse_state.dtype
    )
    lap = padded[:, 2:, 1:-1] + padded[:, :-2, 1:-1] + padded[:, 1:-1, 2:] + padded[:, 1:-1, :-2]
    lap = lap + jnp.roll(coarse_state, 1, 3) + jnp.roll(coarse_state, -1, 3) - 6.0 * coarse_state
    advanced = coarse_state + coef * lap + react(rate, coarse_state)
    places = box_pos[0, 0]
    owners = box_owner[0, 0]
    boxes = owners.shape[0]
    zero = jnp.zeros((), jnp.int32)
    corners = [(zero, zero, zero, places[i] * width) for i in range(boxes)]
    olds = [
        lax.dynamic_slice(coarse_state, corners[i], (species, width, width, width))
        for i in range(boxes)
    ]
    news = [
        lax.dynamic_slice(advanced, corners[i], (species, width, width, width))
        for i in range(boxes)
    ]
    select = (owners[:, None] == jnp.arange(count, dtype=jnp.int32)[None, :]).astype(jnp.float32)
    ghosts = jnp.stack(
        [jnp.stack([cycle_faces(olds[i]), cycle_faces(news[i])]) for i in range(boxes)]
    )
    ghosts = ghosts.reshape(boxes, 2, species, facets)
    outgoing = jnp.einsum("io,iabc->oabc", select, ghosts, precision=lax.Precision.HIGHEST)
    flags = jnp.sum(select, axis=0)[:, None]
    arrived, present = (
        lax.all_to_all(
            outgoing.astype(jnp.bfloat16), "yz", split_axis=0, concat_axis=0, tiled=True
        ).astype(outgoing.dtype),
        lax.all_to_all(
            flags.astype(jnp.bfloat16), "yz", split_axis=0, concat_axis=0, tiled=True
        ).astype(flags.dtype),
    )

    def one_slot(items):
        fine, ghost, flag = items

        def work(unused):
            field, flux_sum, average = fine_box(
                fine.astype(jnp.float32),
                ghost[0].reshape(species, 6, half, half),
                ghost[1].reshape(species, 6, half, half),
                diffusion,
                rate,
            )
            packet = jnp.concatenate(
                [flux_sum.reshape(species, facets), average.reshape(species, half**3)], axis=1
            )
            return (field.astype(jnp.bfloat16), packet)

        def skip(unused):
            return (
                jnp.zeros(fine.shape, jnp.bfloat16),
                jnp.zeros((species, facets + half**3), jnp.float32),
            )

        return lax.cond(flag[0] > 0.5, work, skip, None)

    fine_next, packets = lax.map(one_slot, (fine_state, arrived, present))
    returned = lax.all_to_all(
        packets.astype(jnp.bfloat16), "yz", split_axis=0, concat_axis=0, tiled=True
    ).astype(packets.dtype)
    mine = jnp.einsum("io,oac->iac", select, returned, precision=lax.Precision.HIGHEST)
    fluxes = mine[:, :, :facets].reshape(boxes, species, 6, half, half)
    averages = mine[:, :, facets:].reshape(boxes, species, half, half, half)
    coarse_next = advanced
    for i in range(boxes):
        patch = correct(news[i], olds[i], fluxes[i], averages[i], diffusion)
        coarse_next = lax.dynamic_update_slice(coarse_next, patch, corners[i])
    return (coarse_next, fine_next)


def solution(mesh):
    in_specs = (
        P(None, "gx", "yz", None),
        P(("gx", "yz"), None, None),
        P(),
        P(),
        P("gx", "yz", None),
        P("gx", "yz", None),
    )
    out_specs = (P(None, "gx", "yz", None), P(("gx", "yz"), None, None))
    return jax.shard_map(local, mesh=mesh, in_specs=in_specs, out_specs=out_specs, check_vma=False)
```

profile of v0, /device:TPU:0, one launch (start us, length us, event | category | flops | bytes accessed | tf_op | source)
XLA Modules:
  0.0 182.3 jit_solution(15159520655337657296)
XLA Ops:
  2.9 6.0 %collective-permute-start.1 = (bf16[21,1,6,384]{3,0,2,1:T(8,128)(2,1)}, bf16[21,1,6,384]{3,0,2,1:T(8,128)(2,1)}, u32[]{:S(2)}, u32[]{:S(2)}) collective-permute-start(bf16[21,1,6,384]{3,0,2,1:T(8,128)(2,1)} %get-tuple-element.432), channel_id=1, source_target_pairs={{4,0},{8,4},{12,8},{16,12},{20,16},{24,20},{28,24},{0,28},{5,1},{9... | collective-permute-start | bytes 290312 | tf_op jit(solution)/shard_map/ppermute | solution.py:15
  9.7 3.1 %all-to-all-start = ((bf16[4,1,1]{2,1,0:T(2,128)(2,1)}), bf16[4,1,1]{2,1,0:T(2,128)(2,1)S(1)}, u32[]{:S(2)}, u32[]{:S(2)}) async-start(bf16[4,1,1]{2,1,0:T(2,128)(2,1)} %copy.541), calls=%async_computation | async-start | bytes 4096 | tf_op jit(solution)/shard_map/all_to_all | solution.py:163
  20.6 2.2 %copy.643 = f32[21,4,4,1]{2,0,1,3:T(8,128)} copy(f32[21,4,4,1]{3,0,2,1:T(8,128)} %get-tuple-element.401) | data formatting | bytes 2688
  25.2 2.2 %copy.644 = f32[21,4,4,1]{2,0,1,3:T(8,128)} copy(f32[21,4,4,1]{3,0,2,1:T(8,128)} %get-tuple-element.400) | data formatting | bytes 2688
  32.6 1.8 copy.556
  35.3 2.2 %copy.631 = f32[21,4,4,1]{2,0,1,3:T(8,128)} copy(f32[21,4,4,1]{3,0,2,1:T(8,128)} %get-tuple-element.404) | data formatting | bytes 2688
  39.1 2.2 %copy.632 = f32[21,4,4,1]{2,0,1,3:T(8,128)} copy(f32[21,4,4,1]{3,0,2,1:T(8,128)} %get-tuple-element.403) | data formatting | bytes 2688
  44.2 1.8 copy.542
  48.5 2.2 %copy.649 = f32[21,4,4,1]{2,0,1,3:T(8,128)} copy(f32[21,4,4,1]{3,0,2,1:T(8,128)} %get-tuple-element.406) | data formatting | bytes 2688
  50.7 2.2 %copy.650 = f32[21,4,4,1]{2,0,1,3:T(8,128)} copy(f32[21,4,4,1]{3,0,2,1:T(8,128)} %get-tuple-element.399) | data formatting | bytes 2688
  54.6 2.2 %copy.637 = f32[21,4,4,1]{2,0,1,3:T(8,128)} copy(f32[21,4,4,1]{3,0,2,1:T(8,128)} %get-tuple-element.402) | data formatting | bytes 2688
  64.6 1.8 collective-permute-start.3
  67.0 3.4 %collective-permute-done.3 = bf16[21,8,1,384]{3,0,2,1:T(8,128)(2,1)S(1)} collective-permute-done((bf16[21,8,1,384]{3,0,2,1:T(8,128)(2,1)S(1)}, bf16[21,8,1,384]{3,0,2,1:T(8,128)(2,1)S(1)}, u32[]{:S(2)}, u32[]{:S(2)}) %collective-permute-start.3) | collective-permute-done | bytes 129056 | tf_op jit(solution)/shard_map/ppermute | solution.py:15
  72.7 1.8 convolution_add_fusion
  81.3 3.5 %all-to-all-start.1 = ((bf16[4,2,21,96]{3,1,2,0:T(2,128)(2,1)}), bf16[4,2,21,96]{3,1,2,0:T(2,128)(2,1)S(1)}, u32[]{:S(2)}, u32[]{:S(2)}) async-start(bf16[4,2,21,96]{3,1,2,0:T(2,128)(2,1)} %copy.566), calls=%async_computation.1 | async-start | bytes 86016 | tf_op jit(solution)/shard_map/all_to_all | solution.py:160
  84.9 3.7 %all-to-all-done.1 = bf16[4,2,21,96]{3,1,2,0:T(2,128)(2,1)S(1)} async-done(((bf16[4,2,21,96]{3,1,2,0:T(2,128)(2,1)}), bf16[4,2,21,96]{3,1,2,0:T(2,128)(2,1)S(1)}, u32[]{:S(2)}, u32[]{:S(2)}) %all-to-all-start.1) | async-done | bytes 32288 | tf_op jit(solution)/shard_map/all_to_all | solution.py:160
  88.7 14.3 %while.26 = (s32[]{:T(128)}, bf16[4,21,512]{2,1,0:T(8,128)(2,1)S(1)}, bf16[4,21,160]{2,1,0:T(8,128)(2,1)}, f32[4,1]{0,1:T(1,128)S(1)}, bf16[4,21,512]{1,2,0:T(8,...) while((s32[]{:T(128)}, ...), condition=%wide.region_7.8_spmd, body=%wide.region_1.7_spmd.sunk | while | flops 6025658 | bytes 5798595 | solution.py:192
  95.9 6.5 %conditional.2 = (bf16[1,21,512]{2,1,0:T(8,128)(2,1)S(1)}, bf16[1,21,160]{2,1,0:T(8,128)(2,1)S(1)}) conditional(s32[]{:T(128)} %bitcast.233, () %tuple.183, (bf16[4,21,512]{1,2,0:T(8,128)(2,1)}, s32[]{:T(128)}, f32[21]{0:T(128)S(1)}, f32[4,2,21,96]{2,3,1,0:T(8,128)S(1)}, f32[21,21]{1,0:T(8,128)S(1)}) %tuple.184), branch_computations={%region_2.2_spmd, %region_3.6_spmd} | conditional | flops 6025654 | bytes 5729764 | solution.py:190
  103.0 20.2 %all-to-all-start.2 = ((bf16[4,21,160]{2,1,0:T(8,128)(2,1)}), bf16[4,21,160]{2,1,0:T(8,128)(2,1)S(1)}, u32[]{:S(2)}, u32[]{:S(2)}) async-start(bf16[4,21,160]{2,1,0:T(8,128)(2,1)} %get-tuple-element.263), calls=%async_computation.2 | async-start | bytes 98304 | tf_op jit(solution)/shard_map/all_to_all | solution.py:193
  124.6 2.7 %all-to-all-done.2 = bf16[4,21,160]{2,1,0:T(8,128)(2,1)S(1)} async-done(((bf16[4,21,160]{2,1,0:T(8,128)(2,1)}), bf16[4,21,160]{2,1,0:T(8,128)(2,1)S(1)}, u32[]{:S(2)}, u32[]{:S(2)}) %all-to-all-start.2) | async-done | bytes 26912 | tf_op jit(solution)/shard_map/all_to_all | solution.py:193
  139.9 2.6 %scatter.6 = f32[21,6,6,6]{2,0,1,3:T(8,128)S(1)} dynamic-update-slice(f32[21,6,6,6]{2,0,1,3:T(8,128)S(1)} %scatter-add.49, f32[21,4,4,4]{2,0,1,3:T(8,128)S(1)} %copy.579, s32[]{:T(128)} %constant.566.clone.1, s32[]{:T(128)} %constant.569.clone.1, s32[]{:T(128)} %constant.569.clone.1, s32[]{:T(128)} %constant.569.clone.1) | dynamic-update-slice | bytes 10756 | tf_op jit(solution)/shard_map/scatter | solution.py:123
  143.6 12.3 %dynamic_update_slice.14 = f32[21,6,6,384]{3,0,2,1:T(8,128)S(1)} dynamic-update-slice(f32[21,6,6,384]{3,0,2,1:T(8,128)S(1)} %copy-done.3, f32[21,6,6,6]{3,0,2,1:T(8,128)S(1)} %copy.580, s32[]{:T(128)} %constant.566.clone.1, s32[]{:T(128)} %constant.566.clone.1, s32[]{:T(128)} %constant.566.clone.1, s32[]{:T(128)S(6)} %select_n.162) | dynamic-update-slice | bytes 36292 | tf_op jit(solution)/shard_map/dynamic_update_slice | solution.py:202
  165.2 2.6 %scatter.9 = f32[21,6,6,6]{2,0,1,3:T(8,128)S(1)} dynamic-update-slice(f32[21,6,6,6]{2,0,1,3:T(8,128)S(1)} %scatter-add.59, f32[21,4,4,4]{2,0,1,3:T(8,128)S(1)} %copy.596, s32[]{:T(128)} %constant.566.clone.1, s32[]{:T(128)} %constant.569.clone.1, s32[]{:T(128)} %constant.569.clone.1, s32[]{:T(128)} %constant.569.clone.1) | dynamic-update-slice | bytes 10756 | tf_op jit(solution)/shard_map/scatter | solution.py:123
  168.9 12.3 %dynamic_update_slice.15 = f32[21,6,6,384]{3,0,2,1:T(8,128)S(1)} dynamic-update-slice(f32[21,6,6,384]{3,0,2,1:T(8,128)S(1)} %dynamic_update_slice.14, f32[21,6,6,6]{3,0,2,1:T(8,128)S(1)} %copy.597, s32[]{:T(128)} %constant.566.clone.1, s32[]{:T(128)} %constant.566.clone.1, s32[]{:T(128)} %constant.566.clone.1, s32[]{:T(128)S(6)} %select_n.164) | dynamic-update-slice | bytes 36292 | tf_op jit(solution)/shard_map/dynamic_update_slice | solution.py:202
  (318 shorter events, 81.5 us)
Async XLA Ops:
  0.6 12.2 %copy-start = (f32[21,6,6,384]{3,0,2,1:T(8,128)S(1)}, f32[21,6,6,384]{3,0,2,1:T(8,128)}, u32[]{:S(2)}) copy-start(f32[21,6,6,384]{3,0,2,1:T(8,128)} %param.38) | copy-start | bytes 3483652
  0.6 8.2 %copy-start.17 = (s32[1,1,2]{2,1,0:T(1,128)S(1)}, s32[1,1,2]{2,1,0:T(1,128)}, u32[]{:S(2)}) copy-start(s32[1,1,2]{2,1,0:T(1,128)} %param.43) | copy-start | bytes 28
  2.9 60.8 %collective-permute-start.1 = (bf16[21,1,6,384]{3,0,2,1:T(8,128)(2,1)}, bf16[21,1,6,384]{3,0,2,1:T(8,128)(2,1)}, u32[]{:S(2)}, u32[]{:S(2)}) collective-permute-start(bf16[21,1,6,384]{3,0,2,1:T(8,128)(2,1)} %get-tuple-element.432), channel_id=1, source_target_pairs={{4,0},{8,4},{12,8},{16,12},{20,16},{24,20},{28,24},{0,28},{5,1},{9... | collective-permute-start | bytes 290312 | tf_op jit(solution)/shard_map/ppermute | solution.py:15
  8.9 54.9 %collective-permute-start = (bf16[21,1,6,384]{3,0,2,1:T(8,128)(2,1)}, bf16[21,1,6,384]{3,0,2,1:T(8,128)(2,1)}, u32[]{:S(2)}, u32[]{:S(2)}) collective-permute-start(bf16[21,1,6,384]{3,0,2,1:T(8,128)(2,1)} %get-tuple-element.431), channel_id=1, source_target_pairs={{0,4},{4,8},{8,12},{12,16},{16,20},{20,24},{24,28},{28,0},{1,5},{5... | collective-permute-start | bytes 290312 | tf_op jit(solution)/shard_map/ppermute | solution.py:14
  9.7 71.6 %all-to-all-start = ((bf16[4,1,1]{2,1,0:T(2,128)(2,1)}), bf16[4,1,1]{2,1,0:T(2,128)(2,1)S(1)}, u32[]{:S(2)}, u32[]{:S(2)}) async-start(bf16[4,1,1]{2,1,0:T(2,128)(2,1)} %copy.541), calls=%async_computation | async-start | bytes 4096 | tf_op jit(solution)/shard_map/all_to_all | solution.py:163
  14.3 1.0 copy-start.16
  14.3 3.0 %copy-start.14 = (bf16[4,21,512]{2,0,1:T(4,128)(2,1)S(1)}, bf16[4,21,512]{2,0,1:T(4,128)(2,1)}, u32[]{:S(2)}) copy-start(bf16[4,21,512]{2,0,1:T(4,128)(2,1)} %param.39) | copy-start | bytes 258052
  58.1 8.3 %copy-start.12 = (f32[21,4,4,1]{2,0,1,3:T(8,128)S(1)}, f32[21,4,4,1]{2,0,1,3:T(8,128)}, u32[]{:S(2)}) copy-start(f32[21,4,4,1]{2,0,1,3:T(8,128)} %copy.637) | copy-start | bytes 4036
  64.6 5.8 %collective-permute-start.3 = (bf16[21,8,1,384]{3,0,2,1:T(8,128)(2,1)S(1)}, bf16[21,8,1,384]{3,0,2,1:T(8,128)(2,1)S(1)}, u32[]{:S(2)}, u32[]{:S(2)}) collective-permute-start(bf16[21,8,1,384]{3,0,2,1:T(8,128)(2,1)S(1)} %get-tuple-element.430), channel_id=1, source_target_pairs={{1,0},{2,1},{3,2},{0,3},{5,4},{6,5},{7,6},{4,7},{9,8},{10,9},{11,1... | collective-permute-start | bytes 387080 | tf_op jit(solution)/shard_map/ppermute | solution.py:15
  66.3 5.1 %collective-permute-start.2 = (bf16[21,8,1,384]{3,0,2,1:T(8,128)(2,1)S(1)}, bf16[21,8,1,384]{3,0,2,1:T(8,128)(2,1)S(1)}, u32[]{:S(2)}, u32[]{:S(2)}) collective-permute-start(bf16[21,8,1,384]{3,0,2,1:T(8,128)(2,1)S(1)} %get-tuple-element.429), channel_id=1, source_target_pairs={{0,1},{1,2},{2,3},{3,0},{4,5},{5,6},{6,7},{7,4},{8,9},{9,10},{10,1... | collective-permute-start | bytes 387080 | tf_op jit(solution)/shard_map/ppermute | solution.py:14
  67.0 5.7 %copy-start.1 = (f32[21,6,6,383]{3,0,2,1:T(8,128)S(1)}, f32[21,6,6,383]{3,0,2,1:T(8,128)}, u32[]{:S(2)}) copy-start(f32[21,6,6,383]{3,0,2,1:T(8,128)} %get-tuple-element.426) | copy-start | bytes 3474580
  67.0 5.7 %copy-start.5 = (f32[21,6,6,1]{3,0,2,1:T(8,128)S(1)}, f32[21,6,6,1]{3,0,2,1:T(8,128)}, u32[]{:S(2)}) copy-start(f32[21,6,6,1]{3,0,2,1:T(8,128)} %get-tuple-element.427) | copy-start | bytes 9076
  67.0 5.7 %copy-start.6 = (f32[21,6,6,1]{3,0,2,1:T(8,128)S(1)}, f32[21,6,6,1]{3,0,2,1:T(8,128)}, u32[]{:S(2)}) copy-start(f32[21,6,6,1]{3,0,2,1:T(8,128)} %get-tuple-element.428) | copy-start | bytes 9076
  67.0 5.7 %copy-start.7 = (f32[21,21]{1,0:T(8,128)S(1)}, f32[21,21]{1,0:T(8,128)}, u32[]{:S(2)}) copy-start(f32[21,21]{1,0:T(8,128)} %param.41) | copy-start | bytes 5296
  67.0 5.7 %copy-start.15 = (f32[21]{0:T(128)S(1)}, f32[21]{0:T(128)}, u32[]{:S(2)}) copy-start(f32[21]{0:T(128)} %param.40) | copy-start | bytes 256
  74.5 1.1 copy-start.2
  78.4 10.3 %copy-start.13 = (bf16[4,21,512]{2,1,0:T(8,128)(2,1)S(1)}, bf16[4,21,512]{2,1,0:T(8,128)(2,1)}, u32[]{:S(2)}) copy-start(bf16[4,21,512]{2,1,0:T(8,128)(2,1)} %custom-call.8) | copy-start | bytes 258052
  81.3 7.2 %all-to-all-start.1 = ((bf16[4,2,21,96]{3,1,2,0:T(2,128)(2,1)}), bf16[4,2,21,96]{3,1,2,0:T(2,128)(2,1)S(1)}, u32[]{:S(2)}, u32[]{:S(2)}) async-start(bf16[4,2,21,96]{3,1,2,0:T(2,128)(2,1)} %copy.566), calls=%async_computation.1 | async-start | bytes 86016 | tf_op jit(solution)/shard_map/all_to_all | solution.py:160
  88.7 34.6 %copy-start.11 = (f32[21,4,4,1]{2,0,1,3:T(8,128)S(1)}, f32[21,4,4,1]{2,0,1,3:T(8,128)}, u32[]{:S(2)}) copy-start(f32[21,4,4,1]{2,0,1,3:T(8,128)} %copy.638) | copy-start | bytes 4036
  103.0 26.8 %copy-start.8 = (f32[21,6,4,4]{3,0,2,1:T(8,128)S(1)}, f32[21,6,4,4]{3,0,2,1:T(8,128)}, u32[]{:S(2)}) copy-start(f32[21,6,4,4]{3,0,2,1:T(8,128)} %constant_dynamic-update-slice_fusion.14) | copy-start | bytes 24196
  103.0 26.8 %copy-start.9 = (f32[21,6,4,4]{3,0,2,1:T(8,128)S(1)}, f32[21,6,4,4]{3,0,2,1:T(8,128)}, u32[]{:S(2)}) copy-start(f32[21,6,4,4]{3,0,2,1:T(8,128)} %constant_dynamic-update-slice_fusion.32) | copy-start | bytes 24196
  103.0 24.3 %all-to-all-start.2 = ((bf16[4,21,160]{2,1,0:T(8,128)(2,1)}), bf16[4,21,160]{2,1,0:T(8,128)(2,1)S(1)}, u32[]{:S(2)}, u32[]{:S(2)}) async-start(bf16[4,21,160]{2,1,0:T(8,128)(2,1)} %get-tuple-element.263), calls=%async_computation.2 | async-start | bytes 98304 | tf_op jit(solution)/shard_map/all_to_all | solution.py:193
  128.8 3.1 %copy-start.3 = (f32[21,6,6,384]{3,0,2,1:T(8,128)S(1)}, f32[21,6,6,384]{3,0,2,1:T(8,128)}, u32[]{:S(2)}) copy-start(f32[21,6,6,384]{3,0,2,1:T(8,128)} %copy-done.2) | copy-start | bytes 3483652
  181.2 1.1 copy-start.4
  (1 other events, 0.7 us)
where the time goes:
time: 184 us; the launch traced here: 182 us
  local copies, waits for them, and re-layouts  117 us (64%)
  starting transfers between devices  34.6 us (19%)
  other arithmetic  11.1 us (6%)
  waiting for transfers between devices  10.8 us (6%)
  loops' own time  3.37 us (2%)
  matrix products  2.83 us (2%)
  between operations  2.46 us (1%)
    unnamed x71, local copies, waits for them, and re-layouts  34 us
    dynamic_update_slice x2, local copies, waits for them, and re-layouts, local(): coarse_next = lax.dynamic_update_slice(coarse_next, patch, corners[i])  24.6 us
    all_to_all x1, starting transfers between devices, local(): lax.all_to_all(packets.astype(jnp.bfloat16), 'yz', split_axis=0, concat_a...  20.2 us
    ppermute x2, starting transfers between devices, with_halo(): after = lax.ppermute(initial, axis, down)  7.75 us
    scatter x4, local copies, waits for them, and re-layouts, correct(): return out.at[:, 1:-1, 1:-1, 1:-1].set(average)  7.3 us
    another operation x12, local copies, waits for them, and re-layouts, cycle_faces(): jnp.stack([patch[:, 0, 1:-1, 1:-1], patch[:, -1, 1:-1, 1:-1], patch[:, 1:...  7.08 us
    another operation x6, local copies, waits for them, and re-layouts, inner_faces(): jnp.stack([patch[:, 1, 1:-1, 1:-1], patch[:, -2, 1:-1, 1:-1], patch[:, 1:...  4.95 us
  transfers between devices with their start and end apart: 7, of which 4 were waited for; matrix products, arithmetic and copies ran while one was open for 34% of the time, Pallas kernels for 0%

commit v1 on v0

v1 whole, which is shorter than its diff:
```python
import functools

import jax
import jax.numpy as jnp
import numpy as np
from jax import lax
from jax.experimental import pallas as pl
from jax.experimental.pallas import tpu as pltpu
from jax.sharding import PartitionSpec as P

F32 = jnp.float32
BF16 = jnp.bfloat16
LIMIT = 12 * 1024 * 1024
PATCH = 256
ORDER = 20_000_000


def padded(count, unit):
    return -(-count // unit) * unit


@functools.lru_cache(maxsize=None)
def tables(width, boxes):
    half = width - 2
    edge = 2 * half
    cells = width**3
    lanes = padded(cells, PATCH)
    fine = edge**3
    spread = np.zeros((lanes, fine), np.float32)
    average = np.zeros((fine, lanes), np.float32)
    halo = padded(boxes * 4 * half * half, 128)
    place = np.zeros((halo, lanes), np.float32)

    def cell(x, y, z):
        return (x * width + y) * width + z

    for number in range(6):
        axis, high = divmod(number, 2)
        others = [a for a in range(3) if a != axis]
        for r in range(half):
            for q in range(half):
                at = [0, 0, 0]
                at[axis] = width - 1 if high else 0
                at[others[0]] = r + 1
                at[others[1]] = q + 1
                here = cell(*at)
                for i in range(2):
                    for j in range(2):
                        pos = [0, 0, 0]
                        pos[axis] = edge - 1 if high else 0
                        pos[others[0]] = 2 * r + i
                        pos[others[1]] = 2 * q + j
                        spread[here, (pos[0] * edge + pos[1]) * edge + pos[2]] = 1.0
                if number < 4:
                    for box in range(boxes):
                        place[((box * 4 + number) * half + r) * half + q, here] = 1.0
    for x in range(edge):
        for y in range(edge):
            for z in range(edge):
                average[(x * edge + y) * edge + z, cell(x // 2 + 1, y // 2 + 1, z // 2 + 1)] = 0.125
    return dict(spread=spread, average=average, place=place, ghost=place @ spread)


def column(diffusion, stack):
    species = diffusion.shape[1]
    row = lax.broadcasted_iota(jnp.int32, (stack, species), 0)
    lane = lax.broadcasted_iota(jnp.int32, (stack, species), 1)
    return jnp.sum(jnp.where(row == lane, diffusion[...], 0.0), axis=1, keepdims=True)


def split(value):
    high = value.astype(BF16).astype(F32)
    return high, value - high


def parts(value):
    return jnp.concatenate(split(value), axis=0).astype(BF16)


def dot(a, b):
    return jnp.dot(a, b, preferred_element_type=F32)


def rows_dot(value, table):
    rows = value.shape[0]
    both = dot(parts(value), table)
    return both[:rows] + both[rows:]


GROUP = 5


def mixing(rate, scratch, stack, group):
    species = rate.shape[0]
    size = group * stack
    scratch[...] = jnp.zeros_like(scratch)
    high, low = split(rate[...])
    for b in range(group):
        at = b * stack
        for row, lane, part in ((at, at, high), (at, size + at, high), (size + at, at, low)):
            scratch[row : row + species, lane : lane + species] = part
    return scratch[: 2 * size, : 2 * size].astype(BF16)


def react(mix, fields):
    size = fields.shape[0]
    both = dot(mix, parts(fields))
    return both[:size] + both[size:]


def react_all(mix, fields):
    stack, depth = fields[0].shape
    made = [[] for _ in fields]

    def product(blocks):
        size = len(blocks[0])
        blank = [jnp.zeros_like(blocks[0][0])] * (GROUP - size)
        columns = [jnp.concatenate(block + blank, axis=0) for block in blocks]
        out = react(mix, jnp.concatenate(columns, axis=1))
        lanes = out.shape[1] // len(blocks)
        return [
            [out[b * stack : (b + 1) * stack, n * lanes : (n + 1) * lanes] for b in range(size)]
            for n in range(len(blocks))
        ]

    for lane in range(0, depth, 256):
        if lane + 256 <= depth:
            for at in range(0, len(fields), GROUP):
                block = [f[:, lane : lane + 256] for f in fields[at : at + GROUP]]
                for b, value in enumerate(product([block])[0]):
                    made[at + b].append(value)
        else:
            half = -(-len(fields) // 2)
            blocks = [[f[:, lane:] for f in part] for part in (fields[:half], fields[half:])]
            blocks[1] += [jnp.zeros_like(blocks[0][0])] * (half - len(blocks[1]))
            for n, values in enumerate(product(blocks)):
                for b, value in enumerate(values):
                    if n * half + b < len(fields):
                        made[n * half + b].append(value)
    return [jnp.concatenate(value, axis=1) for value in made]


def lanes_of(stack, lanes=128):
    return lax.broadcasted_iota(jnp.int32, (stack, lanes), 1)


def tiles_of(stack, depth, start, width):
    lane = lanes_of(stack)
    masks = []
    for t in range(depth // 128):
        along = lane + (t * 128 - start)
        masks.append((along >= 0) & (along < width))
    return masks


def fold(value, masks):
    out = value[:, :128]
    for t in range(1, len(masks)):
        out = jnp.where(masks[t], value[:, t * 128 : (t + 1) * 128], out)
    return out


def turn(value, by):
    return pltpu.roll(value, by & 127, 1)


def neighbour(me, count, even_up):
    step = jnp.where((me % 2 == 0) == even_up, 1, count - 1)
    return lax.rem(me + step, count)


def upper():
    return (lax.axis_index("yz") >= lax.axis_size("yz") // 2).astype(jnp.int32)


def layer_rows(width, species, groups=0):
    return padded((width + groups) * species, 16)


def blocks_of(width, species, nz, cells):
    pieces = cells // 128
    across = nz // 128
    places = [((width + n // across) * species, n % across * 128) for n in range(2 * pieces)]
    return places[:pieces], places[pieces:]


def pack_x_kernel(c, fine, first, near_slot, far_slot, own, *refs):
    others, (layer, tmp, held, rows, sem, fine_sem) = refs[:-6], refs[-6:]
    nx, width = c.shape[:2]
    species, count, _ = fine.shape
    stack = padded(species, 8)
    slots = pltpu.make_async_copy(fine, held, fine_sem)
    slots.start()
    copy = pltpu.make_async_copy(c.at[upper() * (nx - 1)], layer, sem)
    copy.start()
    slots.wait()
    step = rows.shape[1] // stack
    pieces = rows.shape[0]
    for s in range(species):
        value = held[s].astype(F32)
        for q in range(pieces):
            rows[q, s * step : s * step + count] = value[:, q * 128 : (q + 1) * 128]

    def slot(at):
        taken = [rows[q, pl.ds(at, species, stride=step), :] for q in range(pieces)]
        return jnp.concatenate(taken, axis=1)

    me = lax.axis_index("yz")
    own[...] = slot(me).astype(BF16)
    for k, out in enumerate(others):
        out[...] = slot(lax.rem(me + 2 + k, count)).astype(out.dtype)
    near_slot[...] = slot(neighbour(me, count, True))
    far_slot[...] = slot(neighbour(me, count, False))
    tmp[width * species :] = jnp.zeros((tmp.shape[0] - width * species, tmp.shape[1]), F32)
    copy.wait()
    for r in range(width):
        tmp[r * species : (r + 1) * species] = layer[r]
    first[...] = tmp[...].astype(BF16)


def pack_x(c, fine, forward):
    nx, ny, species, nz = c.shape
    count, cells = fine.shape[1:]
    stack = padded(species, 8)
    vmem = pl.BlockSpec(memory_space=pltpu.VMEM)
    rows = layer_rows(ny, species)
    outs = [jax.ShapeDtypeStruct((rows, nz), BF16)]
    outs += [jax.ShapeDtypeStruct((species, cells), F32)] * 2
    outs += [jax.ShapeDtypeStruct((species, cells), BF16)]
    kind = F32 if forward else BF16
    outs += [jax.ShapeDtypeStruct((species, cells), kind)] * max(count - 3, 0)
    return pl.pallas_call(
        pack_x_kernel,
        in_specs=[pl.BlockSpec(memory_space=pltpu.HBM)] * 2,
        out_specs=[vmem] * len(outs),
        out_shape=outs,
        scratch_shapes=[
            pltpu.VMEM((ny, species, nz), F32),
            pltpu.VMEM((rows, nz), F32),
            pltpu.VMEM(fine.shape, BF16),
            pltpu.VMEM((cells // 128, stack * padded(count, 8), 128), F32),
            pltpu.SemaphoreType.DMA,
            pltpu.SemaphoreType.DMA,
        ],
        compiler_params=pltpu.CompilerParams(vmem_limit_bytes=LIMIT),
        name="pack_x",
    )(
        pltpu.with_memory_space_constraint(c, pltpu.HBM),
        pltpu.with_memory_space_constraint(fine, pltpu.HBM),
    )


def pack_layer(columns, tmp, species):
    for r, value in enumerate(columns):
        tmp[r * species : (r + 1) * species] = value
    below = len(columns) * species
    tmp[below:] = jnp.zeros((tmp.shape[0] - below, tmp.shape[1]), F32)


def pack_slot(value, places, tmp):
    for q, (row, lane) in enumerate(places):
        tmp[row : row + value.shape[0], lane : lane + 128] = value[:, q * 128 : (q + 1) * 128]


def pack_near_kernel(c, slot, *refs):
    second, (out, tmp) = refs[:-2], refs[-2:]
    nx, ny, species, nz = c.shape
    y = jnp.where(lax.axis_index("yz") % 2 == 0, ny - 1, 0)
    pack_layer([c[r, y] for r in range(nx)], tmp, species)
    places = blocks_of(nx, species, nz, slot.shape[1])
    pack_slot(slot[...], places[0], tmp)
    for value in second:
        pack_slot(value[...], places[1], tmp)
    out[...] = tmp[...].astype(BF16)


def pack_far_kernel(c, slot, *refs):
    passed, (out, x_out, tmp, x_tmp) = refs[:-4], refs[-4:]
    nx, ny, species, nz = c.shape
    y = jnp.where(lax.axis_index("yz") % 2 == 0, 0, ny - 1)
    pack_layer([c[r, y] for r in range(nx)], tmp, species)
    places = blocks_of(nx, species, nz, slot.shape[1])
    pack_slot(slot[...], places[0], tmp)
    for ref in passed:
        tmp[nx * species :] = jnp.where(
            passes(tmp.shape[0] - nx * species, nz, places[1], nx * species, species),
            ref[...].astype(F32)[nx * species :],
            tmp[nx * species :],
        )
    out[...] = tmp[...].astype(BF16)
    x = (1 - upper()) * (nx - 1)
    pack_layer([c[x, r] for r in range(ny)], x_tmp, species)
    x_out[...] = x_tmp[...].astype(BF16)


def passes(rows, lanes, places, base, species):
    row = lax.broadcasted_iota(jnp.int32, (rows, lanes), 0)
    lane = lax.broadcasted_iota(jnp.int32, (rows, lanes), 1)
    mask = row < 0
    for at, start in places:
        here = (row >= at - base) & (row < at - base + species)
        mask = mask | (here & (lane >= start) & (lane < start + 128))
    return mask


def pack_y(kernel, name, c, slot, second, groups, extra):
    nx, ny, species, nz = c.shape
    vmem = pl.BlockSpec(memory_space=pltpu.VMEM)
    shapes = [(layer_rows(nx, species, groups), nz)]
    if extra:
        shapes.append((layer_rows(ny, species), nz))
    return pl.pallas_call(
        kernel,
        in_specs=[vmem] * (2 + len(second)),
        out_specs=[vmem] * len(shapes),
        out_shape=[jax.ShapeDtypeStruct(shape, BF16) for shape in shapes],
        scratch_shapes=[pltpu.VMEM(shape, F32) for shape in shapes],
        compiler_params=pltpu.CompilerParams(vmem_limit_bytes=LIMIT),
        name=name,
    )(c, slot, *second)


def coarse_kernel(
    pos, c, rate, coef, spread, ghost, after, adv, old, new, mix, spread16, ghost16, columns, scratch
):
    count, stack, nz = adv.shape
    boxes = pos.shape[1]
    width = c.shape[0]
    mix[...] = mixing(rate, scratch, stack, 2)
    mixed = mixing(rate, scratch, stack, GROUP)
    spread16[...] = spread[...].astype(BF16)
    ghost16[...] = ghost[...].astype(BF16)
    for k in range(count):
        columns[k, c.shape[2] :] = jnp.zeros((stack - c.shape[2], nz), F32)
        columns[k, : c.shape[2]] = c[k // width, k % width]
    diff = column(coef, stack)
    lane = lanes_of(stack)
    starts = [pos[0, i] * width for i in range(boxes)]
    masks = [tiles_of(stack, nz, start, width) for start in starts]
    tiles = old.shape[1] // 128
    zero = jnp.zeros((stack, 128), F32)
    gathered = [[[zero] * tiles for _ in range(2)] for _ in range(boxes)]
    for first in range(0, count, 2 * GROUP):
        some = range(first, min(first + 2 * GROUP, count))
        made = react_all(mixed, [columns[k] for k in some])
        for k in some:
            x, y = k // width, k % width
            mine = columns[k]
            lap = pltpu.roll(mine, 1, 1) + pltpu.roll(mine, nz - 1, 1) - 6.0 * mine
            if x > 0:
                lap = lap + columns[k - width]
            if x < width - 1:
                lap = lap + columns[k + width]
            if y > 0:
                lap = lap + columns[k - 1]
            if y < width - 1:
                lap = lap + columns[k + 1]
            value = mine + diff * lap + made[k - first]
            adv[k] = value
            if x in (0, width - 1) and y in (0, width - 1):
                continue
            for i in range(boxes):
                for n, source in enumerate((mine, value)):
                    moved = turn(fold(source, masks[i]), k * width - starts[i])
                    for t in range(tiles):
                        low, high = k * width - t * 128, (k + 1) * width - t * 128
                        if high > 0 and low < 128:
                            here = (lane >= low) & (lane < high)
                            gathered[i][n][t] = jnp.where(here, moved, gathered[i][n][t])
    for i in range(boxes):
        for out, parts_of in zip((old, new), gathered[i]):
            for t in range(tiles):
                out[i * stack : (i + 1) * stack, t * 128 : (t + 1) * 128] = parts_of[t]


def coarse_part(pos, c, rate, coef, table, stack, after):
    nx, ny, species, nz = c.shape
    boxes = pos.shape[1]
    lanes = padded(nx**3, PATCH)
    vmem = pl.BlockSpec(memory_space=pltpu.VMEM)
    small = jax.ShapeDtypeStruct((boxes * stack, lanes), F32)
    size = padded(2 * GROUP * stack, 128)
    return pl.pallas_call(
        coarse_kernel,
        in_specs=[vmem] * 6 + [pl.BlockSpec(memory_space=pl.ANY)],
        out_specs=[vmem] * 6,
        out_shape=[
            jax.ShapeDtypeStruct((nx * ny, stack, nz), F32),
            small,
            small,
            jax.ShapeDtypeStruct((4 * stack, 4 * stack), BF16),
            jax.ShapeDtypeStruct(table["spread"].shape, BF16),
            jax.ShapeDtypeStruct(table["ghost"].shape, BF16),
        ],
        scratch_shapes=[
            pltpu.VMEM((nx * ny, stack, nz), F32),
            pltpu.VMEM((size, size), F32),
        ],
        compiler_params=pltpu.CompilerParams(vmem_limit_bytes=LIMIT),
        cost_estimate=pl.CostEstimate(
            flops=800 * c.size, bytes_accessed=12 * c.size, transcendentals=0
        ),
        name="coarse_part",
    )(pos, c, rate, coef, jnp.asarray(table["spread"]), jnp.asarray(table["ghost"]), after)


def by_box(total, boxes, half):
    each = 4 * half * half
    lane = lax.broadcasted_iota(jnp.int32, total.shape, 1)
    rows = [
        jnp.where((lane >= i * each) & (lane < (i + 1) * each), total, 0.0) for i in range(boxes)
    ]
    return jnp.concatenate(rows, axis=0)


def gather_faces(pos, layers, faces, half, stack, species, nz, total):
    lane = lanes_of(stack)
    for ref, face in zip(layers, faces):
        for i in range(pos.shape[1]):
            start = pos[0, i] * (half + 2) + 1
            masks = tiles_of(stack, nz, start, half)
            for r in range(half):
                base = ((i * 4 + face) * half + r) * half
                at = (r + 1) * species
                moved = turn(fold(ref[at : at + stack], masks), base - start)
                tiles = []
                for t in range(total.shape[1] // 128):
                    along = lane + (t * 128 - base)
                    here = (along >= 0) & (along < half)
                    tiles.append(jnp.where(here, moved, total[:, t * 128 : (t + 1) * 128]))
                total = tiles[0] if len(tiles) == 1 else jnp.concatenate(tiles, axis=1)
    return total


def x_faces_kernel(pos, owner, first, own, after, *refs, count, half):
    others, (from_x, field, wide) = refs[:-3], refs[-3:]
    stack = from_x.shape[0]
    species = own.shape[0]
    nz = first.shape[1]
    wide[...] = first[...].astype(F32)
    zero = jnp.zeros(from_x.shape, F32)
    from_x[...] = gather_faces(pos, [wide], [1 - upper()], half, stack, species, nz, zero)
    me = lax.axis_index("yz")
    direct = [ref[...].astype(F32) for ref in (own, *others)]
    for i in range(pos.shape[1]):
        back = lax.rem(me - owner[0, i] + count, count)
        value = direct[0]
        for k in range(len(others)):
            value = jnp.where(back == k + 2, direct[k + 1], value)
        edge = species // 8 * 8
        field[i * stack + edge : (i + 1) * stack] = jnp.zeros((stack - edge, value.shape[1]), F32)
        field[i * stack : i * stack + species] = value


def x_faces(pos, owner, first, own, after, others, half, stack, count):
    vmem = pl.BlockSpec(memory_space=pltpu.VMEM)
    boxes = pos.shape[1]
    lanes = padded(boxes * 4 * half * half, 128)
    return pl.pallas_call(
        functools.partial(x_faces_kernel, count=count, half=half),
        in_specs=[vmem] * 4 + [pl.BlockSpec(memory_space=pl.ANY)] + [vmem] * len(others),
        out_specs=[vmem] * 2,
        out_shape=[
            jax.ShapeDtypeStruct((stack, lanes), F32),
            jax.ShapeDtypeStruct((boxes * stack, own.shape[1]), F32),
        ],
        scratch_shapes=[pltpu.VMEM(first.shape, F32)],
        compiler_params=pltpu.CompilerParams(vmem_limit_bytes=LIMIT),
        cost_estimate=pl.CostEstimate(flops=10**9, bytes_accessed=ORDER, transcendentals=0),
        name="x_faces",
    )(pos, owner, first, own, after, *others)


def fine_kernel(pos, owner, x_second, near, far, start, *refs, count, edge):
    old, new, mix, coef, spread, ghost, from_x = refs[:7]
    packets = refs[7 : 7 + count]
    fix, kept, final, field, wide, x_wide = refs[7 + count :]
    species = packets[0].shape[0]
    stack = from_x.shape[0]
    boxes = final.shape[0] // stack
    cells = final.shape[1]
    me = lax.axis_index("yz")
    mixed = mix[...]

    def reaction(value):
        pairs = [value[at : at + 2 * stack] for at in range(0, boxes * stack, 2 * stack)]
        return jnp.concatenate([react(mixed, pair) for pair in pairs], axis=0)

    nz = near.shape[1]
    half = edge // 2
    wide[0] = near[...].astype(F32)
    wide[1] = far[...].astype(F32)
    first_at, second_at = blocks_of(half + 2, species, nz, cells)
    near_at, far_at = neighbour(me, count, True), neighbour(me, count, False)
    sources = [(near_at, 0, first_at), (far_at, 1, first_at)]
    if count == 4:
        sources.append((lax.rem(me + 2, count), 1, second_at))
    for i in range(boxes):
        for q in range(cells // 128):
            mine = (slice(i * stack, (i + 1) * stack), slice(q * 128, (q + 1) * 128))
            part = start[mine]
            for source, n, places in sources:
                row, at = places[q]
                sent = wide[n, row : row + stack, at : at + 128]
                part = jnp.where(owner[0, i] == source, sent, part)
            field[mine] = part
    diff = jnp.concatenate([column(coef, stack)] * boxes, axis=0)
    old_v, new_v = old[...], new[...]
    sums = old_v + new_v
    spread_v = spread[...]
    both = rows_dot(jnp.concatenate([old_v, sums], axis=0), spread_v)
    ghost0, ghost1 = both[: boxes * stack], both[boxes * stack :]
    index = lax.broadcasted_iota(jnp.int32, (1, cells), 1)
    at = (index // (edge * edge), index // edge % edge, index % edge)
    step = (edge * edge, edge, 1)

    def inside(value):
        lap = -6.0 * value
        for axis in range(3):
            before = pltpu.roll(value, step[axis], 1)
            after = pltpu.roll(value, cells - step[axis], 1)
            lap = lap + jnp.where(at[axis] == 0, 0.0, before)
            lap = lap + jnp.where(at[axis] == edge - 1, 0.0, after)
        return lap

    first = field[...]
    second = first + 2.0 * diff * (inside(first) + ghost0) + 0.5 * reaction(first)
    base = second + diff * (2.0 * inside(second) + ghost1) + 0.5 * reaction(second)
    odd = me % 2
    x_wide[...] = x_second[...].astype(F32)
    layers = (x_wide, wide.at[0], wide.at[1])
    faces = (upper(), 3 - odd, 2 + odd)
    total = gather_faces(pos, layers, faces, half, stack, species, nz, from_x[...])
    kept[...] = total
    stacked = by_box(total, boxes, half).astype(BF16)
    value = base + diff * diff * dot(stacked, ghost[...])
    final[...] = value
    for k, out in enumerate(packets):
        dest = partner(me, k, count)
        packet = jnp.zeros((species, cells), F32)
        for i in range(boxes):
            packet = jnp.where(owner[0, i] == dest, value[i * stack : i * stack + species], packet)
        out[...] = packet.astype(BF16)
    pooled = lax.dot_general(
        parts(first + second), spread_v, (((1,), (1,)), ((), ())), preferred_element_type=F32
    )
    pooled = 0.25 * (pooled[: boxes * stack] + pooled[boxes * stack :])
    width = edge // 2 + 2
    lanes = old.shape[1]
    lane = lax.broadcasted_iota(jnp.int32, (1, lanes), 1)
    at = (lane // (width * width), lane // width % width, lane % width)
    step = (width * width, width, 1)
    inner = [(a >= 1) & (a <= width - 2) for a in at]
    rest = pooled - 0.5 * sums
    result = jnp.zeros_like(old_v)
    for axis in range(3):
        sides = inner[(axis + 1) % 3] & inner[(axis + 2) % 3]
        for edge_at, shift in ((0, lanes - step[axis]), (width - 1, step[axis])):
            mask = sides & (at[axis] == edge_at)
            fixed = rest - pltpu.roll(old_v, shift, 1)
            result = jnp.where(mask, fixed, result)
    fix[...] = diff * result


def fine_part(pos, owner, second, near, far, start, old, new, mix, coef, spread, ghost, from_x, edge, count):
    boxes = owner.shape[1]
    stack = from_x.shape[0]
    cells = start.shape[1]
    vmem = pl.BlockSpec(memory_space=pltpu.VMEM)
    return pl.pallas_call(
        functools.partial(fine_kernel, count=count, edge=edge),
        in_specs=[vmem] * 13,
        out_specs=[vmem] * (count + 3),
        out_shape=[jax.ShapeDtypeStruct((coef.shape[1], cells), BF16)] * count
        + [
            jax.ShapeDtypeStruct((boxes * stack, old.shape[1]), F32),
            jax.ShapeDtypeStruct(from_x.shape, F32),
            jax.ShapeDtypeStruct((boxes * stack, cells), F32),
        ],
        scratch_shapes=[
            pltpu.VMEM((boxes * stack, cells), F32),
            pltpu.VMEM((2, *near.shape), F32),
            pltpu.VMEM(second.shape, F32),
        ],
        compiler_params=pltpu.CompilerParams(vmem_limit_bytes=LIMIT),
        name="fine_part",
    )(
        pos,
        owner,
        second,
        near,
        far,
        start,
        old,
        new,
        mix,
        coef,
        spread,
        ghost,
        from_x,
    )


def delta_of(field, kept, fix, coef, average, place, half, stack):
    boxes = field.shape[0] // stack
    diffs = jnp.concatenate([column(coef, stack)] * boxes, axis=0)
    stacked = by_box(kept[...], boxes, half).astype(BF16)
    halo = dot(stacked, place[...].astype(BF16))
    means = rows_dot(field[...], average[...].astype(BF16))
    return fix[...] - 0.5 * diffs * diffs * halo + means


def correct_kernel(
    pos, adv, x_first, x_second, near, far, coef, field, kept, fix, average, place, out, block, wide, sems, half
):
    count, stack, nz = adv.shape
    species = block.shape[2]
    width = half + 2
    delta = delta_of(field, kept, fix, coef, average, place, half, stack)
    diff = column(coef, stack)
    even = lax.axis_index("yz") % 2 == 0
    rows = x_first.shape[0]
    first_v, second_v = x_first[...].astype(F32), x_second[...].astype(F32)
    near_v, far_v = near[:rows].astype(F32), far[:rows].astype(F32)
    up = upper() == 1
    wide[0, :rows] = jnp.where(up, first_v, second_v)
    wide[1, :rows] = jnp.where(up, second_v, first_v)
    wide[2, :rows] = jnp.where(even, far_v, near_v)
    wide[3, :rows] = jnp.where(even, near_v, far_v)
    boxes = delta.shape[0] // stack
    starts = [pos[0, i] * width for i in range(boxes)]
    cycle = [tiles_of(stack, nz, start, width) for start in starts]
    inside = [tiles_of(stack, nz, start + 1, half) for start in starts]
    lane = lanes_of(stack)
    copies = []
    for k in range(count):
        x, y = k // width, k % width
        value = adv[k]
        for there, at, n in (
            (x == 0, y, 0),
            (x == width - 1, y, 1),
            (y == 0, x, 2),
            (y == width - 1, x, 3),
        ):
            if there:
                value = value + diff * wide[n, at * species : at * species + stack]
        if x not in (0, width - 1) or y not in (0, width - 1):
            tiles = [value[:, t * 128 : (t + 1) * 128] for t in range(nz // 128)]
            covers = 0 < x < width - 1 and 0 < y < width - 1
            for i in range(boxes):
                mine = delta[i * stack : (i + 1) * stack]
                t = k * width // 128
                part = mine[:, t * 128 : (t + 1) * 128]
                if (k + 1) * width > (t + 1) * 128:
                    after = mine[:, (t + 1) * 128 : (t + 2) * 128]
                    part = jnp.where(lane < (k + 1) * width - (t + 1) * 128, after, part)
                moved = turn(part, starts[i] - k * width)
                for t in range(nz // 128):
                    if covers:
                        tiles[t] = jnp.where(inside[i][t], 0.0, tiles[t])
                    tiles[t] = tiles[t] + jnp.where(cycle[i][t], moved, 0.0)
            value = jnp.concatenate(tiles, axis=1)
        block[x, y] = value[:species]
        if y == width - 1:
            copies.append(pltpu.make_async_copy(block.at[x], out.at[x], sems.at[x]))
            copies[-1].start()
    for copy in copies:
        copy.wait()


def correct(pos, adv, halos, coef, field, kept, fix, table, half):
    _, stack, nz = adv.shape
    width = half + 2
    species = coef.shape[1]
    vmem = pl.BlockSpec(memory_space=pltpu.VMEM)
    return pl.pallas_call(
        functools.partial(correct_kernel, half=half),
        in_specs=[vmem] * 12,
        out_specs=pl.BlockSpec(memory_space=pltpu.HBM),
        out_shape=jax.ShapeDtypeStruct((width, width, species, nz), F32),
        scratch_shapes=[
            pltpu.VMEM((width, width, species, nz), F32),
            pltpu.VMEM((4, halos[0].shape[0] + stack, nz), F32),
            pltpu.SemaphoreType.DMA((width,)),
        ],
        compiler_params=pltpu.CompilerParams(vmem_limit_bytes=LIMIT),
        cost_estimate=pl.CostEstimate(
            flops=20 * adv.size, bytes_accessed=12 * adv.size, transcendentals=0
        ),
        name="coarse_correct",
    )(
        pos,
        adv,
        *halos,
        coef,
        field,
        kept,
        fix,
        jnp.asarray(table["average"]),
        jnp.asarray(table["place"]),
    )


def ring(axis, by):
    count = lax.axis_size(axis)
    return [(i, (i + by) % count) for i in range(count)]


def mutual(axis, by):
    count = lax.axis_size(axis)
    one_way = [(i, (i + by) % count) for i in range(0, count, 2)]
    return one_way + [(j, i) for i, j in one_way]


def slabs(by):
    slabs_count, count = lax.axis_size("gx"), lax.axis_size("yz")
    pairs = []
    for g in range(slabs_count):
        for j in range(count):
            to = (g + (by if j < count // 2 else -by)) % slabs_count
            pairs.append((g * count + j, to * count + j))
    return pairs


def partner(me, k, count):
    return me ^ k if count & (count - 1) == 0 else lax.rem(me + k, count)


def origin(me, source, count):
    return me ^ source if count & (count - 1) == 0 else lax.rem(me - source + count, count)


def local(coarse_state, fine_state, diffusion, rate, box_pos, box_owner):
    species, width = coarse_state.shape[:2]
    half = width - 2
    stack = padded(species, 8)
    count = lax.axis_size("yz")
    me = lax.axis_index("yz")
    pos, owner = box_pos[0], box_owner[0]
    table = tables(width, pos.shape[1])
    coef = diffusion[None]
    c = jnp.transpose(coarse_state, (1, 2, 0, 3))

    fine = jnp.transpose(fine_state, (1, 0, 2))
    forward = count == 4
    forward = count == 4
    groups = -(-(2 if forward else 1) * fine.shape[2] // c.shape[3])
    x_first, near_slot, far_slot, own, *others = pack_x(c, fine, forward)
    relayed = others if forward else []
    (near,) = pack_y(pack_near_kernel, "pack_near", c, near_slot, relayed, groups, False)
    near = lax.ppermute(near, "yz", mutual("yz", 1))
    relayed = [near] if forward else []
    far, x_second = pack_y(pack_far_kernel, "pack_far", c, far_slot, relayed, groups, True)
    halos = [
        lax.ppermute(x_first, ("gx", "yz"), slabs(-1)),
        lax.ppermute(x_second, ("gx", "yz"), slabs(1)),
        near,
        lax.ppermute(far, "yz", mutual("yz", -1)),
    ]
    if forward:
        others = []
    others = [lax.ppermute(slot, "yz", ring("yz", 2 + k)) for k, slot in enumerate(others)]

    adv, old, new, mix, spread, ghost = coarse_part(
        pos, c, rate, coef, table, stack, far
    )
    from_x, start = x_faces(pos, owner, halos[0], own, old, others, half, stack, count)
    made = fine_part(
        pos, owner, *halos[1:], start, old, new, mix, coef, spread, ghost, from_x, 2 * half, count
    )
    packets, (fix, kept, field) = made[:count], made[count:]

    def swap(value, k):
        even = count & (count - 1) == 0
        pairs = [(i, i ^ k if even else (i + k) % count) for i in range(count)]
        return lax.ppermute(value, "yz", pairs)

    back = [packets[0]] + [swap(packets[k], k) for k in range(1, count)]
    coarse_next = correct(pos, adv, halos, coef, field, kept, fix, table, half)

    source = lax.broadcasted_iota(jnp.int32, (count, 1, 1), 0)
    turn = origin(me, source, count)
    fine_next = jnp.broadcast_to(back[0][None], (count,) + back[0].shape)
    for k in range(1, count):
        fine_next = jnp.where(turn == k, back[k][None], fine_next)
    return jnp.transpose(coarse_next, (2, 0, 1, 3)), fine_next


def solution(mesh):
    in_specs = (
        P(None, "gx", "yz", None),
        P(("gx", "yz"), None, None),
        P(),
        P(),
        P("gx", "yz", None),
        P("gx", "yz", None),
    )
    out_specs = (P(None, "gx", "yz", None), P(("gx", "yz"), None, None))
    return jax.shard_map(local, mesh=mesh, in_specs=in_specs, out_specs=out_specs, check_vma=False)
```

time: 184 us -> 21.7 us (0.12)
  local copies, waits for them, and re-layouts: 117 us -> 0.36 us
  starting transfers between devices: 34.6 us -> 8.16 us
  other arithmetic: 11.1 us -> 0.77 us
  Pallas kernels: 0 us -> 6.97 us
  waiting for transfers between devices: 10.8 us -> 4.47 us
  loops' own time: 3.37 us -> 0 us
  matrix products: 2.83 us -> 0 us
    unnamed x71 -> x18, local copies, waits for them, and re-layouts: 34 us -> 0.36 us
    dynamic_update_slice x10 -> x0, local copies, waits for them, and re-layouts: 27 us -> none  [the longest x2 24.6 us: local(): coarse_next = lax.dynamic_update_slice(coarse_next, patch, corners[i])]
    all_to_all x3 -> x0, starting transfers between devices: 26.8 us -> none  [the longest x1 20.2 us: local(): lax.all_to_all(packets.astype(jnp.bfloat16), 'yz', split_axis=0, concat_a...]
    another operation x31 -> x0, local copies, waits for them, and re-layouts: 17.5 us -> none  [the longest x12 7.08 us: cycle_faces(): jnp.stack([patch[:, 0, 1:-1, 1:-1], patch[:, -1, 1:-1, 1:-1], patch[:, 1:...]
    slice x47 -> x0, local copies, waits for them, and re-layouts: 13 us -> none  [the longest x3 2.59 us: inner_faces(): patch[:, 1:-1, -2, 1:-1]]
    scatter-add x12 -> x0, local copies, waits for them, and re-layouts: 9.68 us -> none  [the longest x2 2.81 us: correct(): out = out.at[:, 1:-1, -1, 1:-1].add(fix[:, 3])]
    scatter x4 -> x0, local copies, waits for them, and re-layouts: 7.3 us -> none  [correct(): return out.at[:, 1:-1, 1:-1, 1:-1].set(average)]
    pallas_call x0 -> x7, Pallas kernels: none -> 6.97 us  [the longest x1 3.27 us: coarse_part(): pl.pallas_call(coarse_kernel, in_specs=[vmem] * 6 + [pl.BlockSpec(memory_...]
  transfers between devices with their start and end apart: 7 -> 7, of which waited for: 4 -> 2; matrix products, arithmetic and copies ran while one was open for 34% -> 0% of each run, Pallas kernels for 0% -> 24%
where the time goes in v1:
time: 21.7 us; the launch traced here: 21.5 us
  starting transfers between devices  8.16 us (38%)
  Pallas kernels  6.97 us (32%)
  waiting for transfers between devices  4.47 us (21%)
  between operations  0.81 us (4%)
  other arithmetic  0.77 us (4%)
  local copies, waits for them, and re-layouts  0.36 us (2%)
    ppermute x1, starting transfers between devices, local(): lax.ppermute(x_first, ('gx', 'yz'), slabs(-1))  5.59 us
    ppermute x1, waiting for transfers between devices, local(): lax.ppermute(x_second, ('gx', 'yz'), slabs(1))  3.99 us
    pallas_call x1, Pallas kernels, coarse_part(): pl.pallas_call(coarse_kernel, in_specs=[vmem] * 6 + [pl.BlockSpec(memory_...  3.27 us
    ppermute x3, starting transfers between devices, swap(): return lax.ppermute(value, 'yz', pairs)  1.92 us
    pallas_call x1, Pallas kernels, correct(): pl.pallas_call(functools.partial(correct_kernel, half=half), in_specs=[vm...  1.54 us
    pallas_call x1, Pallas kernels, pack_x(): pl.pallas_call(pack_x_kernel, in_specs=[pl.BlockSpec(memory_space=pltpu.H...  1.13 us
    select_n x1, other arithmetic, local(): fine_next = jnp.where(turn == k, back[k][None], fine_next)  0.75 us
    pallas_call x1, Pallas kernels, fine_part(): pl.pallas_call(functools.partial(fine_kernel, count=count, edge=edge), in...  0.71 us
  transfers between devices with their start and end apart: 7, of which 2 were waited for; matrix products, arithmetic and copies ran while one was open for 0% of the time, Pallas kernels for 24%

profile of v1, /device:TPU:0, one launch (start us, length us, event | category | flops | bytes accessed | tf_op | source)
XLA Modules:
  0.0 21.5 jit_solution(12773397037401660854)
XLA Ops:
  0.6 1.1 %pack_x.1 = (bf16[128,384]{1,0:T(8,128)(2,1)S(1)}, f32[21,512]{1,0:T(8,128)S(1)}, f32[21,512]{1,0:T(8,128)S(1)}, bf16[21,512]{1,0:T(8,128)(2,1)S(1)}, f32[21,512]{1,0:T(8,128)S(1)}) custom-call(f32[6,6,21,384]{3,2,1,0:T(8,128)} %bitcast.6, bf16[21,4,512]{2,1,0:T(4,128)(2,1)} %bitcast.20), custom_call_target="tpu_custom_call" | custom-call | tf_op jit(solution)/shard_map/pack_x/pallas_call | solution.py:232
  1.8 0.3 %copy-done = f32[21,6,6,384]{3,0,2,1:T(8,128)S(1)} copy-done((f32[21,6,6,384]{3,0,2,1:T(8,128)S(1)}, f32[21,6,6,384]{3,0,2,1:T(8,128)}, u32[]{:S(2)}) %copy-start) | copy-done | bytes 1161240
  2.1 0.0 copy-start.7
  2.2 0.5 %collective-permute-start = (bf16[192,384]{1,0:T(8,128)(2,1)S(1)}, bf16[192,384]{1,0:T(8,128)(2,1)S(1)}, u32[]{:S(2)}, u32[]{:S(2)}) collective-permute-start(bf16[192,384]{1,0:T(8,128)(2,1)S(1)} %pack_near.1), channel_id=1, source_target_pairs={{0,1},{2,3},{1,0},{3,2},{4,5},{6,7},{5,4},{7,6},{8,9},{10,11},{9,8... | collective-permute-start | bytes 442376 | tf_op jit(solution)/shard_map/ppermute | solution.py:751
  2.7 5.6 %collective-permute-start.1 = (bf16[128,384]{1,0:T(8,128)(2,1)S(1)}, bf16[128,384]{1,0:T(8,128)(2,1)S(1)}, u32[]{:S(2)}, u32[]{:S(2)}) collective-permute-start(bf16[128,384]{1,0:T(8,128)(2,1)S(1)} %get-tuple-element.29), channel_id=1, source_target_pairs={{0,28},{1,29},{2,6},{3,7},{4,0},{5,1},{6,10},{7,11},{8,4},{9,5},{1... | collective-permute-start | bytes 294920 | tf_op jit(solution)/shard_map/ppermute | solution.py:755
  8.3 0.0 collective-permute-done.refs_0_.near
  8.3 0.1 pack_far.1
  8.4 0.0 copy-start.8
  8.4 0.1 collective-permute-start.3
  8.5 0.1 collective-permute-start.2
  8.6 3.3 %coarse_part.1 = (f32[36,24,384]{2,1,0:T(8,128)S(1)}, f32[48,256]{1,0:T(8,128)S(1)}, f32[48,256]{1,0:T(8,128)S(1)}, bf16[96,96]{1,0:T(8,128)(2,1)S(1)}, bf16[256...) custom-call(s32[1,2]{1,0:T(1,128)S(1)} %bitcast.10, f32[6,6,21,384]{3,2,1,0:T(8,128)S(1)} %bitcast.9, ...), custom_call_target="tpu_custom_call" | custom-call | flops 232243200 | bytes 3483648 | tf_op jit(solution)/shard_map/coarse_part/pallas_call | solution.py:383
  11.9 0.0 collective-permute-done.1.first.x_first
  11.9 0.0 copy-start.4
  11.9 0.2 x_faces.1
  12.1 4.0 %collective-permute-done.2.x_second = bf16[128,384]{1,0:T(8,128)(2,1)S(1)} collective-permute-done((bf16[128,384]{1,0:T(8,128)(2,1)S(1)}, bf16[128,384]{1,0:T(8,128)(2,1)S(1)}, u32[]{:S(2)}, u32[]{:S(2)}) %collective-permute-start.2) | collective-permute-done | bytes 98336 | tf_op jit(solution)/shard_map/ppermute | solution.py:756
  16.1 0.0 collective-permute-done.3.far
  16.1 0.7 %fine_part.1 = (bf16[21,512]{1,0:T(8,128)(2,1)S(1)}, bf16[21,512]{1,0:T(8,128)(2,1)S(1)}, bf16[21,512]{1,0:T(8,128)(2,1)S(1)}, bf16[21,512]{1,0:T(8,128)(2,1)S(1...) custom-call(s32[1,2]{1,0:T(1,128)S(1)} %bitcast.12, s32[1,2]{1,0:T(1,128)S(1)} %bitcast.18, ...), custom_call_target="tpu_custom_call" | custom-call | tf_op jit(solution)/shard_map/fine_part/pallas_call | solution.py:570
  16.8 0.1 collective-permute-start.4
  16.9 1.0 %collective-permute-start.5 = (bf16[21,512]{1,0:T(8,128)(2,1)S(1)}, bf16[21,512]{1,0:T(8,128)(2,1)S(1)}, u32[]{:S(2)}, u32[]{:S(2)}) collective-permute-start(bf16[21,512]{1,0:T(8,128)(2,1)S(1)} %get-tuple-element.43), channel_id=1, source_target_pairs={{0,2},{1,3},{2,0},{3,1},{4,6},{5,7},{6,4},{7,5},{8,10},{9,11},{10,... | collective-permute-start | bytes 64520 | tf_op jit(solution)/shard_map/ppermute | solution.py:776
  17.8 0.9 %collective-permute-start.6 = (bf16[21,512]{1,0:T(8,128)(2,1)S(1)}, bf16[21,512]{1,0:T(8,128)(2,1)S(1)}, u32[]{:S(2)}, u32[]{:S(2)}) collective-permute-start(bf16[21,512]{1,0:T(8,128)(2,1)S(1)} %get-tuple-element.44), channel_id=1, source_target_pairs={{0,1},{1,0},{2,3},{3,2},{4,5},{5,4},{6,7},{7,6},{8,9},{9,8},{10,11... | collective-permute-start | bytes 64520 | tf_op jit(solution)/shard_map/ppermute | solution.py:776
  18.7 1.5 %coarse_correct.1 = f32[6,6,21,384]{3,2,1,0:T(8,128)} custom-call(s32[1,2]{1,0:T(1,128)S(1)} %bitcast.13, f32[36,24,384]{2,1,0:T(8,128)S(1)} %get-tuple-element.28.adv, bf16[128,384]{1,0:T(8,128)(2,1)S(1)} %collective-permute-done.1.first.x_first, bf16[128,384]{1,0:T(8,128)(2,1)S(1)} %collective-permute-done.2.x_second, ...), custom_call_target="tpu_custom_call" | custom-call | flops 6635520 | bytes 3981312 | tf_op jit(solution)/shard_map/coarse_correct/pallas_call | solution.py:676
  20.3 0.5 %collective-permute-done.5 = bf16[21,512]{1,0:T(8,128)(2,1)S(1)} collective-permute-done((bf16[21,512]{1,0:T(8,128)(2,1)S(1)}, bf16[21,512]{1,0:T(8,128)(2,1)S(1)}, u32[]{:S(2)}, u32[]{:S(2)}) %collective-permute-start.5) | collective-permute-done | bytes 21536 | tf_op jit(solution)/shard_map/ppermute | solution.py:776
  20.8 0.0 collective-permute-done.6
  20.8 0.8 %select_select_fusion = bf16[4,21,512]{2,0,1:T(4,128)(2,1)} fusion(pred[4]{0:T(512)(128)(4,1)S(1)} %get-tuple-element.47, pred[4]{0:T(512)(128)(4,1)S(1)} %fusion.2, pred[4]{0:T(512)(128)(4,1)S(1)} %get-tuple-element.46, bf16[21,512]{1,0:T(8,128)(2,1)S(1)} %get-tuple-element.45, bf16[21,512]{1,0:T(8,128)(2,1)S(1)} %collective-permute-done.6, ...), kind=kLoop, calls=%fused_computation | loop fusion | flops 129024 | bytes 172044 | tf_op jit(solution)/shard_map/jit(_where)/select_n | solution.py:785
  (18 shorter events, 0.1 us)
Async XLA Ops:
  0.6 1.5 %copy-start = (f32[21,6,6,384]{3,0,2,1:T(8,128)S(1)}, f32[21,6,6,384]{3,0,2,1:T(8,128)}, u32[]{:S(2)}) copy-start(f32[21,6,6,384]{3,0,2,1:T(8,128)} %param.10) | copy-start | bytes 3483652
  2.1 6.4 %copy-start.2 = (f32[256,512]{1,0:T(8,128)S(1)}, f32[256,512]{1,0:T(8,128)}, u32[]{:S(2)}) copy-start(f32[256,512]{1,0:T(8,128)} %constant.18.clone.spread) | copy-start | bytes 1572868
  2.1 6.4 %copy-start.3 = (f32[128,512]{1,0:T(8,128)S(1)}, f32[128,512]{1,0:T(8,128)}, u32[]{:S(2)}) copy-start(f32[128,512]{1,0:T(8,128)} %constant.19.clone.ghost) | copy-start | bytes 786436
  2.1 6.5 %copy-start.5 = (f32[21,21]{1,0:T(8,128)S(1)}, f32[21,21]{1,0:T(8,128)}, u32[]{:S(2)}) copy-start(f32[21,21]{1,0:T(8,128)} %rate.1) | copy-start | bytes 5296
  2.1 6.5 %copy-start.6 = (s32[1,1,2]{2,1,0:T(1,128)S(1)}, s32[1,1,2]{2,1,0:T(1,128)}, u32[]{:S(2)}) copy-start(s32[1,1,2]{2,1,0:T(1,128)} %param.14) | copy-start | bytes 28
  2.1 6.5 %copy-start.7 = (f32[21]{0:T(128)S(1)}, f32[21]{0:T(128)}, u32[]{:S(2)}) copy-start(f32[21]{0:T(128)} %param.12) | copy-start | bytes 256
  2.2 6.1 %collective-permute-start = (bf16[192,384]{1,0:T(8,128)(2,1)S(1)}, bf16[192,384]{1,0:T(8,128)(2,1)S(1)}, u32[]{:S(2)}, u32[]{:S(2)}) collective-permute-start(bf16[192,384]{1,0:T(8,128)(2,1)S(1)} %pack_near.1), channel_id=1, source_target_pairs={{0,1},{2,3},{1,0},{3,2},{4,5},{6,7},{5,4},{7,6},{8,9},{10,11},{9,8... | collective-permute-start | bytes 442376 | tf_op jit(solution)/shard_map/ppermute | solution.py:751
  2.7 9.2 %collective-permute-start.1 = (bf16[128,384]{1,0:T(8,128)(2,1)S(1)}, bf16[128,384]{1,0:T(8,128)(2,1)S(1)}, u32[]{:S(2)}, u32[]{:S(2)}) collective-permute-start(bf16[128,384]{1,0:T(8,128)(2,1)S(1)} %get-tuple-element.29), channel_id=1, source_target_pairs={{0,28},{1,29},{2,6},{3,7},{4,0},{5,1},{6,10},{7,11},{8,4},{9,5},{1... | collective-permute-start | bytes 294920 | tf_op jit(solution)/shard_map/ppermute | solution.py:755
  8.4 3.5 %copy-start.8 = (s32[1,1,2]{2,1,0:T(1,128)S(1)}, s32[1,1,2]{2,1,0:T(1,128)}, u32[]{:S(2)}) copy-start(s32[1,1,2]{2,1,0:T(1,128)} %param.15) | copy-start | bytes 28
  8.4 7.7 %collective-permute-start.3 = (bf16[192,384]{1,0:T(8,128)(2,1)S(1)}, bf16[192,384]{1,0:T(8,128)(2,1)S(1)}, u32[]{:S(2)}, u32[]{:S(2)}) collective-permute-start(bf16[192,384]{1,0:T(8,128)(2,1)S(1)} %get-tuple-element.27.after), channel_id=1, source_target_pairs={{0,3},{2,1},{3,0},{1,2},{4,7},{6,5},{7,4},{5,6},{8,11},{10,9},{11,... | collective-permute-start | bytes 442376 | tf_op jit(solution)/shard_map/ppermute | solution.py:758
  8.5 7.6 %collective-permute-start.2 = (bf16[128,384]{1,0:T(8,128)(2,1)S(1)}, bf16[128,384]{1,0:T(8,128)(2,1)S(1)}, u32[]{:S(2)}, u32[]{:S(2)}) collective-permute-start(bf16[128,384]{1,0:T(8,128)(2,1)S(1)} %get-tuple-element.30), channel_id=1, source_target_pairs={{0,4},{1,5},{2,30},{3,31},{4,8},{5,9},{6,2},{7,3},{8,12},{9,13},{1... | collective-permute-start | bytes 294920 | tf_op jit(solution)/shard_map/ppermute | solution.py:756
  11.9 6.9 %copy-start.4 = (f32[128,256]{1,0:T(8,128)S(1)}, f32[128,256]{1,0:T(8,128)}, u32[]{:S(2)}) copy-start(f32[128,256]{1,0:T(8,128)} %constant.21.clone.place) | copy-start | bytes 393220
  12.1 6.7 %copy-start.1 = (f32[512,256]{1,0:T(8,128)S(1)}, f32[512,256]{1,0:T(8,128)}, u32[]{:S(2)}) copy-start(f32[512,256]{1,0:T(8,128)} %constant.20.clone.average) | copy-start | bytes 1572868
  16.8 3.5 %collective-permute-start.4 = (bf16[21,512]{1,0:T(8,128)(2,1)S(1)}, bf16[21,512]{1,0:T(8,128)(2,1)S(1)}, u32[]{:S(2)}, u32[]{:S(2)}) collective-permute-start(bf16[21,512]{1,0:T(8,128)(2,1)S(1)} %get-tuple-element.42), channel_id=1, source_target_pairs={{0,3},{1,2},{2,1},{3,0},{4,7},{5,6},{6,5},{7,4},{8,11},{9,10},{10,... | collective-permute-start | bytes 64520 | tf_op jit(solution)/shard_map/ppermute | solution.py:776
  16.9 3.9 %collective-permute-start.5 = (bf16[21,512]{1,0:T(8,128)(2,1)S(1)}, bf16[21,512]{1,0:T(8,128)(2,1)S(1)}, u32[]{:S(2)}, u32[]{:S(2)}) collective-permute-start(bf16[21,512]{1,0:T(8,128)(2,1)S(1)} %get-tuple-element.43), channel_id=1, source_target_pairs={{0,2},{1,3},{2,0},{3,1},{4,6},{5,7},{6,4},{7,5},{8,10},{9,11},{10,... | collective-permute-start | bytes 64520 | tf_op jit(solution)/shard_map/ppermute | solution.py:776
  17.8 2.9 %collective-permute-start.6 = (bf16[21,512]{1,0:T(8,128)(2,1)S(1)}, bf16[21,512]{1,0:T(8,128)(2,1)S(1)}, u32[]{:S(2)}, u32[]{:S(2)}) collective-permute-start(bf16[21,512]{1,0:T(8,128)(2,1)S(1)} %get-tuple-element.44), channel_id=1, source_target_pairs={{0,1},{1,0},{2,3},{3,2},{4,5},{5,4},{6,7},{7,6},{8,9},{9,8},{10,11... | collective-permute-start | bytes 64520 | tf_op jit(solution)/shard_map/ppermute | solution.py:776

commit v2 on v1

--- a/solution.py
+++ b/solution.py
@@ -169,30 +169,34 @@
     return lax.rem(me + step, count)
 
 
-def upper():
-    return (lax.axis_index("yz") >= lax.axis_size("yz") // 2).astype(jnp.int32)
-
-
 def layer_rows(width, species, groups=0):
     return padded((width + groups) * species, 16)
 
 
-def blocks_of(width, species, nz, cells):
-    pieces = cells // 128
+def blocks_of(width, species, nz, pieces):
     across = nz // 128
-    places = [((width + n // across) * species, n % across * 128) for n in range(2 * pieces)]
-    return places[:pieces], places[pieces:]
-
-
-def pack_x_kernel(c, fine, first, near_slot, far_slot, own, *refs):
-    others, (layer, tmp, held, rows, sem, fine_sem) = refs[:-6], refs[-6:]
-    nx, width = c.shape[:2]
-    species, count, _ = fine.shape
+    return [((width + n // across) * species, n % across * 128) for n in range(pieces)]
+
+
+def pack_layer(columns, tmp, species):
+    for r, value in enumerate(columns):
+        tmp[r * species : (r + 1) * species] = value
+    below = len(columns) * species
+    tmp[below:] = jnp.zeros((tmp.shape[0] - below, tmp.shape[1]), F32)
+
+
+def pack_y_kernel(c, fine, near, far, own, *refs):
+    others, (layer, tmp, held, rows, sems, fine_sem) = refs[:-6], refs[-6:]
+    nx, ny, species, nz = c.shape
+    count = fine.shape[1]
     stack = padded(species, 8)
+    me = lax.axis_index("yz")
     slots = pltpu.make_async_copy(fine, held, fine_sem)
     slots.start()
-    copy = pltpu.make_async_copy(c.at[upper() * (nx - 1)], layer, sem)
-    copy.start()
+    copies = []
+    for n, y in enumerate((jnp.where(me % 2 == 0, ny - 1, 0), jnp.where(me % 2 == 0, 0, ny - 1))):
+        copies.append(pltpu.make_async_copy(c.at[:, y], layer.at[n], sems.at[n]))
+        copies[-1].start()
     slots.wait()
     step = rows.shape[1] // stack
     pieces = rows.shape[0]
@@ -202,122 +206,69 @@
             rows[q, s * step : s * step + count] = value[:, q * 128 : (q + 1) * 128]
 
     def slot(at):
-        taken = [rows[q, pl.ds(at, species, stride=step), :] for q in range(pieces)]
-        return jnp.concatenate(taken, axis=1)
-
-    me = lax.axis_index("yz")
-    own[...] = slot(me).astype(BF16)
+        return [rows[q, pl.ds(at, species, stride=step), :] for q in range(pieces)]
+
+    own[...] = jnp.concatenate(slot(me), axis=1).astype(BF16)
     for k, out in enumerate(others):
-        out[...] = slot(lax.rem(me + 2 + k, count)).astype(out.dtype)
-    near_slot[...] = slot(neighbour(me, count, True))
-    far_slot[...] = slot(neighbour(me, count, False))
-    tmp[width * species :] = jnp.zeros((tmp.shape[0] - width * species, tmp.shape[1]), F32)
-    copy.wait()
-    for r in range(width):
-        tmp[r * species : (r + 1) * species] = layer[r]
-    first[...] = tmp[...].astype(BF16)
-
-
-def pack_x(c, fine, forward):
+        out[...] = jnp.concatenate(slot(lax.rem(me + 2 + k, count)), axis=1).astype(BF16)
+    for n, out in enumerate((far, near)):
+        n = 1 - n
+        copies[n].wait()
+        pack_layer([layer[n, r] for r in range(nx)], tmp, species)
+        places = blocks_of(nx, species, nz, pieces)
+        for (row, lane), piece in zip(places, slot(neighbour(me, count, n == 0))):
+            tmp[row : row + species, lane : lane + 128] = piece
+        out[...] = tmp[...].astype(BF16)
+
+
+def pack_y(c, fine):
     nx, ny, species, nz = c.shape
     count, cells = fine.shape[1:]
     stack = padded(species, 8)
     vmem = pl.BlockSpec(memory_space=pltpu.VMEM)
-    rows = layer_rows(ny, species)
-    outs = [jax.ShapeDtypeStruct((rows, nz), BF16)]
-    outs += [jax.ShapeDtypeStruct((species, cells), F32)] * 2
-    outs += [jax.ShapeDtypeStruct((species, cells), BF16)]
-    kind = F32 if forward else BF16
-    outs += [jax.ShapeDtypeStruct((species, cells), kind)] * max(count - 3, 0)
+    rows = layer_rows(nx, species, -(-cells // nz))
+    outs = [jax.ShapeDtypeStruct((rows, nz), BF16)] * 2
+    outs += [jax.ShapeDtypeStruct((species, cells), BF16)] * (1 + max(count - 3, 0))
     return pl.pallas_call(
-        pack_x_kernel,
+        pack_y_kernel,
         in_specs=[pl.BlockSpec(memory_space=pltpu.HBM)] * 2,
         out_specs=[vmem] * len(outs),
         out_shape=outs,
         scratch_shapes=[
-            pltpu.VMEM((ny, species, nz), F32),
+            pltpu.VMEM((2, nx, species, nz), F32),
             pltpu.VMEM((rows, nz), F32),
             pltpu.VMEM(fine.shape, BF16),
             pltpu.VMEM((cells // 128, stack * padded(count, 8), 128), F32),
-            pltpu.SemaphoreType.DMA,
+            pltpu.SemaphoreType.DMA((2,)),
             pltpu.SemaphoreType.DMA,
         ],
         compiler_params=pltpu.CompilerParams(vmem_limit_bytes=LIMIT),
-        name="pack_x",
+        name="pack_y",
     )(
         pltpu.with_memory_space_constraint(c, pltpu.HBM),
         pltpu.with_memory_space_constraint(fine, pltpu.HBM),
     )
 
 
-def pack_layer(columns, tmp, species):
-    for r, value in enumerate(columns):
-        tmp[r * species : (r + 1) * species] = value
-    below = len(columns) * species
-    tmp[below:] = jnp.zeros((tmp.shape[0] - below, tmp.shape[1]), F32)
-
-
-def pack_slot(value, places, tmp):
-    for q, (row, lane) in enumerate(places):
-        tmp[row : row + value.shape[0], lane : lane + 128] = value[:, q * 128 : (q + 1) * 128]
-
-
-def pack_near_kernel(c, slot, *refs):
-    second, (out, tmp) = refs[:-2], refs[-2:]
-    nx, ny, species, nz = c.shape
-    y = jnp.where(lax.axis_index("yz") % 2 == 0, ny - 1, 0)
-    pack_layer([c[r, y] for r in range(nx)], tmp, species)
-    places = blocks_of(nx, species, nz, slot.shape[1])
-    pack_slot(slot[...], places[0], tmp)
-    for value in second:
-        pack_slot(value[...], places[1], tmp)
+def pack_x_kernel(c, after, out, tmp, x):
+    nx, ny, species, _ = c.shape
+    pack_layer([c[x, r] for r in range(ny)], tmp, species)
     out[...] = tmp[...].astype(BF16)
 
 
-def pack_far_kernel(c, slot, *refs):
-    passed, (out, x_out, tmp, x_tmp) = refs[:-4], refs[-4:]
-    nx, ny, species, nz = c.shape
-    y = jnp.where(lax.axis_index("yz") % 2 == 0, 0, ny - 1)
-    pack_layer([c[r, y] for r in range(nx)], tmp, species)
-    places = blocks_of(nx, species, nz, slot.shape[1])
-    pack_slot(slot[...], places[0], tmp)
-    for ref in passed:
-        tmp[nx * species :] = jnp.where(
-            passes(tmp.shape[0] - nx * species, nz, places[1], nx * species, species),
-            ref[...].astype(F32)[nx * species :],
-            tmp[nx * species :],
-        )
-    out[...] = tmp[...].astype(BF16)
-    x = (1 - upper()) * (nx - 1)
-    pack_layer([c[x, r] for r in range(ny)], x_tmp, species)
-    x_out[...] = x_tmp[...].astype(BF16)
-
-
-def passes(rows, lanes, places, base, species):
-    row = lax.broadcasted_iota(jnp.int32, (rows, lanes), 0)
-    lane = lax.broadcasted_iota(jnp.int32, (rows, lanes), 1)
-    mask = row < 0
-    for at, start in places:
-        here = (row >= at - base) & (row < at - base + species)
-        mask = mask | (here & (lane >= start) & (lane < start + 128))
-    return mask
-
-
-def pack_y(kernel, name, c, slot, second, groups, extra):
+def pack_x(c, after, x):
     nx, ny, species, nz = c.shape
     vmem = pl.BlockSpec(memory_space=pltpu.VMEM)
-    shapes = [(layer_rows(nx, species, groups), nz)]
-    if extra:
-        shapes.append((layer_rows(ny, species), nz))
+    shape = (layer_rows(ny, species), nz)
     return pl.pallas_call(
-        kernel,
-        in_specs=[vmem] * (2 + len(second)),
-        out_specs=[vmem] * len(shapes),
-        out_shape=[jax.ShapeDtypeStruct(shape, BF16) for shape in shapes],
-        scratch_shapes=[pltpu.VMEM(shape, F32) for shape in shapes],
+        functools.partial(pack_x_kernel, x=x),
+        in_specs=[vmem, pl.BlockSpec(memory_space=pl.ANY)],
+        out_specs=vmem,
+        out_shape=jax.ShapeDtypeStruct(shape, BF16),
+        scratch_shapes=[pltpu.VMEM(shape, F32)],
         compiler_params=pltpu.CompilerParams(vmem_limit_bytes=LIMIT),
-        name=name,
-    )(c, slot, *second)
+        name="pack_x",
+    )(c, after)
 
 
 def coarse_kernel(
@@ -334,12 +285,6 @@
         columns[k, c.shape[2] :] = jnp.zeros((stack - c.shape[2], nz), F32)
         columns[k, : c.shape[2]] = c[k // width, k % width]
     diff = column(coef, stack)
-    lane = lanes_of(stack)
-    starts = [pos[0, i] * width for i in range(boxes)]
-    masks = [tiles_of(stack, nz, start, width) for start in starts]
-    tiles = old.shape[1] // 128
-    zero = jnp.zeros((stack, 128), F32)
-    gathered = [[[zero] * tiles for _ in range(2)] for _ in range(boxes)]
     for first in range(0, count, 2 * GROUP):
         some = range(first, min(first + 2 * GROUP, count))
         made = react_all(mixed, [columns[k] for k in some])
@@ -357,20 +302,21 @@
                 lap = lap + columns[k + 1]
             value = mine + diff * lap + made[k - first]
             adv[k] = value
-            if x in (0, width - 1) and y in (0, width - 1):
-                continue
-            for i in range(boxes):
-                for n, source in enumerate((mine, value)):
-                    moved = turn(fold(source, masks[i]), k * width - starts[i])
-                    for t in range(tiles):
-                        low, high = k * width - t * 128, (k + 1) * width - t * 128
-                        if high > 0 and low < 128:
-                            here = (lane >= low) & (lane < high)
-                            gathered[i][n][t] = jnp.where(here, moved, gathered[i][n][t])
+    lanes = old.shape[1]
+    cell = lanes_of(stack, lanes) // width
     for i in range(boxes):
-        for out, parts_of in zip((old, new), gathered[i]):
-            for t in range(tiles):
-                out[i * stack : (i + 1) * stack, t * 128 : (t + 1) * 128] = parts_of[t]
+        lane = pos[0, i] * width
+        start = pl.multiple_of(jnp.minimum(lane // 128, nz // 128 - 2) * 128, 128)
+        offset = lane - start
+        for source, out in ((columns, old), (adv, new)):
+            total = jnp.zeros((stack, lanes), F32)
+            for k in range(count):
+                if k // width in (0, width - 1) and k % width in (0, width - 1):
+                    continue
+                part = source[k, :, pl.ds(start, PATCH)]
+                moved = pltpu.roll(part, (k * width - offset) & (PATCH - 1), 1)
+                total = jnp.where(cell == k, moved, total)
+            out[i * stack : (i + 1) * stack] = total
 
 
 def coarse_part(pos, c, rate, coef, table, stack, after):
@@ -432,51 +378,66 @@
     return total
 
 
-def x_faces_kernel(pos, owner, first, own, after, *refs, count, half):
-    others, (from_x, field, wide) = refs[:-3], refs[-3:]
-    stack = from_x.shape[0]
-    species = own.shape[0]
-    nz = first.shape[1]
-    wide[...] = first[...].astype(F32)
-    zero = jnp.zeros(from_x.shape, F32)
-    from_x[...] = gather_faces(pos, [wide], [1 - upper()], half, stack, species, nz, zero)
-    me = lax.axis_index("yz")
+def y_faces_kernel(pos, owner, near, far, x_low, own, after, *refs):
+    others, (from_y, start, wide, x_wide) = refs[:-4], refs[-4:]
+    stack = from_y.shape[0]
+    species, cells = own.shape
+    nz = near.shape[1]
+    boxes = pos.shape[1]
+    width = (near.shape[0] // species) - (-(-cells // nz))
+    half = width - 2
+    wide[0] = near[...].astype(F32)
+    wide[1] = far[...].astype(F32)
+    x_wide[...] = x_low[...].astype(F32)
+    me, count = lax.axis_index("yz"), lax.axis_size("yz")
+    odd = me % 2
+    zero = jnp.zeros(from_y.shape, F32)
+    layers = (wide.at[0], wide.at[1], x_wide)
+    from_y[...] = gather_faces(pos, layers, (3 - odd, 2 + odd, 0), half, stack, species, nz, zero)
     direct = [ref[...].astype(F32) for ref in (own, *others)]
-    for i in range(pos.shape[1]):
+    places = blocks_of(width, species, nz, cells // 128)
+    edge = species // 8 * 8
+    for i in range(boxes):
+        by_near = owner[0, i] == neighbour(me, count, True)
+        by_far = owner[0, i] == neighbour(me, count, False)
+        at = i * stack
+        start[at + edge : at + stack] = jnp.zeros((stack - edge, cells), F32)
         back = lax.rem(me - owner[0, i] + count, count)
         value = direct[0]
         for k in range(len(others)):
             value = jnp.where(back == k + 2, direct[k + 1], value)
-        edge = species // 8 * 8
-        field[i * stack + edge : (i + 1) * stack] = jnp.zeros((stack - edge, value.shape[1]), F32)
-        field[i * stack : i * stack + species] = value
-
-
-def x_faces(pos, owner, first, own, after, others, half, stack, count):
+        for q, (row, lane) in enumerate(places):
+            part = value[:, q * 128 : (q + 1) * 128]
+            sent = [wide[n, row : row + species, lane : lane + 128] for n in range(2)]
+            part = jnp.where(by_far, sent[1], jnp.where(by_near, sent[0], part))
+            start[at : at + species, q * 128 : (q + 1) * 128] = part
+
+
+def y_faces(pos, owner, near, far, x_low, own, after, others, half, stack):
     vmem = pl.BlockSpec(memory_space=pltpu.VMEM)
     boxes = pos.shape[1]
     lanes = padded(boxes * 4 * half * half, 128)
     return pl.pallas_call(
-        functools.partial(x_faces_kernel, count=count, half=half),
-        in_specs=[vmem] * 4 + [pl.BlockSpec(memory_space=pl.ANY)] + [vmem] * len(others),
+        y_faces_kernel,
+        in_specs=[vmem] * 6 + [pl.BlockSpec(memory_space=pl.ANY)] + [vmem] * len(others),
         out_specs=[vmem] * 2,
         out_shape=[
             jax.ShapeDtypeStruct((stack, lanes), F32),
             jax.ShapeDtypeStruct((boxes * stack, own.shape[1]), F32),
         ],
-        scratch_shapes=[pltpu.VMEM(first.shape, F32)],
+        scratch_shapes=[pltpu.VMEM((2, *near.shape), F32), pltpu.VMEM(x_low.shape, F32)],
         compiler_params=pltpu.CompilerParams(vmem_limit_bytes=LIMIT),
         cost_estimate=pl.CostEstimate(flops=10**9, bytes_accessed=ORDER, transcendentals=0),
-        name="x_faces",
-    )(pos, owner, first, own, after, *others)
-
-
-def fine_kernel(pos, owner, x_second, near, far, start, *refs, count, edge):
-    old, new, mix, coef, spread, ghost, from_x = refs[:7]
+        name="y_faces",
+    )(pos, owner, near, far, x_low, own, after, *others)
+
+
+def fine_kernel(pos, owner, x_high, field, *refs, count, edge):
+    old, new, mix, coef, spread, ghost, from_y = refs[:7]
     packets = refs[7 : 7 + count]
-    fix, kept, final, field, wide, x_wide = refs[7 + count :]
+    fix, kept, final, wide = refs[7 + count :]
     species = packets[0].shape[0]
-    stack = from_x.shape[0]
+    stack = from_y.shape[0]
     boxes = final.shape[0] // stack
     cells = final.shape[1]
     me = lax.axis_index("yz")
@@ -486,24 +447,9 @@
         pairs = [value[at : at + 2 * stack] for at in range(0, boxes * stack, 2 * stack)]
         return jnp.concatenate([react(mixed, pair) for pair in pairs], axis=0)
 
-    nz = near.shape[1]
+    nz = x_high.shape[1]
     half = edge // 2
-    wide[0] = near[...].astype(F32)
-    wide[1] = far[...].astype(F32)
-    first_at, second_at = blocks_of(half + 2, species, nz, cells)
-    near_at, far_at = neighbour(me, count, True), neighbour(me, count, False)
-    sources = [(near_at, 0, first_at), (far_at, 1, first_at)]
-    if count == 4:
-        sources.append((lax.rem(me + 2, count), 1, second_at))
-    for i in range(boxes):
-        for q in range(cells // 128):
-            mine = (slice(i * stack, (i + 1) * stack), slice(q * 128, (q + 1) * 128))
-            part = start[mine]
-            for source, n, places in sources:
-                row, at = places[q]
-                sent = wide[n, row : row + stack, at : at + 128]
-                part = jnp.where(owner[0, i] == source, sent, part)
-            field[mine] = part
+    wide[...] = x_high[...].astype(F32)
     diff = jnp.concatenate([column(coef, stack)] * boxes, axis=0)
     old_v, new_v = old[...], new[...]
     sums = old_v + new_v
@@ -526,11 +472,7 @@
     first = field[...]
     second = first + 2.0 * diff * (inside(first) + ghost0) + 0.5 * reaction(first)
     base = second + diff * (2.0 * inside(second) + ghost1) + 0.5 * reaction(second)
-    odd = me % 2
-    x_wide[...] = x_second[...].astype(F32)
-    layers = (x_wide, wide.at[0], wide.at[1])
-    faces = (upper(), 3 - odd, 2 + odd)
-    total = gather_faces(pos, layers, faces, half, stack, species, nz, from_x[...])
+    total = gather_faces(pos, [wide], [1], half, stack, species, nz, from_y[...])
     kept[...] = total
     stacked = by_box(total, boxes, half).astype(BF16)
     value = base + diff * diff * dot(stacked, ghost[...])
@@ -562,43 +504,27 @@
     fix[...] = diff * result
 
 
-def fine_part(pos, owner, second, near, far, start, old, new, mix, coef, spread, ghost, from_x, edge, count):
+def fine_part(pos, owner, high, start, old, new, mix, coef, spread, ghost, from_y, count, edge):
     boxes = owner.shape[1]
-    stack = from_x.shape[0]
+    stack = from_y.shape[0]
     cells = start.shape[1]
     vmem = pl.BlockSpec(memory_space=pltpu.VMEM)
     return pl.pallas_call(
         functools.partial(fine_kernel, count=count, edge=edge),
-        in_specs=[vmem] * 13,
+        in_specs=[vmem] * 11,
         out_specs=[vmem] * (count + 3),
         out_shape=[jax.ShapeDtypeStruct((coef.shape[1], cells), BF16)] * count
         + [
             jax.ShapeDtypeStruct((boxes * stack, old.shape[1]), F32),
-            jax.ShapeDtypeStruct(from_x.shape, F32),
+            jax.ShapeDtypeStruct(from_y.shape, F32),
             jax.ShapeDtypeStruct((boxes * stack, cells), F32),
         ],
         scratch_shapes=[
-            pltpu.VMEM((boxes * stack, cells), F32),
-            pltpu.VMEM((2, *near.shape), F32),
-            pltpu.VMEM(second.shape, F32),
+            pltpu.VMEM(high.shape, F32),
         ],
         compiler_params=pltpu.CompilerParams(vmem_limit_bytes=LIMIT),
         name="fine_part",
-    )(
-        pos,
-        owner,
-        second,
-        near,
-        far,
-        start,
-        old,
-        new,
-        mix,
-        coef,
-        spread,
-        ghost,
-        from_x,
-    )
+    )(pos, owner, high, start, old, new, mix, coef, spread, ghost, from_y)
 
 
 def delta_of(field, kept, fix, coef, average, place, half, stack):
@@ -620,11 +546,9 @@
     diff = column(coef, stack)
     even = lax.axis_index("yz") % 2 == 0
     rows = x_first.shape[0]
-    first_v, second_v = x_first[...].astype(F32), x_second[...].astype(F32)
     near_v, far_v = near[:rows].astype(F32), far[:rows].astype(F32)
-    up = upper() == 1
-    wide[0, :rows] = jnp.where(up, first_v, second_v)
-    wide[1, :rows] = jnp.where(up, second_v, first_v)
+    wide[0, :rows] = x_first[...].astype(F32)
+    wide[1, : x_second.shape[0]] = x_second[...].astype(F32)
     wide[2, :rows] = jnp.where(even, far_v, near_v)
     wide[3, :rows] = jnp.where(even, near_v, far_v)
     boxes = delta.shape[0] // stack
@@ -712,16 +636,6 @@
     return one_way + [(j, i) for i, j in one_way]
 
 
-def slabs(by):
-    slabs_count, count = lax.axis_size("gx"), lax.axis_size("yz")
-    pairs = []
-    for g in range(slabs_count):
-        for j in range(count):
-            to = (g + (by if j < count // 2 else -by)) % slabs_count
-            pairs.append((g * count + j, to * count + j))
-    return pairs
-
-
 def partner(me, k, count):
     return me ^ k if count & (count - 1) == 0 else lax.rem(me + k, count)
 
@@ -742,31 +656,25 @@
     c = jnp.transpose(coarse_state, (1, 2, 0, 3))
 
     fine = jnp.transpose(fine_state, (1, 0, 2))
-    forward = count == 4
-    forward = count == 4
-    groups = -(-(2 if forward else 1) * fine.shape[2] // c.shape[3])
-    x_first, near_slot, far_slot, own, *others = pack_x(c, fine, forward)
-    relayed = others if forward else []
-    (near,) = pack_y(pack_near_kernel, "pack_near", c, near_slot, relayed, groups, False)
-    near = lax.ppermute(near, "yz", mutual("yz", 1))
-    relayed = [near] if forward else []
-    far, x_second = pack_y(pack_far_kernel, "pack_far", c, far_slot, relayed, groups, True)
+    near, far, own, *others = pack_y(c, fine)
+    x_high = pack_x(c, own, c.shape[0] - 1)
+    x_low = pack_x(c, x_high, 0)
     halos = [
-        lax.ppermute(x_first, ("gx", "yz"), slabs(-1)),
-        lax.ppermute(x_second, ("gx", "yz"), slabs(1)),
-        near,
+        lax.ppermute(x_high, "gx", ring("gx", 1)),
+        lax.ppermute(x_low, "gx", ring("gx", -1)),
+        lax.ppermute(near, "yz", mutual("yz", 1)),
         lax.ppermute(far, "yz", mutual("yz", -1)),
     ]
-    if forward:
-        others = []
     others = [lax.ppermute(slot, "yz", ring("yz", 2 + k)) for k, slot in enumerate(others)]
 
     adv, old, new, mix, spread, ghost = coarse_part(
-        pos, c, rate, coef, table, stack, far
+        pos, c, rate, coef, table, stack, x_low
     )
-    from_x, start = x_faces(pos, owner, halos[0], own, old, others, half, stack, count)
+    from_y, start = y_faces(
+        pos, owner, *halos[2:], halos[0], own, old, others, half, stack
+    )
     made = fine_part(
-        pos, owner, *halos[1:], start, old, new, mix, coef, spread, ghost, from_x, 2 * half, count
+        pos, owner, halos[1], start, old, new, mix, coef, spread, ghost, from_y, count, 2 * half
     )
     packets, (fix, kept, field) = made[:count], made[count:]
 
@@ -775,7 +683,8 @@
         pairs = [(i, i ^ k if even else (i + k) % count) for i in range(count)]
         return lax.ppermute(value, "yz", pairs)
 
-    back = [packets[0]] + [swap(packets[k], k) for k in range(1, count)]
+    back = [swap(packets[k], k) for k in range(count - 1, 0, -1)][::-1]
+    back = [packets[0]] + back
     coarse_next = correct(pos, adv, halos, coef, field, kept, fix, table, half)
 
     source = lax.broadcasted_iota(jnp.int32, (count, 1, 1), 0)

time: 21.7 us -> 20 us (0.922)
  waiting for transfers between devices: 4.47 us -> 2.09 us
  starting transfers between devices: 8.16 us -> 10.3 us
  Pallas kernels: 6.97 us -> 5.89 us
  local copies, waits for them, and re-layouts: 0.36 us -> 0.05 us
    ppermute x3 -> x4, waiting for transfers between devices: 3.99 us -> 0.95 us  [the longest x1 0.69 us: local(): lax.ppermute(x_low, 'gx', ring('gx', -1))]
    ppermute x1, starting transfers between devices: 0.07 us -> 2.64 us  [local(): lax.ppermute(far, 'yz', mutual('yz', -1))]
    pallas_call x1, Pallas kernels: 3.27 us -> 2.12 us  [coarse_part(): pl.pallas_call(coarse_kernel, in_specs=[vmem] * 6 + [pl.BlockSpec(memory_...]
    ppermute x3, waiting for transfers between devices: 0.48 us -> 1.14 us  [swap(): return lax.ppermute(value, 'yz', pairs)]
    ppermute x3 -> x4, starting transfers between devices: 6.17 us -> 5.74 us  [the longest x1 3.17 us: local(): lax.ppermute(x_low, 'gx', ring('gx', -1))]
    unnamed x18, local copies, waits for them, and re-layouts: 0.36 us -> 0.05 us
  transfers between devices with their start and end apart: 7 -> 8, of which waited for: 2 -> 3; matrix products, arithmetic and copies ran while one was open for 0% -> 0% of each run, Pallas kernels for 24% -> 20%
where the time goes in v2:
time: 20 us; the launch traced here: 19.9 us
  starting transfers between devices  10.3 us (52%)
  Pallas kernels  5.89 us (29%)
  waiting for transfers between devices  2.09 us (10%)
  between operations  0.77 us (4%)
  other arithmetic  0.76 us (4%)
    ppermute x1, starting transfers between devices, local(): lax.ppermute(x_low, 'gx', ring('gx', -1))  3.17 us
    ppermute x1, starting transfers between devices, local(): lax.ppermute(far, 'yz', mutual('yz', -1))  2.64 us
    pallas_call x1, Pallas kernels, coarse_part(): pl.pallas_call(coarse_kernel, in_specs=[vmem] * 6 + [pl.BlockSpec(memory_...  2.12 us
    ppermute x3, starting transfers between devices, swap(): return lax.ppermute(value, 'yz', pairs)  1.93 us
    ppermute x1, starting transfers between devices, local(): lax.ppermute(x_high, 'gx', ring('gx', 1))  1.54 us
    pallas_call x1, Pallas kernels, correct(): pl.pallas_call(functools.partial(correct_kernel, half=half), in_specs=[vm...  1.52 us
    pallas_call x1, Pallas kernels, pack_y(): pl.pallas_call(pack_y_kernel, in_specs=[pl.BlockSpec(memory_space=pltpu.H...  1.3 us
    ppermute x3, waiting for transfers between devices, swap(): return lax.ppermute(value, 'yz', pairs)  1.14 us
  transfers between devices with their start and end apart: 8, of which 3 were waited for; matrix products, arithmetic and copies ran while one was open for 0% of the time, Pallas kernels for 20%

profile of v2, /device:TPU:0, one launch (start us, length us, event | category | flops | bytes accessed | tf_op | source)
XLA Modules:
  0.0 19.9 jit_solution(9932048226438565774)
XLA Ops:
  0.6 1.3 %pack_y.1 = (bf16[176,384]{1,0:T(8,128)(2,1)S(1)}, bf16[176,384]{1,0:T(8,128)(2,1)S(1)}, bf16[21,512]{1,0:T(8,128)(2,1)S(1)}, bf16[21,512]{1,0:T(8,128)(2,1)S(1)}) custom-call(f32[6,6,21,384]{3,2,1,0:T(8,128)} %bitcast.6, bf16[21,4,512]{2,1,0:T(4,128)(2,1)} %bitcast.20), custom_call_target="tpu_custom_call" | custom-call | tf_op jit(solution)/shard_map/pack_y/pallas_call | solution.py:232
  1.9 0.5 %collective-permute-start.2 = (bf16[176,384]{1,0:T(8,128)(2,1)S(1)}, bf16[176,384]{1,0:T(8,128)(2,1)S(1)}, u32[]{:S(2)}, u32[]{:S(2)}) collective-permute-start(bf16[176,384]{1,0:T(8,128)(2,1)S(1)} %get-tuple-element.23), channel_id=1, source_target_pairs={{0,1},{2,3},{1,0},{3,2},{4,5},{6,7},{5,4},{7,6},{8,9},{10,11},{9,8... | collective-permute-start | bytes 405512 | tf_op jit(solution)/shard_map/ppermute | solution.py:665
  2.5 2.6 %collective-permute-start.3 = (bf16[176,384]{1,0:T(8,128)(2,1)S(1)}, bf16[176,384]{1,0:T(8,128)(2,1)S(1)}, u32[]{:S(2)}, u32[]{:S(2)}) collective-permute-start(bf16[176,384]{1,0:T(8,128)(2,1)S(1)} %get-tuple-element.24), channel_id=1, source_target_pairs={{0,3},{2,1},{3,0},{1,2},{4,7},{6,5},{7,4},{5,6},{8,11},{10,9},{11,... | collective-permute-start | bytes 405512 | tf_op jit(solution)/shard_map/ppermute | solution.py:666
  5.1 0.0 copy-start.6
  5.1 0.0 copy-start.7
  5.2 1.5 %collective-permute-start = (bf16[128,384]{1,0:T(8,128)(2,1)S(1)}, bf16[128,384]{1,0:T(8,128)(2,1)S(1)}, u32[]{:S(2)}, u32[]{:S(2)}) collective-permute-start(bf16[128,384]{1,0:T(8,128)(2,1)S(1)} %pack_x.2.after), channel_id=1, source_target_pairs={{0,4},{4,8},{8,12},{12,16},{16,20},{20,24},{24,28},{28,0},{1,5},{5... | collective-permute-start | bytes 294920 | tf_op jit(solution)/shard_map/ppermute | solution.py:663
  6.7 0.5 %collective-permute-start.4 = (bf16[21,512]{1,0:T(8,128)(2,1)S(1)}, bf16[21,512]{1,0:T(8,128)(2,1)S(1)}, u32[]{:S(2)}, u32[]{:S(2)}) collective-permute-start(bf16[21,512]{1,0:T(8,128)(2,1)S(1)} %get-tuple-element.26), channel_id=1, source_target_pairs={{0,2},{1,3},{2,0},{3,1},{4,6},{5,7},{6,4},{7,5},{8,10},{9,11},{10,... | collective-permute-start | bytes 64520 | tf_op jit(solution)/shard_map/ppermute | solution.py:668
  7.3 0.0 copy-start.8
  7.3 3.2 %collective-permute-start.1 = (bf16[128,384]{1,0:T(8,128)(2,1)S(1)}, bf16[128,384]{1,0:T(8,128)(2,1)S(1)}, u32[]{:S(2)}, u32[]{:S(2)}) collective-permute-start(bf16[128,384]{1,0:T(8,128)(2,1)S(1)} %pack_x.3.after), channel_id=1, source_target_pairs={{0,28},{4,0},{8,4},{12,8},{16,12},{20,16},{24,20},{28,24},{1,29},{... | collective-permute-start | bytes 294920 | tf_op jit(solution)/shard_map/ppermute | solution.py:664
  10.5 2.1 %coarse_part.1 = (f32[36,24,384]{2,1,0:T(8,128)S(1)}, f32[48,256]{1,0:T(8,128)S(1)}, f32[48,256]{1,0:T(8,128)S(1)}, bf16[96,96]{1,0:T(8,128)(2,1)S(1)}, bf16[256...) custom-call(s32[1,2]{1,0:T(1,128)S(1)} %bitcast.10, f32[6,6,21,384]{3,2,1,0:T(8,128)S(1)} %bitcast.9, ...), custom_call_target="tpu_custom_call" | custom-call | flops 232243200 | bytes 3483648 | tf_op jit(solution)/shard_map/coarse_part/pallas_call | solution.py:329
  12.6 0.0 collective-permute-done.4.refs_0_
  12.6 0.3 %collective-permute-done.x_low.x_first = bf16[128,384]{1,0:T(8,128)(2,1)S(1)} collective-permute-done((bf16[128,384]{1,0:T(8,128)(2,1)S(1)}, bf16[128,384]{1,0:T(8,128)(2,1)S(1)}, u32[]{:S(2)}, u32[]{:S(2)}) %collective-permute-start) | collective-permute-done | bytes 98336 | tf_op jit(solution)/shard_map/ppermute | solution.py:663
  12.9 0.0 copy-start.1
  12.9 0.0 copy-start.4
  12.9 0.2 %y_faces.1 = (f32[24,128]{1,0:T(8,128)S(1)}, f32[48,512]{1,0:T(8,128)S(1)}) custom-call(s32[1,2]{1,0:T(1,128)S(1)} %bitcast.11, s32[1,2]{1,0:T(1,128)S(1)} %bitcast.17, bf16[176,384]{1,0:T(8,128)(2,1)S(1)} %collective-permute-done.2.near, bf16[176,384]{1,0:T(8,128)(2,1)S(1)} %collective-permute-done.3.far, ...), custom_call_target="tpu_custom_call" | custom-call | flops 1000000000 | bytes 20000000 | tf_op jit(solution)/shard_map/y_faces/pallas_call | solution.py:420
  13.2 0.7 %collective-permute-done.1.x_high.x_second = bf16[128,384]{1,0:T(8,128)(2,1)S(1)} collective-permute-done((bf16[128,384]{1,0:T(8,128)(2,1)S(1)}, bf16[128,384]{1,0:T(8,128)(2,1)S(1)}, u32[]{:S(2)}, u32[]{:S(2)}) %collective-permute-start.1) | collective-permute-done | bytes 98336 | tf_op jit(solution)/shard_map/ppermute | solution.py:664
  13.8 0.7 %fine_part.1 = (bf16[21,512]{1,0:T(8,128)(2,1)S(1)}, bf16[21,512]{1,0:T(8,128)(2,1)S(1)}, bf16[21,512]{1,0:T(8,128)(2,1)S(1)}, bf16[21,512]{1,0:T(8,128)(2,1)S(1...) custom-call(s32[1,2]{1,0:T(1,128)S(1)} %bitcast.12, s32[1,2]{1,0:T(1,128)S(1)} %bitcast.18, ...), custom_call_target="tpu_custom_call" | custom-call | tf_op jit(solution)/shard_map/fine_part/pallas_call | solution.py:512
  14.5 0.8 %collective-permute-start.5 = (bf16[21,512]{1,0:T(8,128)(2,1)S(1)}, bf16[21,512]{1,0:T(8,128)(2,1)S(1)}, u32[]{:S(2)}, u32[]{:S(2)}) collective-permute-start(bf16[21,512]{1,0:T(8,128)(2,1)S(1)} %get-tuple-element.36), channel_id=1, source_target_pairs={{0,3},{1,2},{2,1},{3,0},{4,7},{5,6},{6,5},{7,4},{8,11},{9,10},{10,... | collective-permute-start | bytes 64520 | tf_op jit(solution)/shard_map/ppermute | solution.py:684
  15.3 0.7 %collective-permute-start.6 = (bf16[21,512]{1,0:T(8,128)(2,1)S(1)}, bf16[21,512]{1,0:T(8,128)(2,1)S(1)}, u32[]{:S(2)}, u32[]{:S(2)}) collective-permute-start(bf16[21,512]{1,0:T(8,128)(2,1)S(1)} %get-tuple-element.37), channel_id=1, source_target_pairs={{0,2},{1,3},{2,0},{3,1},{4,6},{5,7},{6,4},{7,5},{8,10},{9,11},{10,... | collective-permute-start | bytes 64520 | tf_op jit(solution)/shard_map/ppermute | solution.py:684
  16.0 0.5 %collective-permute-start.7 = (bf16[21,512]{1,0:T(8,128)(2,1)S(1)}, bf16[21,512]{1,0:T(8,128)(2,1)S(1)}, u32[]{:S(2)}, u32[]{:S(2)}) collective-permute-start(bf16[21,512]{1,0:T(8,128)(2,1)S(1)} %get-tuple-element.38), channel_id=1, source_target_pairs={{0,1},{1,0},{2,3},{3,2},{4,5},{5,4},{6,7},{7,6},{8,9},{9,8},{10,11... | collective-permute-start | bytes 64520 | tf_op jit(solution)/shard_map/ppermute | solution.py:684
  16.4 1.5 %coarse_correct.1 = f32[6,6,21,384]{3,2,1,0:T(8,128)} custom-call(s32[1,2]{1,0:T(1,128)S(1)} %bitcast.13, f32[36,24,384]{2,1,0:T(8,128)S(1)} %get-tuple-element.22.adv, bf16[128,384]{1,0:T(8,128)(2,1)S(1)} %collective-permute-done.x_low.x_first, bf16[128,384]{1,0:T(8,128)(2,1)S(1)} %collective-permute-done.1.x_high.x_second, ...), custom_call_target="tpu_custom_call" | custom-call | flops 6635520 | bytes 3981312 | tf_op jit(solution)/shard_map/coarse_correct/pallas_call | solution.py:600
  18.0 0.0 collective-permute-done.5
  18.0 1.1 %collective-permute-done.6 = bf16[21,512]{1,0:T(8,128)(2,1)S(1)} collective-permute-done((bf16[21,512]{1,0:T(8,128)(2,1)S(1)}, bf16[21,512]{1,0:T(8,128)(2,1)S(1)}, u32[]{:S(2)}, u32[]{:S(2)}) %collective-permute-start.6) | collective-permute-done | bytes 21536 | tf_op jit(solution)/shard_map/ppermute | solution.py:684
  19.1 0.8 %select_select_fusion = bf16[4,21,512]{2,0,1:T(4,128)(2,1)} fusion(pred[4]{0:T(512)(128)(4,1)S(1)} %get-tuple-element.41, pred[4]{0:T(512)(128)(4,1)S(1)} %fusion.2, pred[4]{0:T(512)(128)(4,1)S(1)} %get-tuple-element.40, bf16[21,512]{1,0:T(8,128)(2,1)S(1)} %get-tuple-element.39, bf16[21,512]{1,0:T(8,128)(2,1)S(1)} %collective-permute-done.7, ...), kind=kLoop, calls=%fused_computation | loop fusion | flops 129024 | bytes 172044 | tf_op jit(solution)/shard_map/jit(_where)/select_n | solution.py:694
  (20 shorter events, 0.1 us)
Async XLA Ops:
  0.6 4.5 %copy-start = (f32[21,6,6,384]{3,0,2,1:T(8,128)S(1)}, f32[21,6,6,384]{3,0,2,1:T(8,128)}, u32[]{:S(2)}) copy-start(f32[21,6,6,384]{3,0,2,1:T(8,128)} %param.10) | copy-start | bytes 3483652
  1.9 10.9 %collective-permute-start.2 = (bf16[176,384]{1,0:T(8,128)(2,1)S(1)}, bf16[176,384]{1,0:T(8,128)(2,1)S(1)}, u32[]{:S(2)}, u32[]{:S(2)}) collective-permute-start(bf16[176,384]{1,0:T(8,128)(2,1)S(1)} %get-tuple-element.23), channel_id=1, source_target_pairs={{0,1},{2,3},{1,0},{3,2},{4,5},{6,7},{5,4},{7,6},{8,9},{10,11},{9,8... | collective-permute-start | bytes 405512 | tf_op jit(solution)/shard_map/ppermute | solution.py:665
  2.5 10.4 %collective-permute-start.3 = (bf16[176,384]{1,0:T(8,128)(2,1)S(1)}, bf16[176,384]{1,0:T(8,128)(2,1)S(1)}, u32[]{:S(2)}, u32[]{:S(2)}) collective-permute-start(bf16[176,384]{1,0:T(8,128)(2,1)S(1)} %get-tuple-element.24), channel_id=1, source_target_pairs={{0,3},{2,1},{3,0},{1,2},{4,7},{6,5},{7,4},{5,6},{8,11},{10,9},{11,... | collective-permute-start | bytes 405512 | tf_op jit(solution)/shard_map/ppermute | solution.py:666
  5.1 5.3 %copy-start.2 = (f32[256,512]{1,0:T(8,128)S(1)}, f32[256,512]{1,0:T(8,128)}, u32[]{:S(2)}) copy-start(f32[256,512]{1,0:T(8,128)} %constant.18.clone.spread) | copy-start | bytes 1572868
  5.1 5.3 %copy-start.3 = (f32[128,512]{1,0:T(8,128)S(1)}, f32[128,512]{1,0:T(8,128)}, u32[]{:S(2)}) copy-start(f32[128,512]{1,0:T(8,128)} %constant.19.clone.ghost) | copy-start | bytes 786436
  5.1 5.3 %copy-start.5 = (f32[21,21]{1,0:T(8,128)S(1)}, f32[21,21]{1,0:T(8,128)}, u32[]{:S(2)}) copy-start(f32[21,21]{1,0:T(8,128)} %rate.1) | copy-start | bytes 5296
  5.1 5.3 %copy-start.6 = (s32[1,1,2]{2,1,0:T(1,128)S(1)}, s32[1,1,2]{2,1,0:T(1,128)}, u32[]{:S(2)}) copy-start(s32[1,1,2]{2,1,0:T(1,128)} %param.14) | copy-start | bytes 28
  5.1 5.3 %copy-start.7 = (f32[21]{0:T(128)S(1)}, f32[21]{0:T(128)}, u32[]{:S(2)}) copy-start(f32[21]{0:T(128)} %param.12) | copy-start | bytes 256
  5.2 7.7 %collective-permute-start = (bf16[128,384]{1,0:T(8,128)(2,1)S(1)}, bf16[128,384]{1,0:T(8,128)(2,1)S(1)}, u32[]{:S(2)}, u32[]{:S(2)}) collective-permute-start(bf16[128,384]{1,0:T(8,128)(2,1)S(1)} %pack_x.2.after), channel_id=1, source_target_pairs={{0,4},{4,8},{8,12},{12,16},{16,20},{20,24},{24,28},{28,0},{1,5},{5... | collective-permute-start | bytes 294920 | tf_op jit(solution)/shard_map/ppermute | solution.py:663
  6.7 5.9 %collective-permute-start.4 = (bf16[21,512]{1,0:T(8,128)(2,1)S(1)}, bf16[21,512]{1,0:T(8,128)(2,1)S(1)}, u32[]{:S(2)}, u32[]{:S(2)}) collective-permute-start(bf16[21,512]{1,0:T(8,128)(2,1)S(1)} %get-tuple-element.26), channel_id=1, source_target_pairs={{0,2},{1,3},{2,0},{3,1},{4,6},{5,7},{6,4},{7,5},{8,10},{9,11},{10,... | collective-permute-start | bytes 64520 | tf_op jit(solution)/shard_map/ppermute | solution.py:668
  7.3 5.6 %copy-start.8 = (s32[1,1,2]{2,1,0:T(1,128)S(1)}, s32[1,1,2]{2,1,0:T(1,128)}, u32[]{:S(2)}) copy-start(s32[1,1,2]{2,1,0:T(1,128)} %param.15) | copy-start | bytes 28
  7.3 6.6 %collective-permute-start.1 = (bf16[128,384]{1,0:T(8,128)(2,1)S(1)}, bf16[128,384]{1,0:T(8,128)(2,1)S(1)}, u32[]{:S(2)}, u32[]{:S(2)}) collective-permute-start(bf16[128,384]{1,0:T(8,128)(2,1)S(1)} %pack_x.3.after), channel_id=1, source_target_pairs={{0,28},{4,0},{8,4},{12,8},{16,12},{20,16},{24,20},{28,24},{1,29},{... | collective-permute-start | bytes 294920 | tf_op jit(solution)/shard_map/ppermute | solution.py:664
  12.9 3.5 %copy-start.1 = (f32[512,256]{1,0:T(8,128)S(1)}, f32[512,256]{1,0:T(8,128)}, u32[]{:S(2)}) copy-start(f32[512,256]{1,0:T(8,128)} %constant.20.clone.average) | copy-start | bytes 1572868
  12.9 3.5 %copy-start.4 = (f32[128,256]{1,0:T(8,128)S(1)}, f32[128,256]{1,0:T(8,128)}, u32[]{:S(2)}) copy-start(f32[128,256]{1,0:T(8,128)} %constant.21.clone.place) | copy-start | bytes 393220
  14.5 3.5 %collective-permute-start.5 = (bf16[21,512]{1,0:T(8,128)(2,1)S(1)}, bf16[21,512]{1,0:T(8,128)(2,1)S(1)}, u32[]{:S(2)}, u32[]{:S(2)}) collective-permute-start(bf16[21,512]{1,0:T(8,128)(2,1)S(1)} %get-tuple-element.36), channel_id=1, source_target_pairs={{0,3},{1,2},{2,1},{3,0},{4,7},{5,6},{6,5},{7,4},{8,11},{9,10},{10,... | collective-permute-start | bytes 64520 | tf_op jit(solution)/shard_map/ppermute | solution.py:684
  15.3 3.9 %collective-permute-start.6 = (bf16[21,512]{1,0:T(8,128)(2,1)S(1)}, bf16[21,512]{1,0:T(8,128)(2,1)S(1)}, u32[]{:S(2)}, u32[]{:S(2)}) collective-permute-start(bf16[21,512]{1,0:T(8,128)(2,1)S(1)} %get-tuple-element.37), channel_id=1, source_target_pairs={{0,2},{1,3},{2,0},{3,1},{4,6},{5,7},{6,4},{7,5},{8,10},{9,11},{10,... | collective-permute-start | bytes 64520 | tf_op jit(solution)/shard_map/ppermute | solution.py:684
  16.0 3.2 %collective-permute-start.7 = (bf16[21,512]{1,0:T(8,128)(2,1)S(1)}, bf16[21,512]{1,0:T(8,128)(2,1)S(1)}, u32[]{:S(2)}, u32[]{:S(2)}) collective-permute-start(bf16[21,512]{1,0:T(8,128)(2,1)S(1)} %get-tuple-element.38), channel_id=1, source_target_pairs={{0,1},{1,0},{2,3},{3,2},{4,5},{5,4},{6,7},{7,6},{8,9},{9,8},{10,11... | collective-permute-start | bytes 64520 | tf_op jit(solution)/shard_map/ppermute | solution.py:684

commit v3 on v2

--- a/solution.py
+++ b/solution.py
@@ -173,9 +173,10 @@
     return padded((width + groups) * species, 16)
 
 
-def blocks_of(width, species, nz, pieces):
+def blocks_of(width, species, nz, pieces, slot=0):
     across = nz // 128
-    return [((width + n // across) * species, n % across * 128) for n in range(pieces)]
+    numbers = range(slot * pieces, (slot + 1) * pieces)
+    return [((width + n // across) * species, n % across * 128) for n in numbers]
 
 
 def pack_layer(columns, tmp, species):
@@ -215,10 +216,13 @@
         n = 1 - n
         copies[n].wait()
         pack_layer([layer[n, r] for r in range(nx)], tmp, species)
-        places = blocks_of(nx, species, nz, pieces)
-        for (row, lane), piece in zip(places, slot(neighbour(me, count, n == 0))):
-            tmp[row : row + species, lane : lane + 128] = piece
-        out[...] = tmp[...].astype(BF16)
+        sent = [slot(neighbour(me, count, n == 0))]
+        if n == 0 and relays(count):
+            sent.append(slot(lax.rem(me + 2, count)))
+        for m, value in enumerate(sent):
+            for (row, lane), piece in zip(blocks_of(nx, species, nz, pieces, m), value):
+                tmp[row : row + species, lane : lane + 128] = piece
+        out[...] = tmp[: out.shape[0]].astype(BF16)
 
 
 def pack_y(c, fine):
@@ -226,9 +230,11 @@
     count, cells = fine.shape[1:]
     stack = padded(species, 8)
     vmem = pl.BlockSpec(memory_space=pltpu.VMEM)
-    rows = layer_rows(nx, species, -(-cells // nz))
-    outs = [jax.ShapeDtypeStruct((rows, nz), BF16)] * 2
-    outs += [jax.ShapeDtypeStruct((species, cells), BF16)] * (1 + max(count - 3, 0))
+    far_rows = layer_rows(nx, species, -(-cells // nz))
+    rows = layer_rows(nx, species, -(-2 * cells // nz)) if relays(count) else far_rows
+    outs = [jax.ShapeDtypeStruct((n, nz), BF16) for n in (rows, far_rows)]
+    direct = 0 if relays(count) else max(count - 3, 0)
+    outs += [jax.ShapeDtypeStruct((species, cells), BF16)] * (1 + direct)
     return pl.pallas_call(
         pack_y_kernel,
         in_specs=[pl.BlockSpec(memory_space=pltpu.HBM)] * 2,
@@ -248,6 +254,31 @@
         pltpu.with_memory_space_constraint(c, pltpu.HBM),
         pltpu.with_memory_space_constraint(fine, pltpu.HBM),
     )
+
+
+def relays(count):
+    return count == 4
+
+
+def relay_kernel(near, after, out, wide, width):
+    species, cells = out.shape
+    wide[...] = near[...].astype(F32)
+    places = blocks_of(width, species, near.shape[1], cells // 128, 1)
+    pieces = [wide[row : row + species, lane : lane + 128] for row, lane in places]
+    out[...] = jnp.concatenate(pieces, axis=1).astype(BF16)
+
+
+def relay(near, after, width, species, cells):
+    vmem = pl.BlockSpec(memory_space=pltpu.VMEM)
+    return pl.pallas_call(
+        functools.partial(relay_kernel, width=width),
+        in_specs=[vmem, pl.BlockSpec(memory_space=pl.ANY)],
+        out_specs=vmem,
+        out_shape=jax.ShapeDtypeStruct((species, cells), BF16),
+        scratch_shapes=[pltpu.VMEM(near.shape, F32)],
+        compiler_params=pltpu.CompilerParams(vmem_limit_bytes=LIMIT),
+        name="relay",
+    )(near, after)
 
 
 def pack_x_kernel(c, after, out, tmp, x):
@@ -378,23 +409,21 @@
     return total
 
 
-def y_faces_kernel(pos, owner, near, far, x_low, own, after, *refs):
-    others, (from_y, start, wide, x_wide) = refs[:-4], refs[-4:]
+def y_faces_kernel(pos, owner, near, far, own, after, from_y, start, wide):
     stack = from_y.shape[0]
     species, cells = own.shape
     nz = near.shape[1]
     boxes = pos.shape[1]
-    width = (near.shape[0] // species) - (-(-cells // nz))
+    width = far.shape[0] // species - -(-cells // nz)
     half = width - 2
     wide[0] = near[...].astype(F32)
-    wide[1] = far[...].astype(F32)
-    x_wide[...] = x_low[...].astype(F32)
+    wide[1, : far.shape[0]] = far[...].astype(F32)
     me, count = lax.axis_index("yz"), lax.axis_size("yz")
     odd = me % 2
     zero = jnp.zeros(from_y.shape, F32)
-    layers = (wide.at[0], wide.at[1], x_wide)
-    from_y[...] = gather_faces(pos, layers, (3 - odd, 2 + odd, 0), half, stack, species, nz, zero)
-    direct = [ref[...].astype(F32) for ref in (own, *others)]
+    layers = (wide.at[0], wide.at[1])
+    from_y[...] = gather_faces(pos, layers, (3 - odd, 2 + odd), half, stack, species, nz, zero)
+    direct = own[...].astype(F32)
     places = blocks_of(width, species, nz, cells // 128)
     edge = species // 8 * 8
     for i in range(boxes):
@@ -402,40 +431,37 @@
         by_far = owner[0, i] == neighbour(me, count, False)
         at = i * stack
         start[at + edge : at + stack] = jnp.zeros((stack - edge, cells), F32)
-        back = lax.rem(me - owner[0, i] + count, count)
-        value = direct[0]
-        for k in range(len(others)):
-            value = jnp.where(back == k + 2, direct[k + 1], value)
         for q, (row, lane) in enumerate(places):
-            part = value[:, q * 128 : (q + 1) * 128]
+            part = direct[:, q * 128 : (q + 1) * 128]
             sent = [wide[n, row : row + species, lane : lane + 128] for n in range(2)]
             part = jnp.where(by_far, sent[1], jnp.where(by_near, sent[0], part))
             start[at : at + species, q * 128 : (q + 1) * 128] = part
 
 
-def y_faces(pos, owner, near, far, x_low, own, after, others, half, stack):
+def y_faces(pos, owner, near, far, own, after, half, stack):
     vmem = pl.BlockSpec(memory_space=pltpu.VMEM)
     boxes = pos.shape[1]
     lanes = padded(boxes * 4 * half * half, 128)
     return pl.pallas_call(
         y_faces_kernel,
-        in_specs=[vmem] * 6 + [pl.BlockSpec(memory_space=pl.ANY)] + [vmem] * len(others),
+        in_specs=[vmem] * 5 + [pl.BlockSpec(memory_space=pl.ANY)],
         out_specs=[vmem] * 2,
         out_shape=[
             jax.ShapeDtypeStruct((stack, lanes), F32),
             jax.ShapeDtypeStruct((boxes * stack, own.shape[1]), F32),
         ],
-        scratch_shapes=[pltpu.VMEM((2, *near.shape), F32), pltpu.VMEM(x_low.shape, F32)],
+        scratch_shapes=[pltpu.VMEM((2, *near.shape), F32)],
         compiler_params=pltpu.CompilerParams(vmem_limit_bytes=LIMIT),
         cost_estimate=pl.CostEstimate(flops=10**9, bytes_accessed=ORDER, transcendentals=0),
         name="y_faces",
-    )(pos, owner, near, far, x_low, own, after, *others)
-
-
-def fine_kernel(pos, owner, x_high, field, *refs, count, edge):
+    )(pos, owner, near, far, own, after)
+
+
+def fine_kernel(pos, owner, x_low, x_high, start, *refs, count, edge):
+    others, refs = refs[: count - 3], refs[count - 3 :]
     old, new, mix, coef, spread, ghost, from_y = refs[:7]
     packets = refs[7 : 7 + count]
-    fix, kept, final, wide = refs[7 + count :]
+    fix, kept, final, field, wide = refs[7 + count :]
     species = packets[0].shape[0]
     stack = from_y.shape[0]
     boxes = final.shape[0] // stack
@@ -447,9 +473,19 @@
         pairs = [value[at : at + 2 * stack] for at in range(0, boxes * stack, 2 * stack)]
         return jnp.concatenate([react(mixed, pair) for pair in pairs], axis=0)
 
-    nz = x_high.shape[1]
+    nz = x_low.shape[1]
     half = edge // 2
-    wide[...] = x_high[...].astype(F32)
+    wide[0, : x_low.shape[0]] = x_low[...].astype(F32)
+    wide[1, : x_high.shape[0]] = x_high[...].astype(F32)
+    sent = [ref[...].astype(F32) for ref in others]
+    for i in range(boxes):
+        at = i * stack
+        field[at : at + stack] = start[at : at + stack]
+        back = lax.rem(me - owner[0, i] + count, count)
+        value = start[at : at + species]
+        for k in range(len(sent)):
+            value = jnp.where(back == k + 2, sent[k], value)
+        field[at : at + species] = value
     diff = jnp.concatenate([column(coef, stack)] * boxes, axis=0)
     old_v, new_v = old[...], new[...]
     sums = old_v + new_v
@@ -472,7 +508,8 @@
     first = field[...]
     second = first + 2.0 * diff * (inside(first) + ghost0) + 0.5 * reaction(first)
     base = second + diff * (2.0 * inside(second) + ghost1) + 0.5 * reaction(second)
-    total = gather_faces(pos, [wide], [1], half, stack, species, nz, from_y[...])
+    layers = (wide.at[0], wide.at[1])
+    total = gather_faces(pos, layers, (0, 1), half, stack, species, nz, from_y[...])
     kept[...] = total
     stacked = by_box(total, boxes, half).astype(BF16)
     value = base + diff * diff * dot(stacked, ghost[...])
@@ -504,14 +541,15 @@
     fix[...] = diff * result
 
 
-def fine_part(pos, owner, high, start, old, new, mix, coef, spread, ghost, from_y, count, edge):
+def fine_part(pos, owner, low, high, start, others, old, new, mix, coef, spread, ghost, from_y, edge):
     boxes = owner.shape[1]
+    count = len(others) + 3
     stack = from_y.shape[0]
     cells = start.shape[1]
     vmem = pl.BlockSpec(memory_space=pltpu.VMEM)
     return pl.pallas_call(
         functools.partial(fine_kernel, count=count, edge=edge),
-        in_specs=[vmem] * 11,
+        in_specs=[vmem] * (count + 9),
         out_specs=[vmem] * (count + 3),
         out_shape=[jax.ShapeDtypeStruct((coef.shape[1], cells), BF16)] * count
         + [
@@ -520,11 +558,12 @@
             jax.ShapeDtypeStruct((boxes * stack, cells), F32),
         ],
         scratch_shapes=[
-            pltpu.VMEM(high.shape, F32),
+            pltpu.VMEM((boxes * stack, cells), F32),
+            pltpu.VMEM((2, *low.shape), F32),
         ],
         compiler_params=pltpu.CompilerParams(vmem_limit_bytes=LIMIT),
         name="fine_part",
-    )(pos, owner, high, start, old, new, mix, coef, spread, ghost, from_y)
+    )(pos, owner, low, high, start, *others, old, new, mix, coef, spread, ghost, from_y)
 
 
 def delta_of(field, kept, fix, coef, average, place, half, stack):
@@ -625,6 +664,38 @@
     )
 
 
+def unpack_kernel(*refs):
+    packets, (out, rows) = refs[:-2], refs[-2:]
+    species, cells = packets[0].shape
+    count = len(packets)
+    step = rows.shape[1] // padded(species, 8)
+    me = lax.axis_index("yz")
+    for n, packet in enumerate(packets):
+        source = origin(me, (count - n) % count, count)
+        value = packet[...].astype(F32)
+        for q in range(cells // 128):
+            rows[q, pl.ds(source, species, stride=step), :] = value[:, q * 128 : (q + 1) * 128]
+    for s in range(species):
+        pieces = [rows[q, s * step : s * step + count] for q in range(cells // 128)]
+        out[s] = jnp.concatenate(pieces, axis=1).astype(BF16)
+
+
+def unpack(packets):
+    species, cells = packets[0].shape
+    count = len(packets)
+    vmem = pl.BlockSpec(memory_space=pltpu.VMEM)
+    rows = padded(species, 8) * padded(count, 8)
+    return pl.pallas_call(
+        unpack_kernel,
+        in_specs=[vmem] * count,
+        out_specs=vmem,
+        out_shape=jax.ShapeDtypeStruct((species, count, cells), BF16),
+        scratch_shapes=[pltpu.VMEM((cells // 128, rows, 128), F32)],
+        compiler_params=pltpu.CompilerParams(vmem_limit_bytes=LIMIT),
+        name="unpack",
+    )(packets[0], *packets[:0:-1])
+
+
 def ring(axis, by):
     count = lax.axis_size(axis)
     return [(i, (i + by) % count) for i in range(count)]
@@ -665,16 +736,19 @@
         lax.ppermute(near, "yz", mutual("yz", 1)),
         lax.ppermute(far, "yz", mutual("yz", -1)),
     ]
-    others = [lax.ppermute(slot, "yz", ring("yz", 2 + k)) for k, slot in enumerate(others)]
+    if relays(count):
+        after = passed = relay(halos[2], x_low, width, *own.shape)
+        others = [lax.ppermute(passed, "yz", mutual("yz", -1))]
+    else:
+        after = x_low
+        others = [lax.ppermute(slot, "yz", ring("yz", 2 + k)) for k, slot in enumerate(others)]
 
     adv, old, new, mix, spread, ghost = coarse_part(
-        pos, c, rate, coef, table, stack, x_low
+        pos, c, rate, coef, table, stack, after
     )
-    from_y, start = y_faces(
-        pos, owner, *halos[2:], halos[0], own, old, others, half, stack
-    )
+    from_y, start = y_faces(pos, owner, *halos[2:], own, old, half, stack)
     made = fine_part(
-        pos, owner, halos[1], start, old, new, mix, coef, spread, ghost, from_y, count, 2 * half
+        pos, owner, *halos[:2], start, others, old, new, mix, coef, spread, ghost, from_y, 2 * half
     )
     packets, (fix, kept, field) = made[:count], made[count:]
 
@@ -683,15 +757,10 @@
         pairs = [(i, i ^ k if even else (i + k) % count) for i in range(count)]
         return lax.ppermute(value, "yz", pairs)
 
-    back = [swap(packets[k], k) for k in range(count - 1, 0, -1)][::-1]
-    back = [packets[0]] + back
+    back = [packets[0]] + [swap(packets[k], k) for k in range(1, count)]
     coarse_next = correct(pos, adv, halos, coef, field, kept, fix, table, half)
 
-    source = lax.broadcasted_iota(jnp.int32, (count, 1, 1), 0)
-    turn = origin(me, source, count)
-    fine_next = jnp.broadcast_to(back[0][None], (count,) + back[0].shape)
-    for k in range(1, count):
-        fine_next = jnp.where(turn == k, back[k][None], fine_next)
+    fine_next = jnp.transpose(unpack(back), (1, 0, 2))
     return jnp.transpose(coarse_next, (2, 0, 1, 3)), fine_next
 
 

time: 20 us -> 19.8 us (0.990)
  Pallas kernels: 5.89 us -> 6.67 us
  other arithmetic: 0.76 us -> 0 us
  starting transfers between devices: 10.3 us -> 9.99 us
    select_n x1 -> x0, other arithmetic: 0.75 us -> none  [local(): fine_next = jnp.where(turn == k, back[k][None], fine_next)]
    pallas_call x1 -> x3, Pallas kernels: 0.23 us -> 0.93 us  [the longest x1 0.71 us: unpack(): pl.pallas_call(unpack_kernel, in_specs=[vmem] * count, out_specs=vmem, ou...]
    ppermute x1, starting transfers between devices: 0.51 us -> 0.07 us  [local(): others = [lax.ppermute(passed, 'yz', mutual('yz', -1))]]
    ppermute x1, waiting for transfers between devices: 0.26 us -> 0.01 us  [local(): lax.ppermute(x_high, 'gx', ring('gx', 1))]
    ppermute x1, waiting for transfers between devices: 0.69 us -> 0.91 us  [local(): lax.ppermute(x_low, 'gx', ring('gx', -1))]
where the time goes in v3:
time: 19.8 us; the launch traced here: 19.7 us
  starting transfers between devices  9.99 us (50%)
  Pallas kernels  6.67 us (34%)
  waiting for transfers between devices  2.18 us (11%)
  between operations  0.79 us (4%)
    ppermute x1, starting transfers between devices, local(): lax.ppermute(x_low, 'gx', ring('gx', -1))  3.28 us
    ppermute x1, starting transfers between devices, local(): lax.ppermute(far, 'yz', mutual('yz', -1))  2.64 us
    pallas_call x1, Pallas kernels, coarse_part(): pl.pallas_call(coarse_kernel, in_specs=[vmem] * 6 + [pl.BlockSpec(memory_...  2.17 us
    ppermute x3, starting transfers between devices, swap(): return lax.ppermute(value, 'yz', pairs)  1.93 us
    ppermute x1, starting transfers between devices, local(): lax.ppermute(x_high, 'gx', ring('gx', 1))  1.54 us
    pallas_call x1, Pallas kernels, correct(): pl.pallas_call(functools.partial(correct_kernel, half=half), in_specs=[vm...  1.52 us
    pallas_call x1, Pallas kernels, pack_y(): pl.pallas_call(pack_y_kernel, in_specs=[pl.BlockSpec(memory_space=pltpu.H...  1.31 us
    ppermute x3, waiting for transfers between devices, swap(): return lax.ppermute(value, 'yz', pairs)  1.26 us
  transfers between devices with their start and end apart: 8, of which 3 were waited for; matrix products, arithmetic and copies ran while one was open for 0% of the time, Pallas kernels for 20%

profile of v3, /device:TPU:0, one launch (start us, length us, event | category | flops | bytes accessed | tf_op | source)
XLA Modules:
  0.0 19.7 jit_solution(7749599405666017634)
XLA Ops:
  0.6 1.3 %pack_y.1 = (bf16[192,384]{1,0:T(8,128)(2,1)S(1)}, bf16[176,384]{1,0:T(8,128)(2,1)S(1)}, bf16[21,512]{1,0:T(8,128)(2,1)S(1)}) custom-call(f32[6,6,21,384]{3,2,1,0:T(8,128)} %bitcast.7, bf16[21,4,512]{2,1,0:T(4,128)(2,1)} %bitcast.22), custom_call_target="tpu_custom_call" | custom-call | tf_op jit(solution)/shard_map/pack_y/pallas_call | solution.py:238
  2.0 0.5 %collective-permute-start = (bf16[192,384]{1,0:T(8,128)(2,1)S(1)}, bf16[192,384]{1,0:T(8,128)(2,1)S(1)}, u32[]{:S(2)}, u32[]{:S(2)}) collective-permute-start(bf16[192,384]{1,0:T(8,128)(2,1)S(1)} %get-tuple-element.20), channel_id=1, source_target_pairs={{0,1},{2,3},{1,0},{3,2},{4,5},{6,7},{5,4},{7,6},{8,9},{10,11},{9,8... | collective-permute-start | bytes 442376 | tf_op jit(solution)/shard_map/ppermute | solution.py:736
  2.5 2.6 %collective-permute-start.3 = (bf16[176,384]{1,0:T(8,128)(2,1)S(1)}, bf16[176,384]{1,0:T(8,128)(2,1)S(1)}, u32[]{:S(2)}, u32[]{:S(2)}) collective-permute-start(bf16[176,384]{1,0:T(8,128)(2,1)S(1)} %get-tuple-element.23), channel_id=1, source_target_pairs={{0,3},{2,1},{3,0},{1,2},{4,7},{6,5},{7,4},{5,6},{8,11},{10,9},{11,... | collective-permute-start | bytes 405512 | tf_op jit(solution)/shard_map/ppermute | solution.py:737
  5.1 0.0 copy-start.6
  5.1 0.0 copy-start.7
  5.2 1.5 %collective-permute-start.1 = (bf16[128,384]{1,0:T(8,128)(2,1)S(1)}, bf16[128,384]{1,0:T(8,128)(2,1)S(1)}, u32[]{:S(2)}, u32[]{:S(2)}) collective-permute-start(bf16[128,384]{1,0:T(8,128)(2,1)S(1)} %pack_x.2.after), channel_id=1, source_target_pairs={{0,4},{4,8},{8,12},{12,16},{16,20},{20,24},{24,28},{28,0},{1,5},{5... | collective-permute-start | bytes 294920 | tf_op jit(solution)/shard_map/ppermute | solution.py:734
  6.8 0.0 copy-start.8
  6.8 3.3 %collective-permute-start.2 = (bf16[128,384]{1,0:T(8,128)(2,1)S(1)}, bf16[128,384]{1,0:T(8,128)(2,1)S(1)}, u32[]{:S(2)}, u32[]{:S(2)}) collective-permute-start(bf16[128,384]{1,0:T(8,128)(2,1)S(1)} %pack_x.3.after), channel_id=1, source_target_pairs={{0,28},{4,0},{8,4},{12,8},{16,12},{20,16},{24,20},{28,24},{1,29},{... | collective-permute-start | bytes 294920 | tf_op jit(solution)/shard_map/ppermute | solution.py:735
  10.1 0.0 collective-permute-done.near
  10.1 0.1 collective-permute-start.4
  10.2 2.2 %coarse_part.1 = (f32[36,24,384]{2,1,0:T(8,128)S(1)}, f32[48,256]{1,0:T(8,128)S(1)}, f32[48,256]{1,0:T(8,128)S(1)}, bf16[96,96]{1,0:T(8,128)(2,1)S(1)}, bf16[256...) custom-call(s32[1,2]{1,0:T(1,128)S(1)} %bitcast.11, f32[6,6,21,384]{3,2,1,0:T(8,128)S(1)} %bitcast.10, ...), custom_call_target="tpu_custom_call" | custom-call | flops 232243200 | bytes 3483648 | tf_op jit(solution)/shard_map/coarse_part/pallas_call | solution.py:360
  12.4 0.0 copy-start.1
  12.4 0.0 copy-start.4
  12.4 0.2 %y_faces.1 = (f32[24,128]{1,0:T(8,128)S(1)}, f32[48,512]{1,0:T(8,128)S(1)}) custom-call(s32[1,2]{1,0:T(1,128)S(1)} %bitcast.12, s32[1,2]{1,0:T(1,128)S(1)} %bitcast.18, bf16[192,384]{1,0:T(8,128)(2,1)S(1)} %collective-permute-done.near, bf16[176,384]{1,0:T(8,128)(2,1)S(1)} %collective-permute-done.3.far, bf16[21,512]{1,0:T(8,128)(2,1)S(1)} %get-tuple-element.21.after.own, ...), custom_call_target="tpu_custom_call" | custom-call | flops 1000000000 | bytes 20000000 | tf_op jit(solution)/shard_map/y_faces/pallas_call | solution.py:445
  12.6 0.9 %collective-permute-done.2.x_high.x_second = bf16[128,384]{1,0:T(8,128)(2,1)S(1)} collective-permute-done((bf16[128,384]{1,0:T(8,128)(2,1)S(1)}, bf16[128,384]{1,0:T(8,128)(2,1)S(1)}, u32[]{:S(2)}, u32[]{:S(2)}) %collective-permute-start.2) | collective-permute-done | bytes 98336 | tf_op jit(solution)/shard_map/ppermute | solution.py:735
  13.6 0.0 collective-permute-done.1.x_low.x_first
  13.6 0.7 %fine_part.1 = (bf16[21,512]{1,0:T(8,128)(2,1)S(1)}, bf16[21,512]{1,0:T(8,128)(2,1)S(1)}, bf16[21,512]{1,0:T(8,128)(2,1)S(1)}, bf16[21,512]{1,0:T(8,128)(2,1)S(1...) custom-call(s32[1,2]{1,0:T(1,128)S(1)} %bitcast.13, s32[1,2]{1,0:T(1,128)S(1)} %bitcast.19, ...), custom_call_target="tpu_custom_call" | custom-call | tf_op jit(solution)/shard_map/fine_part/pallas_call | solution.py:550
  14.2 0.9 %collective-permute-start.5 = (bf16[21,512]{1,0:T(8,128)(2,1)S(1)}, bf16[21,512]{1,0:T(8,128)(2,1)S(1)}, u32[]{:S(2)}, u32[]{:S(2)}) collective-permute-start(bf16[21,512]{1,0:T(8,128)(2,1)S(1)} %get-tuple-element.35), channel_id=1, source_target_pairs={{0,3},{1,2},{2,1},{3,0},{4,7},{5,6},{6,5},{7,4},{8,11},{9,10},{10,... | collective-permute-start | bytes 64520 | tf_op jit(solution)/shard_map/ppermute | solution.py:758
  15.1 0.6 %collective-permute-start.6 = (bf16[21,512]{1,0:T(8,128)(2,1)S(1)}, bf16[21,512]{1,0:T(8,128)(2,1)S(1)}, u32[]{:S(2)}, u32[]{:S(2)}) collective-permute-start(bf16[21,512]{1,0:T(8,128)(2,1)S(1)} %get-tuple-element.36), channel_id=1, source_target_pairs={{0,2},{1,3},{2,0},{3,1},{4,6},{5,7},{6,4},{7,5},{8,10},{9,11},{10,... | collective-permute-start | bytes 64520 | tf_op jit(solution)/shard_map/ppermute | solution.py:758
  15.7 0.4 %collective-permute-start.7 = (bf16[21,512]{1,0:T(8,128)(2,1)S(1)}, bf16[21,512]{1,0:T(8,128)(2,1)S(1)}, u32[]{:S(2)}, u32[]{:S(2)}) collective-permute-start(bf16[21,512]{1,0:T(8,128)(2,1)S(1)} %get-tuple-element.37), channel_id=1, source_target_pairs={{0,1},{1,0},{2,3},{3,2},{4,5},{5,4},{6,7},{7,6},{8,9},{9,8},{10,11... | collective-permute-start | bytes 64520 | tf_op jit(solution)/shard_map/ppermute | solution.py:758
  16.2 1.5 %coarse_correct.1 = f32[6,6,21,384]{3,2,1,0:T(8,128)} custom-call(s32[1,2]{1,0:T(1,128)S(1)} %bitcast.14, f32[36,24,384]{2,1,0:T(8,128)S(1)} %get-tuple-element.22.adv, bf16[128,384]{1,0:T(8,128)(2,1)S(1)} %collective-permute-done.1.x_low.x_first, bf16[128,384]{1,0:T(8,128)(2,1)S(1)} %collective-permute-done.2.x_high.x_second, ...), custom_call_target="tpu_custom_call" | custom-call | flops 6635520 | bytes 3981312 | tf_op jit(solution)/shard_map/coarse_correct/pallas_call | solution.py:639
  17.7 0.1 collective-permute-done.5.refs_1_
  17.8 1.2 %collective-permute-done.6.refs_2_ = bf16[21,512]{1,0:T(8,128)(2,1)S(1)} collective-permute-done((bf16[21,512]{1,0:T(8,128)(2,1)S(1)}, bf16[21,512]{1,0:T(8,128)(2,1)S(1)}, u32[]{:S(2)}, u32[]{:S(2)}) %collective-permute-start.6) | collective-permute-done | bytes 21536 | tf_op jit(solution)/shard_map/ppermute | solution.py:758
  19.0 0.7 %unpack.1 = bf16[21,4,512]{2,1,0:T(4,128)(2,1)} custom-call(bf16[21,512]{1,0:T(8,128)(2,1)S(1)} %get-tuple-element.34.refs_0_, bf16[21,512]{1,0:T(8,128)(2,1)S(1)} %collective-permute-done.5.refs_1_, bf16[21,512]{1,0:T(8,128)(2,1)S(1)} %collective-permute-done.6.refs_2_, bf16[21,512]{1,0:T(8,128)(2,1)S(1)} %collective-permute-done.7.refs_3_), custom_call_target="tpu_custom_call" | custom-call | tf_op jit(solution)/shard_map/unpack/pallas_call | solution.py:688
  (19 shorter events, 0.1 us)
Async XLA Ops:
  0.6 4.5 %copy-start = (f32[21,6,6,384]{3,0,2,1:T(8,128)S(1)}, f32[21,6,6,384]{3,0,2,1:T(8,128)}, u32[]{:S(2)}) copy-start(f32[21,6,6,384]{3,0,2,1:T(8,128)} %param.10) | copy-start | bytes 3483652
  2.0 8.1 %collective-permute-start = (bf16[192,384]{1,0:T(8,128)(2,1)S(1)}, bf16[192,384]{1,0:T(8,128)(2,1)S(1)}, u32[]{:S(2)}, u32[]{:S(2)}) collective-permute-start(bf16[192,384]{1,0:T(8,128)(2,1)S(1)} %get-tuple-element.20), channel_id=1, source_target_pairs={{0,1},{2,3},{1,0},{3,2},{4,5},{6,7},{5,4},{7,6},{8,9},{10,11},{9,8... | collective-permute-start | bytes 442376 | tf_op jit(solution)/shard_map/ppermute | solution.py:736
  2.5 9.9 %collective-permute-start.3 = (bf16[176,384]{1,0:T(8,128)(2,1)S(1)}, bf16[176,384]{1,0:T(8,128)(2,1)S(1)}, u32[]{:S(2)}, u32[]{:S(2)}) collective-permute-start(bf16[176,384]{1,0:T(8,128)(2,1)S(1)} %get-tuple-element.23), channel_id=1, source_target_pairs={{0,3},{2,1},{3,0},{1,2},{4,7},{6,5},{7,4},{5,6},{8,11},{10,9},{11,... | collective-permute-start | bytes 405512 | tf_op jit(solution)/shard_map/ppermute | solution.py:737
  5.1 5.0 %copy-start.2 = (f32[256,512]{1,0:T(8,128)S(1)}, f32[256,512]{1,0:T(8,128)}, u32[]{:S(2)}) copy-start(f32[256,512]{1,0:T(8,128)} %constant.8.clone.spread) | copy-start | bytes 1572868
  5.1 5.1 %copy-start.3 = (f32[128,512]{1,0:T(8,128)S(1)}, f32[128,512]{1,0:T(8,128)}, u32[]{:S(2)}) copy-start(f32[128,512]{1,0:T(8,128)} %constant.9.clone.ghost) | copy-start | bytes 786436
  5.1 5.1 %copy-start.5 = (f32[21,21]{1,0:T(8,128)S(1)}, f32[21,21]{1,0:T(8,128)}, u32[]{:S(2)}) copy-start(f32[21,21]{1,0:T(8,128)} %rate.1) | copy-start | bytes 5296
  5.1 5.1 %copy-start.6 = (s32[1,1,2]{2,1,0:T(1,128)S(1)}, s32[1,1,2]{2,1,0:T(1,128)}, u32[]{:S(2)}) copy-start(s32[1,1,2]{2,1,0:T(1,128)} %param.14) | copy-start | bytes 28
  5.1 5.1 %copy-start.7 = (f32[21]{0:T(128)S(1)}, f32[21]{0:T(128)}, u32[]{:S(2)}) copy-start(f32[21]{0:T(128)} %param.12) | copy-start | bytes 256
  5.2 8.4 %collective-permute-start.1 = (bf16[128,384]{1,0:T(8,128)(2,1)S(1)}, bf16[128,384]{1,0:T(8,128)(2,1)S(1)}, u32[]{:S(2)}, u32[]{:S(2)}) collective-permute-start(bf16[128,384]{1,0:T(8,128)(2,1)S(1)} %pack_x.2.after), channel_id=1, source_target_pairs={{0,4},{4,8},{8,12},{12,16},{16,20},{20,24},{24,28},{28,0},{1,5},{5... | collective-permute-start | bytes 294920 | tf_op jit(solution)/shard_map/ppermute | solution.py:734
  6.8 5.6 %copy-start.8 = (s32[1,1,2]{2,1,0:T(1,128)S(1)}, s32[1,1,2]{2,1,0:T(1,128)}, u32[]{:S(2)}) copy-start(s32[1,1,2]{2,1,0:T(1,128)} %param.15) | copy-start | bytes 28
  6.8 6.8 %collective-permute-start.2 = (bf16[128,384]{1,0:T(8,128)(2,1)S(1)}, bf16[128,384]{1,0:T(8,128)(2,1)S(1)}, u32[]{:S(2)}, u32[]{:S(2)}) collective-permute-start(bf16[128,384]{1,0:T(8,128)(2,1)S(1)} %pack_x.3.after), channel_id=1, source_target_pairs={{0,28},{4,0},{8,4},{12,8},{16,12},{20,16},{24,20},{28,24},{1,29},{... | collective-permute-start | bytes 294920 | tf_op jit(solution)/shard_map/ppermute | solution.py:735
  10.1 3.5 %collective-permute-start.4 = (bf16[21,512]{1,0:T(8,128)(2,1)S(1)}, bf16[21,512]{1,0:T(8,128)(2,1)S(1)}, u32[]{:S(2)}, u32[]{:S(2)}) collective-permute-start(bf16[21,512]{1,0:T(8,128)(2,1)S(1)} %relay.1.after), channel_id=1, source_target_pairs={{0,3},{2,1},{3,0},{1,2},{4,7},{6,5},{7,4},{5,6},{8,11},{10,9},{11,... | collective-permute-start | bytes 64520 | tf_op jit(solution)/shard_map/ppermute | solution.py:741
  12.4 3.8 %copy-start.1 = (f32[512,256]{1,0:T(8,128)S(1)}, f32[512,256]{1,0:T(8,128)}, u32[]{:S(2)}) copy-start(f32[512,256]{1,0:T(8,128)} %constant.10.clone.average) | copy-start | bytes 1572868
  12.4 3.7 %copy-start.4 = (f32[128,256]{1,0:T(8,128)S(1)}, f32[128,256]{1,0:T(8,128)}, u32[]{:S(2)}) copy-start(f32[128,256]{1,0:T(8,128)} %constant.11.clone.place) | copy-start | bytes 393220
  14.2 3.6 %collective-permute-start.5 = (bf16[21,512]{1,0:T(8,128)(2,1)S(1)}, bf16[21,512]{1,0:T(8,128)(2,1)S(1)}, u32[]{:S(2)}, u32[]{:S(2)}) collective-permute-start(bf16[21,512]{1,0:T(8,128)(2,1)S(1)} %get-tuple-element.35), channel_id=1, source_target_pairs={{0,3},{1,2},{2,1},{3,0},{4,7},{5,6},{6,5},{7,4},{8,11},{9,10},{10,... | collective-permute-start | bytes 64520 | tf_op jit(solution)/shard_map/ppermute | solution.py:758
  15.1 3.8 %collective-permute-start.6 = (bf16[21,512]{1,0:T(8,128)(2,1)S(1)}, bf16[21,512]{1,0:T(8,128)(2,1)S(1)}, u32[]{:S(2)}, u32[]{:S(2)}) collective-permute-start(bf16[21,512]{1,0:T(8,128)(2,1)S(1)} %get-tuple-element.36), channel_id=1, source_target_pairs={{0,2},{1,3},{2,0},{3,1},{4,6},{5,7},{6,4},{7,5},{8,10},{9,11},{10,... | collective-permute-start | bytes 64520 | tf_op jit(solution)/shard_map/ppermute | solution.py:758
  15.7 3.2 %collective-permute-start.7 = (bf16[21,512]{1,0:T(8,128)(2,1)S(1)}, bf16[21,512]{1,0:T(8,128)(2,1)S(1)}, u32[]{:S(2)}, u32[]{:S(2)}) collective-permute-start(bf16[21,512]{1,0:T(8,128)(2,1)S(1)} %get-tuple-element.37), channel_id=1, source_target_pairs={{0,1},{1,0},{2,3},{3,2},{4,5},{5,4},{6,7},{7,6},{8,9},{9,8},{10,11... | collective-permute-start | bytes 64520 | tf_op jit(solution)/shard_map/ppermute | solution.py:758

commit v4 on v3

--- a/solution.py
+++ b/solution.py
@@ -664,14 +664,18 @@
     )
 
 
+def return_order(count):
+    return [0, 2, 3, 1] if count == 4 else list(range(count))
+
+
 def unpack_kernel(*refs):
     packets, (out, rows) = refs[:-2], refs[-2:]
     species, cells = packets[0].shape
     count = len(packets)
     step = rows.shape[1] // padded(species, 8)
     me = lax.axis_index("yz")
-    for n, packet in enumerate(packets):
-        source = origin(me, (count - n) % count, count)
+    for k, packet in zip(return_order(count), packets):
+        source = origin(me, k, count)
         value = packet[...].astype(F32)
         for q in range(cells // 128):
             rows[q, pl.ds(source, species, stride=step), :] = value[:, q * 128 : (q + 1) * 128]
@@ -693,7 +697,7 @@
         scratch_shapes=[pltpu.VMEM((cells // 128, rows, 128), F32)],
         compiler_params=pltpu.CompilerParams(vmem_limit_bytes=LIMIT),
         name="unpack",
-    )(packets[0], *packets[:0:-1])
+    )(*[packets[k] for k in return_order(count)])
 
 
 def ring(axis, by):

time: 19.8 us -> 19.2 us (0.970)
  waiting for transfers between devices: 2.18 us -> 1.27 us
  starting transfers between devices: 9.99 us -> 10.3 us
    ppermute x3, waiting for transfers between devices: 1.26 us -> 0.36 us  [swap(): return lax.ppermute(value, 'yz', pairs)]
    ppermute x3, starting transfers between devices: 1.93 us -> 2.21 us  [swap(): return lax.ppermute(value, 'yz', pairs)]
  transfers between devices with their start and end apart: 8 -> 8, of which waited for: 3 -> 2; matrix products, arithmetic and copies ran while one was open for 0% -> 0% of each run, Pallas kernels for 20% -> 21%
where the time goes in v4:
time: 19.2 us; the launch traced here: 19 us
  starting transfers between devices  10.3 us (54%)
  Pallas kernels  6.68 us (35%)
  waiting for transfers between devices  1.27 us (7%)
  between operations  0.79 us (4%)
    ppermute x1, starting transfers between devices, local(): lax.ppermute(x_low, 'gx', ring('gx', -1))  3.28 us
    ppermute x1, starting transfers between devices, local(): lax.ppermute(far, 'yz', mutual('yz', -1))  2.64 us
    ppermute x3, starting transfers between devices, swap(): return lax.ppermute(value, 'yz', pairs)  2.21 us
    pallas_call x1, Pallas kernels, coarse_part(): pl.pallas_call(coarse_kernel, in_specs=[vmem] * 6 + [pl.BlockSpec(memory_...  2.18 us
    ppermute x1, starting transfers between devices, local(): lax.ppermute(x_high, 'gx', ring('gx', 1))  1.54 us
    pallas_call x1, Pallas kernels, correct(): pl.pallas_call(functools.partial(correct_kernel, half=half), in_specs=[vm...  1.52 us
    pallas_call x1, Pallas kernels, pack_y(): pl.pallas_call(pack_y_kernel, in_specs=[pl.BlockSpec(memory_space=pltpu.H...  1.31 us
    ppermute x1, waiting for transfers between devices, local(): lax.ppermute(x_low, 'gx', ring('gx', -1))  0.9 us
  transfers between devices with their start and end apart: 8, of which 2 were waited for; matrix products, arithmetic and copies ran while one was open for 0% of the time, Pallas kernels for 21%

profile of v4, /device:TPU:0, one launch (start us, length us, event | category | flops | bytes accessed | tf_op | source)
XLA Modules:
  0.0 19.0 jit_solution(9642714080997583849)
XLA Ops:
  0.6 1.3 %pack_y.1 = (bf16[192,384]{1,0:T(8,128)(2,1)S(1)}, bf16[176,384]{1,0:T(8,128)(2,1)S(1)}, bf16[21,512]{1,0:T(8,128)(2,1)S(1)}) custom-call(f32[6,6,21,384]{3,2,1,0:T(8,128)} %bitcast.7, bf16[21,4,512]{2,1,0:T(4,128)(2,1)} %bitcast.22), custom_call_target="tpu_custom_call" | custom-call | tf_op jit(solution)/shard_map/pack_y/pallas_call | solution.py:238
  2.0 0.5 %collective-permute-start = (bf16[192,384]{1,0:T(8,128)(2,1)S(1)}, bf16[192,384]{1,0:T(8,128)(2,1)S(1)}, u32[]{:S(2)}, u32[]{:S(2)}) collective-permute-start(bf16[192,384]{1,0:T(8,128)(2,1)S(1)} %get-tuple-element.20), channel_id=1, source_target_pairs={{0,1},{2,3},{1,0},{3,2},{4,5},{6,7},{5,4},{7,6},{8,9},{10,11},{9,8... | collective-permute-start | bytes 442376 | tf_op jit(solution)/shard_map/ppermute | solution.py:740
  2.5 2.6 %collective-permute-start.3 = (bf16[176,384]{1,0:T(8,128)(2,1)S(1)}, bf16[176,384]{1,0:T(8,128)(2,1)S(1)}, u32[]{:S(2)}, u32[]{:S(2)}) collective-permute-start(bf16[176,384]{1,0:T(8,128)(2,1)S(1)} %get-tuple-element.23), channel_id=1, source_target_pairs={{0,3},{2,1},{3,0},{1,2},{4,7},{6,5},{7,4},{5,6},{8,11},{10,9},{11,... | collective-permute-start | bytes 405512 | tf_op jit(solution)/shard_map/ppermute | solution.py:741
  5.1 0.0 copy-start.6
  5.1 0.0 copy-start.7
  5.2 1.5 %collective-permute-start.1 = (bf16[128,384]{1,0:T(8,128)(2,1)S(1)}, bf16[128,384]{1,0:T(8,128)(2,1)S(1)}, u32[]{:S(2)}, u32[]{:S(2)}) collective-permute-start(bf16[128,384]{1,0:T(8,128)(2,1)S(1)} %pack_x.2.after), channel_id=1, source_target_pairs={{0,4},{4,8},{8,12},{12,16},{16,20},{20,24},{24,28},{28,0},{1,5},{5... | collective-permute-start | bytes 294920 | tf_op jit(solution)/shard_map/ppermute | solution.py:738
  6.8 0.0 copy-start.8
  6.8 3.3 %collective-permute-start.2 = (bf16[128,384]{1,0:T(8,128)(2,1)S(1)}, bf16[128,384]{1,0:T(8,128)(2,1)S(1)}, u32[]{:S(2)}, u32[]{:S(2)}) collective-permute-start(bf16[128,384]{1,0:T(8,128)(2,1)S(1)} %pack_x.3.after), channel_id=1, source_target_pairs={{0,28},{4,0},{8,4},{12,8},{16,12},{20,16},{24,20},{28,24},{1,29},{... | collective-permute-start | bytes 294920 | tf_op jit(solution)/shard_map/ppermute | solution.py:739
  10.1 0.0 collective-permute-done.near
  10.1 0.1 collective-permute-start.4
  10.2 2.2 %coarse_part.1 = (f32[36,24,384]{2,1,0:T(8,128)S(1)}, f32[48,256]{1,0:T(8,128)S(1)}, f32[48,256]{1,0:T(8,128)S(1)}, bf16[96,96]{1,0:T(8,128)(2,1)S(1)}, bf16[256...) custom-call(s32[1,2]{1,0:T(1,128)S(1)} %bitcast.11, f32[6,6,21,384]{3,2,1,0:T(8,128)S(1)} %bitcast.10, ...), custom_call_target="tpu_custom_call" | custom-call | flops 232243200 | bytes 3483648 | tf_op jit(solution)/shard_map/coarse_part/pallas_call | solution.py:360
  12.4 0.0 collective-permute-done.3.far
  12.4 0.0 copy-start.1
  12.4 0.0 copy-start.4
  12.4 0.2 %y_faces.1 = (f32[24,128]{1,0:T(8,128)S(1)}, f32[48,512]{1,0:T(8,128)S(1)}) custom-call(s32[1,2]{1,0:T(1,128)S(1)} %bitcast.12, s32[1,2]{1,0:T(1,128)S(1)} %bitcast.18, bf16[192,384]{1,0:T(8,128)(2,1)S(1)} %collective-permute-done.near, bf16[176,384]{1,0:T(8,128)(2,1)S(1)} %collective-permute-done.3.far, bf16[21,512]{1,0:T(8,128)(2,1)S(1)} %get-tuple-element.21.after.own, ...), custom_call_target="tpu_custom_call" | custom-call | flops 1000000000 | bytes 20000000 | tf_op jit(solution)/shard_map/y_faces/pallas_call | solution.py:445
  12.7 0.9 %collective-permute-done.2.x_high.x_second = bf16[128,384]{1,0:T(8,128)(2,1)S(1)} collective-permute-done((bf16[128,384]{1,0:T(8,128)(2,1)S(1)}, bf16[128,384]{1,0:T(8,128)(2,1)S(1)}, u32[]{:S(2)}, u32[]{:S(2)}) %collective-permute-start.2) | collective-permute-done | bytes 98336 | tf_op jit(solution)/shard_map/ppermute | solution.py:739
  13.6 0.0 collective-permute-done.1.x_low.x_first
  13.6 0.7 %fine_part.1 = (bf16[21,512]{1,0:T(8,128)(2,1)S(1)}, bf16[21,512]{1,0:T(8,128)(2,1)S(1)}, bf16[21,512]{1,0:T(8,128)(2,1)S(1)}, bf16[21,512]{1,0:T(8,128)(2,1)S(1...) custom-call(s32[1,2]{1,0:T(1,128)S(1)} %bitcast.13, s32[1,2]{1,0:T(1,128)S(1)} %bitcast.19, ...), custom_call_target="tpu_custom_call" | custom-call | tf_op jit(solution)/shard_map/fine_part/pallas_call | solution.py:550
  14.2 0.6 %collective-permute-start.5 = (bf16[21,512]{1,0:T(8,128)(2,1)S(1)}, bf16[21,512]{1,0:T(8,128)(2,1)S(1)}, u32[]{:S(2)}, u32[]{:S(2)}) collective-permute-start(bf16[21,512]{1,0:T(8,128)(2,1)S(1)} %get-tuple-element.35), channel_id=1, source_target_pairs={{0,2},{1,3},{2,0},{3,1},{4,6},{5,7},{6,4},{7,5},{8,10},{9,11},{10,... | collective-permute-start | bytes 64520 | tf_op jit(solution)/shard_map/ppermute | solution.py:762
  14.8 0.6 %collective-permute-start.6 = (bf16[21,512]{1,0:T(8,128)(2,1)S(1)}, bf16[21,512]{1,0:T(8,128)(2,1)S(1)}, u32[]{:S(2)}, u32[]{:S(2)}) collective-permute-start(bf16[21,512]{1,0:T(8,128)(2,1)S(1)} %get-tuple-element.36), channel_id=1, source_target_pairs={{0,3},{1,2},{2,1},{3,0},{4,7},{5,6},{6,5},{7,4},{8,11},{9,10},{10,... | collective-permute-start | bytes 64520 | tf_op jit(solution)/shard_map/ppermute | solution.py:762
  15.5 1.0 %collective-permute-start.7 = (bf16[21,512]{1,0:T(8,128)(2,1)S(1)}, bf16[21,512]{1,0:T(8,128)(2,1)S(1)}, u32[]{:S(2)}, u32[]{:S(2)}) collective-permute-start(bf16[21,512]{1,0:T(8,128)(2,1)S(1)} %get-tuple-element.37), channel_id=1, source_target_pairs={{0,1},{1,0},{2,3},{3,2},{4,5},{5,4},{6,7},{7,6},{8,9},{9,8},{10,11... | collective-permute-start | bytes 64520 | tf_op jit(solution)/shard_map/ppermute | solution.py:762
  16.5 1.5 %coarse_correct.1 = f32[6,6,21,384]{3,2,1,0:T(8,128)} custom-call(s32[1,2]{1,0:T(1,128)S(1)} %bitcast.14, f32[36,24,384]{2,1,0:T(8,128)S(1)} %get-tuple-element.22.adv, bf16[128,384]{1,0:T(8,128)(2,1)S(1)} %collective-permute-done.1.x_low.x_first, bf16[128,384]{1,0:T(8,128)(2,1)S(1)} %collective-permute-done.2.x_high.x_second, ...), custom_call_target="tpu_custom_call" | custom-call | flops 6635520 | bytes 3981312 | tf_op jit(solution)/shard_map/coarse_correct/pallas_call | solution.py:639
  18.0 0.4 %collective-permute-done.5.refs_1_ = bf16[21,512]{1,0:T(8,128)(2,1)S(1)} collective-permute-done((bf16[21,512]{1,0:T(8,128)(2,1)S(1)}, bf16[21,512]{1,0:T(8,128)(2,1)S(1)}, u32[]{:S(2)}, u32[]{:S(2)}) %collective-permute-start.5) | collective-permute-done | bytes 21536 | tf_op jit(solution)/shard_map/ppermute | solution.py:762
  18.3 0.7 %unpack.1 = bf16[21,4,512]{2,1,0:T(4,128)(2,1)} custom-call(bf16[21,512]{1,0:T(8,128)(2,1)S(1)} %get-tuple-element.34.refs_0_, bf16[21,512]{1,0:T(8,128)(2,1)S(1)} %collective-permute-done.5.refs_1_, bf16[21,512]{1,0:T(8,128)(2,1)S(1)} %collective-permute-done.6.refs_2_, bf16[21,512]{1,0:T(8,128)(2,1)S(1)} %collective-permute-done.7.refs_3_), custom_call_target="tpu_custom_call" | custom-call | tf_op jit(solution)/shard_map/unpack/pallas_call | solution.py:692
  (19 shorter events, 0.1 us)
Async XLA Ops:
  0.6 4.5 %copy-start = (f32[21,6,6,384]{3,0,2,1:T(8,128)S(1)}, f32[21,6,6,384]{3,0,2,1:T(8,128)}, u32[]{:S(2)}) copy-start(f32[21,6,6,384]{3,0,2,1:T(8,128)} %param.10) | copy-start | bytes 3483652
  2.0 8.1 %collective-permute-start = (bf16[192,384]{1,0:T(8,128)(2,1)S(1)}, bf16[192,384]{1,0:T(8,128)(2,1)S(1)}, u32[]{:S(2)}, u32[]{:S(2)}) collective-permute-start(bf16[192,384]{1,0:T(8,128)(2,1)S(1)} %get-tuple-element.20), channel_id=1, source_target_pairs={{0,1},{2,3},{1,0},{3,2},{4,5},{6,7},{5,4},{7,6},{8,9},{10,11},{9,8... | collective-permute-start | bytes 442376 | tf_op jit(solution)/shard_map/ppermute | solution.py:740
  2.5 9.9 %collective-permute-start.3 = (bf16[176,384]{1,0:T(8,128)(2,1)S(1)}, bf16[176,384]{1,0:T(8,128)(2,1)S(1)}, u32[]{:S(2)}, u32[]{:S(2)}) collective-permute-start(bf16[176,384]{1,0:T(8,128)(2,1)S(1)} %get-tuple-element.23), channel_id=1, source_target_pairs={{0,3},{2,1},{3,0},{1,2},{4,7},{6,5},{7,4},{5,6},{8,11},{10,9},{11,... | collective-permute-start | bytes 405512 | tf_op jit(solution)/shard_map/ppermute | solution.py:741
  5.1 5.0 %copy-start.2 = (f32[256,512]{1,0:T(8,128)S(1)}, f32[256,512]{1,0:T(8,128)}, u32[]{:S(2)}) copy-start(f32[256,512]{1,0:T(8,128)} %constant.8.clone.spread) | copy-start | bytes 1572868
  5.1 5.1 %copy-start.3 = (f32[128,512]{1,0:T(8,128)S(1)}, f32[128,512]{1,0:T(8,128)}, u32[]{:S(2)}) copy-start(f32[128,512]{1,0:T(8,128)} %constant.9.clone.ghost) | copy-start | bytes 786436
  5.1 5.1 %copy-start.5 = (f32[21,21]{1,0:T(8,128)S(1)}, f32[21,21]{1,0:T(8,128)}, u32[]{:S(2)}) copy-start(f32[21,21]{1,0:T(8,128)} %rate.1) | copy-start | bytes 5296
  5.1 5.1 %copy-start.6 = (s32[1,1,2]{2,1,0:T(1,128)S(1)}, s32[1,1,2]{2,1,0:T(1,128)}, u32[]{:S(2)}) copy-start(s32[1,1,2]{2,1,0:T(1,128)} %param.14) | copy-start | bytes 28
  5.1 5.1 %copy-start.7 = (f32[21]{0:T(128)S(1)}, f32[21]{0:T(128)}, u32[]{:S(2)}) copy-start(f32[21]{0:T(128)} %param.12) | copy-start | bytes 256
  5.2 8.4 %collective-permute-start.1 = (bf16[128,384]{1,0:T(8,128)(2,1)S(1)}, bf16[128,384]{1,0:T(8,128)(2,1)S(1)}, u32[]{:S(2)}, u32[]{:S(2)}) collective-permute-start(bf16[128,384]{1,0:T(8,128)(2,1)S(1)} %pack_x.2.after), channel_id=1, source_target_pairs={{0,4},{4,8},{8,12},{12,16},{16,20},{20,24},{24,28},{28,0},{1,5},{5... | collective-permute-start | bytes 294920 | tf_op jit(solution)/shard_map/ppermute | solution.py:738
  6.8 5.7 %copy-start.8 = (s32[1,1,2]{2,1,0:T(1,128)S(1)}, s32[1,1,2]{2,1,0:T(1,128)}, u32[]{:S(2)}) copy-start(s32[1,1,2]{2,1,0:T(1,128)} %param.15) | copy-start | bytes 28
  6.8 6.8 %collective-permute-start.2 = (bf16[128,384]{1,0:T(8,128)(2,1)S(1)}, bf16[128,384]{1,0:T(8,128)(2,1)S(1)}, u32[]{:S(2)}, u32[]{:S(2)}) collective-permute-start(bf16[128,384]{1,0:T(8,128)(2,1)S(1)} %pack_x.3.after), channel_id=1, source_target_pairs={{0,28},{4,0},{8,4},{12,8},{16,12},{20,16},{24,20},{28,24},{1,29},{... | collective-permute-start | bytes 294920 | tf_op jit(solution)/shard_map/ppermute | solution.py:739
  10.1 3.5 %collective-permute-start.4 = (bf16[21,512]{1,0:T(8,128)(2,1)S(1)}, bf16[21,512]{1,0:T(8,128)(2,1)S(1)}, u32[]{:S(2)}, u32[]{:S(2)}) collective-permute-start(bf16[21,512]{1,0:T(8,128)(2,1)S(1)} %relay.1.after), channel_id=1, source_target_pairs={{0,3},{2,1},{3,0},{1,2},{4,7},{6,5},{7,4},{5,6},{8,11},{10,9},{11,... | collective-permute-start | bytes 64520 | tf_op jit(solution)/shard_map/ppermute | solution.py:745
  12.4 4.0 %copy-start.1 = (f32[512,256]{1,0:T(8,128)S(1)}, f32[512,256]{1,0:T(8,128)}, u32[]{:S(2)}) copy-start(f32[512,256]{1,0:T(8,128)} %constant.10.clone.average) | copy-start | bytes 1572868
  12.4 4.0 %copy-start.4 = (f32[128,256]{1,0:T(8,128)S(1)}, f32[128,256]{1,0:T(8,128)}, u32[]{:S(2)}) copy-start(f32[128,256]{1,0:T(8,128)} %constant.11.clone.place) | copy-start | bytes 393220
  14.2 4.1 %collective-permute-start.5 = (bf16[21,512]{1,0:T(8,128)(2,1)S(1)}, bf16[21,512]{1,0:T(8,128)(2,1)S(1)}, u32[]{:S(2)}, u32[]{:S(2)}) collective-permute-start(bf16[21,512]{1,0:T(8,128)(2,1)S(1)} %get-tuple-element.35), channel_id=1, source_target_pairs={{0,2},{1,3},{2,0},{3,1},{4,6},{5,7},{6,4},{7,5},{8,10},{9,11},{10,... | collective-permute-start | bytes 64520 | tf_op jit(solution)/shard_map/ppermute | solution.py:762
  14.8 3.5 %collective-permute-start.6 = (bf16[21,512]{1,0:T(8,128)(2,1)S(1)}, bf16[21,512]{1,0:T(8,128)(2,1)S(1)}, u32[]{:S(2)}, u32[]{:S(2)}) collective-permute-start(bf16[21,512]{1,0:T(8,128)(2,1)S(1)} %get-tuple-element.36), channel_id=1, source_target_pairs={{0,3},{1,2},{2,1},{3,0},{4,7},{5,6},{6,5},{7,4},{8,11},{9,10},{10,... | collective-permute-start | bytes 64520 | tf_op jit(solution)/shard_map/ppermute | solution.py:762
  15.5 2.9 %collective-permute-start.7 = (bf16[21,512]{1,0:T(8,128)(2,1)S(1)}, bf16[21,512]{1,0:T(8,128)(2,1)S(1)}, u32[]{:S(2)}, u32[]{:S(2)}) collective-permute-start(bf16[21,512]{1,0:T(8,128)(2,1)S(1)} %get-tuple-element.37), channel_id=1, source_target_pairs={{0,1},{1,0},{2,3},{3,2},{4,5},{5,4},{6,7},{7,6},{8,9},{9,8},{10,11... | collective-permute-start | bytes 64520 | tf_op jit(solution)/shard_map/ppermute | solution.py:762

commit v5 on v4

--- a/solution.py
+++ b/solution.py
@@ -457,15 +457,12 @@
     )(pos, owner, near, far, own, after)
 
 
-def fine_kernel(pos, owner, x_low, x_high, start, *refs, count, edge):
+def fine_base_kernel(pos, owner, x_low, start, *refs, count, edge):
     others, refs = refs[: count - 3], refs[count - 3 :]
-    old, new, mix, coef, spread, ghost, from_y = refs[:7]
-    packets = refs[7 : 7 + count]
-    fix, kept, final, field, wide = refs[7 + count :]
-    species = packets[0].shape[0]
+    old, new, mix, coef, spread, from_y, base, fix, gathered, field, wide = refs
+    species = coef.shape[1]
     stack = from_y.shape[0]
-    boxes = final.shape[0] // stack
-    cells = final.shape[1]
+    boxes, cells = base.shape[0] // stack, base.shape[1]
     me = lax.axis_index("yz")
     mixed = mix[...]
 
@@ -475,8 +472,8 @@
 
     nz = x_low.shape[1]
     half = edge // 2
-    wide[0, : x_low.shape[0]] = x_low[...].astype(F32)
-    wide[1, : x_high.shape[0]] = x_high[...].astype(F32)
+    wide[...] = x_low[...].astype(F32)
+    gathered[...] = gather_faces(pos, [wide], [0], half, stack, species, nz, from_y[...])
     sent = [ref[...].astype(F32) for ref in others]
     for i in range(boxes):
         at = i * stack
@@ -507,19 +504,7 @@
 
     first = field[...]
     second = first + 2.0 * diff * (inside(first) + ghost0) + 0.5 * reaction(first)
-    base = second + diff * (2.0 * inside(second) + ghost1) + 0.5 * reaction(second)
-    layers = (wide.at[0], wide.at[1])
-    total = gather_faces(pos, layers, (0, 1), half, stack, species, nz, from_y[...])
-    kept[...] = total
-    stacked = by_box(total, boxes, half).astype(BF16)
-    value = base + diff * diff * dot(stacked, ghost[...])
-    final[...] = value
-    for k, out in enumerate(packets):
-        dest = partner(me, k, count)
-        packet = jnp.zeros((species, cells), F32)
-        for i in range(boxes):
-            packet = jnp.where(owner[0, i] == dest, value[i * stack : i * stack + species], packet)
-        out[...] = packet.astype(BF16)
+    base[...] = second + diff * (2.0 * inside(second) + ghost1) + 0.5 * reaction(second)
     pooled = lax.dot_general(
         parts(first + second), spread_v, (((1,), (1,)), ((), ())), preferred_element_type=F32
     )
@@ -541,29 +526,56 @@
     fix[...] = diff * result
 
 
-def fine_part(pos, owner, low, high, start, others, old, new, mix, coef, spread, ghost, from_y, edge):
-    boxes = owner.shape[1]
+def fine_base(pos, owner, low, start, others, old, new, mix, coef, spread, from_y, edge):
     count = len(others) + 3
-    stack = from_y.shape[0]
-    cells = start.shape[1]
-    vmem = pl.BlockSpec(memory_space=pltpu.VMEM)
-    return pl.pallas_call(
-        functools.partial(fine_kernel, count=count, edge=edge),
-        in_specs=[vmem] * (count + 9),
-        out_specs=[vmem] * (count + 3),
-        out_shape=[jax.ShapeDtypeStruct((coef.shape[1], cells), BF16)] * count
-        + [
-            jax.ShapeDtypeStruct((boxes * stack, old.shape[1]), F32),
-            jax.ShapeDtypeStruct(from_y.shape, F32),
-            jax.ShapeDtypeStruct((boxes * stack, cells), F32),
-        ],
-        scratch_shapes=[
-            pltpu.VMEM((boxes * stack, cells), F32),
-            pltpu.VMEM((2, *low.shape), F32),
-        ],
-        compiler_params=pltpu.CompilerParams(vmem_limit_bytes=LIMIT),
-        name="fine_part",
-    )(pos, owner, low, high, start, *others, old, new, mix, coef, spread, ghost, from_y)
+    vmem = pl.BlockSpec(memory_space=pltpu.VMEM)
+    return pl.pallas_call(
+        functools.partial(fine_base_kernel, count=count, edge=edge),
+        in_specs=[vmem] * (count + 7),
+        out_specs=[vmem] * 3,
+        out_shape=[jax.ShapeDtypeStruct(a.shape, F32) for a in (start, old, from_y)],
+        scratch_shapes=[pltpu.VMEM(start.shape, F32), pltpu.VMEM(low.shape, F32)],
+        compiler_params=pltpu.CompilerParams(vmem_limit_bytes=LIMIT),
+        name="fine_base",
+    )(pos, owner, low, start, *others, old, new, mix, coef, spread, from_y)
+
+
+def fine_finish_kernel(pos, owner, x_high, base, coef, ghost, gathered, *refs, half):
+    packets, (kept, final, wide) = refs[:-3], refs[-3:]
+    species, cells = packets[0].shape
+    count = len(packets)
+    stack = kept.shape[0]
+    boxes = base.shape[0] // stack
+    me = lax.axis_index("yz")
+    wide[...] = x_high[...].astype(F32)
+    total = gathered[...]
+    total = gather_faces(pos, [wide], [1], half, stack, species, wide.shape[1], total)
+    kept[...] = total
+    diff = jnp.concatenate([column(coef, stack)] * boxes, axis=0)
+    stacked = by_box(total, boxes, half).astype(BF16)
+    value = base[...] + diff * diff * dot(stacked, ghost[...])
+    final[...] = value
+    for k, out in enumerate(packets):
+        dest = partner(me, k, count)
+        packet = jnp.zeros((species, cells), F32)
+        for i in range(boxes):
+            packet = jnp.where(owner[0, i] == dest, value[i * stack : i * stack + species], packet)
+        out[...] = packet.astype(BF16)
+
+
+def fine_finish(pos, owner, high, base, coef, ghost, gathered, count, half):
+    vmem = pl.BlockSpec(memory_space=pltpu.VMEM)
+    packet = jax.ShapeDtypeStruct((coef.shape[1], base.shape[1]), BF16)
+    return pl.pallas_call(
+        functools.partial(fine_finish_kernel, half=half),
+        in_specs=[vmem] * 7,
+        out_specs=[vmem] * (count + 2),
+        out_shape=[packet] * count
+        + [jax.ShapeDtypeStruct(a.shape, F32) for a in (gathered, base)],
+        scratch_shapes=[pltpu.VMEM(high.shape, F32)],
+        compiler_params=pltpu.CompilerParams(vmem_limit_bytes=LIMIT),
+        name="fine_finish",
+    )(pos, owner, high, base, coef, ghost, gathered)
 
 
 def delta_of(field, kept, fix, coef, average, place, half, stack):
@@ -751,10 +763,11 @@
         pos, c, rate, coef, table, stack, after
     )
     from_y, start = y_faces(pos, owner, *halos[2:], own, old, half, stack)
-    made = fine_part(
-        pos, owner, *halos[:2], start, others, old, new, mix, coef, spread, ghost, from_y, 2 * half
+    base, fix, gathered = fine_base(
+        pos, owner, halos[0], start, others, old, new, mix, coef, spread, from_y, 2 * half
     )
-    packets, (fix, kept, field) = made[:count], made[count:]
+    made = fine_finish(pos, owner, halos[1], base, coef, ghost, gathered, count, half)
+    packets, (kept, field) = made[:count], made[count:]
 
     def swap(value, k):
         even = count & (count - 1) == 0

time: 19.2 us -> 19.3 us (level)
  Pallas kernels: 6.68 us -> 6.98 us
    ppermute x1, waiting for transfers between devices: 0.9 us -> 0.01 us  [local(): lax.ppermute(x_low, 'gx', ring('gx', -1))]
    ppermute x1, waiting for transfers between devices: 0.01 us -> 0.55 us  [local(): others = [lax.ppermute(passed, 'yz', mutual('yz', -1))]]
    pallas_call x1 -> x2, Pallas kernels: 0.68 us -> 0.99 us  [the longest x1 0.66 us: fine_base(): pl.pallas_call(functools.partial(fine_base_kernel, count=count, edge=edge...]
    ppermute x1, waiting for transfers between devices: 0.01 us -> 0.26 us  [local(): lax.ppermute(x_high, 'gx', ring('gx', 1))]
  transfers between devices with their start and end apart: 8 -> 8, of which waited for: 2 -> 3; matrix products, arithmetic and copies ran while one was open for 0% -> 0% of each run, Pallas kernels for 21% -> 24%
where the time goes in v5:
time: 19.3 us; the launch traced here: 19.2 us
  starting transfers between devices  10.3 us (53%)
  Pallas kernels  6.98 us (36%)
  waiting for transfers between devices  1.1 us (6%)
  between operations  0.81 us (4%)
    ppermute x1, starting transfers between devices, local(): lax.ppermute(x_low, 'gx', ring('gx', -1))  3.28 us
    ppermute x1, starting transfers between devices, local(): lax.ppermute(far, 'yz', mutual('yz', -1))  2.64 us
    ppermute x3, starting transfers between devices, swap(): return lax.ppermute(value, 'yz', pairs)  2.21 us
    pallas_call x1, Pallas kernels, coarse_part(): pl.pallas_call(coarse_kernel, in_specs=[vmem] * 6 + [pl.BlockSpec(memory_...  2.17 us
    ppermute x1, starting transfers between devices, local(): lax.ppermute(x_high, 'gx', ring('gx', 1))  1.54 us
    pallas_call x1, Pallas kernels, correct(): pl.pallas_call(functools.partial(correct_kernel, half=half), in_specs=[vm...  1.51 us
    pallas_call x1, Pallas kernels, pack_y(): pl.pallas_call(pack_y_kernel, in_specs=[pl.BlockSpec(memory_space=pltpu.H...  1.31 us
    pallas_call x1, Pallas kernels, unpack(): pl.pallas_call(unpack_kernel, in_specs=[vmem] * count, out_specs=vmem, ou...  0.71 us
  transfers between devices with their start and end apart: 8, of which 3 were waited for; matrix products, arithmetic and copies ran while one was open for 0% of the time, Pallas kernels for 24%

profile of v5, /device:TPU:0, one launch (start us, length us, event | category | flops | bytes accessed | tf_op | source)
XLA Modules:
  0.0 19.2 jit_solution(14217640883988995003)
XLA Ops:
  0.6 1.3 %pack_y.1 = (bf16[192,384]{1,0:T(8,128)(2,1)S(1)}, bf16[176,384]{1,0:T(8,128)(2,1)S(1)}, bf16[21,512]{1,0:T(8,128)(2,1)S(1)}) custom-call(f32[6,6,21,384]{3,2,1,0:T(8,128)} %bitcast.7, bf16[21,4,512]{2,1,0:T(4,128)(2,1)} %bitcast.25), custom_call_target="tpu_custom_call" | custom-call | tf_op jit(solution)/shard_map/pack_y/pallas_call | solution.py:238
  2.0 0.5 %collective-permute-start = (bf16[192,384]{1,0:T(8,128)(2,1)S(1)}, bf16[192,384]{1,0:T(8,128)(2,1)S(1)}, u32[]{:S(2)}, u32[]{:S(2)}) collective-permute-start(bf16[192,384]{1,0:T(8,128)(2,1)S(1)} %get-tuple-element.22), channel_id=1, source_target_pairs={{0,1},{2,3},{1,0},{3,2},{4,5},{6,7},{5,4},{7,6},{8,9},{10,11},{9,8... | collective-permute-start | bytes 442376 | tf_op jit(solution)/shard_map/ppermute | solution.py:752
  2.5 2.6 %collective-permute-start.3 = (bf16[176,384]{1,0:T(8,128)(2,1)S(1)}, bf16[176,384]{1,0:T(8,128)(2,1)S(1)}, u32[]{:S(2)}, u32[]{:S(2)}) collective-permute-start(bf16[176,384]{1,0:T(8,128)(2,1)S(1)} %get-tuple-element.25), channel_id=1, source_target_pairs={{0,3},{2,1},{3,0},{1,2},{4,7},{6,5},{7,4},{5,6},{8,11},{10,9},{11,... | collective-permute-start | bytes 405512 | tf_op jit(solution)/shard_map/ppermute | solution.py:753
  5.1 0.0 copy-start.6
  5.1 0.0 copy-start.7
  5.2 1.5 %collective-permute-start.1 = (bf16[128,384]{1,0:T(8,128)(2,1)S(1)}, bf16[128,384]{1,0:T(8,128)(2,1)S(1)}, u32[]{:S(2)}, u32[]{:S(2)}) collective-permute-start(bf16[128,384]{1,0:T(8,128)(2,1)S(1)} %pack_x.2.after), channel_id=1, source_target_pairs={{0,4},{4,8},{8,12},{12,16},{16,20},{20,24},{24,28},{28,0},{1,5},{5... | collective-permute-start | bytes 294920 | tf_op jit(solution)/shard_map/ppermute | solution.py:750
  6.8 0.0 copy-start.8
  6.8 3.3 %collective-permute-start.2 = (bf16[128,384]{1,0:T(8,128)(2,1)S(1)}, bf16[128,384]{1,0:T(8,128)(2,1)S(1)}, u32[]{:S(2)}, u32[]{:S(2)}) collective-permute-start(bf16[128,384]{1,0:T(8,128)(2,1)S(1)} %pack_x.3.after), channel_id=1, source_target_pairs={{0,28},{4,0},{8,4},{12,8},{16,12},{20,16},{24,20},{28,24},{1,29},{... | collective-permute-start | bytes 294920 | tf_op jit(solution)/shard_map/ppermute | solution.py:751
  10.1 0.0 collective-permute-done.near
  10.1 0.1 collective-permute-start.4
  10.2 2.2 %coarse_part.1 = (f32[36,24,384]{2,1,0:T(8,128)S(1)}, f32[48,256]{1,0:T(8,128)S(1)}, f32[48,256]{1,0:T(8,128)S(1)}, bf16[96,96]{1,0:T(8,128)(2,1)S(1)}, bf16[256...) custom-call(s32[1,2]{1,0:T(1,128)S(1)} %bitcast.11, f32[6,6,21,384]{3,2,1,0:T(8,128)S(1)} %bitcast.10, ...), custom_call_target="tpu_custom_call" | custom-call | flops 232243200 | bytes 3483648 | tf_op jit(solution)/shard_map/coarse_part/pallas_call | solution.py:360
  12.4 0.0 copy-start.4
  12.4 0.2 %y_faces.1 = (f32[24,128]{1,0:T(8,128)S(1)}, f32[48,512]{1,0:T(8,128)S(1)}) custom-call(s32[1,2]{1,0:T(1,128)S(1)} %bitcast.12, s32[1,2]{1,0:T(1,128)S(1)} %bitcast.20, bf16[192,384]{1,0:T(8,128)(2,1)S(1)} %collective-permute-done.near, bf16[176,384]{1,0:T(8,128)(2,1)S(1)} %collective-permute-done.3.far, bf16[21,512]{1,0:T(8,128)(2,1)S(1)} %get-tuple-element.23.after.own, ...), custom_call_target="tpu_custom_call" | custom-call | flops 1000000000 | bytes 20000000 | tf_op jit(solution)/shard_map/y_faces/pallas_call | solution.py:445
  12.6 0.0 copy-start.1
  12.6 0.3 %collective-permute-done.1.x_low.x_first = bf16[128,384]{1,0:T(8,128)(2,1)S(1)} collective-permute-done((bf16[128,384]{1,0:T(8,128)(2,1)S(1)}, bf16[128,384]{1,0:T(8,128)(2,1)S(1)}, u32[]{:S(2)}, u32[]{:S(2)}) %collective-permute-start.1) | collective-permute-done | bytes 98336 | tf_op jit(solution)/shard_map/ppermute | solution.py:750
  12.9 0.5 %collective-permute-done.4.refs_0_ = bf16[21,512]{1,0:T(8,128)(2,1)S(1)} collective-permute-done((bf16[21,512]{1,0:T(8,128)(2,1)S(1)}, bf16[21,512]{1,0:T(8,128)(2,1)S(1)}, u32[]{:S(2)}, u32[]{:S(2)}) %collective-permute-start.4) | collective-permute-done | bytes 21536 | tf_op jit(solution)/shard_map/ppermute | solution.py:757
  13.5 0.7 %fine_base.1 = (f32[48,512]{1,0:T(8,128)S(1)}, f32[48,256]{1,0:T(8,128)S(1)}, f32[24,128]{1,0:T(8,128)S(1)}) custom-call(s32[1,2]{1,0:T(1,128)S(1)} %bitcast.13, s32[1,2]{1,0:T(1,128)S(1)} %bitcast.21, bf16[128,384]{1,0:T(8,128)(2,1)S(1)} %collective-permute-done.1.x_low.x_first, f32[48,512]{1,0:T(8,128)S(1)} %get-tuple-element.27.start, ...), custom_call_target="tpu_custom_call" | custom-call | tf_op jit(solution)/shard_map/fine_base/pallas_call | solution.py:532
  14.1 0.3 %fine_finish.1 = (bf16[21,512]{1,0:T(8,128)(2,1)S(1)}, bf16[21,512]{1,0:T(8,128)(2,1)S(1)}, bf16[21,512]{1,0:T(8,128)(2,1)S(1)}, bf16[21,512]{1,0:T(8,128)(2,1)S...) custom-call(s32[1,2]{1,0:T(1,128)S(1)} %bitcast.14, s32[1,2]{1,0:T(1,128)S(1)} %bitcast.22, ...), custom_call_target="tpu_custom_call" | custom-call | tf_op jit(solution)/shard_map/fine_finish/pallas_call | solution.py:569
  14.5 0.5 %collective-permute-start.5 = (bf16[21,512]{1,0:T(8,128)(2,1)S(1)}, bf16[21,512]{1,0:T(8,128)(2,1)S(1)}, u32[]{:S(2)}, u32[]{:S(2)}) collective-permute-start(bf16[21,512]{1,0:T(8,128)(2,1)S(1)} %get-tuple-element.39), channel_id=1, source_target_pairs={{0,2},{1,3},{2,0},{3,1},{4,6},{5,7},{6,4},{7,5},{8,10},{9,11},{10,... | collective-permute-start | bytes 64520 | tf_op jit(solution)/shard_map/ppermute | solution.py:775
  15.0 0.8 %collective-permute-start.6 = (bf16[21,512]{1,0:T(8,128)(2,1)S(1)}, bf16[21,512]{1,0:T(8,128)(2,1)S(1)}, u32[]{:S(2)}, u32[]{:S(2)}) collective-permute-start(bf16[21,512]{1,0:T(8,128)(2,1)S(1)} %get-tuple-element.40), channel_id=1, source_target_pairs={{0,3},{1,2},{2,1},{3,0},{4,7},{5,6},{6,5},{7,4},{8,11},{9,10},{10,... | collective-permute-start | bytes 64520 | tf_op jit(solution)/shard_map/ppermute | solution.py:775
  15.8 0.9 %collective-permute-start.7 = (bf16[21,512]{1,0:T(8,128)(2,1)S(1)}, bf16[21,512]{1,0:T(8,128)(2,1)S(1)}, u32[]{:S(2)}, u32[]{:S(2)}) collective-permute-start(bf16[21,512]{1,0:T(8,128)(2,1)S(1)} %get-tuple-element.41), channel_id=1, source_target_pairs={{0,1},{1,0},{2,3},{3,2},{4,5},{5,4},{6,7},{7,6},{8,9},{9,8},{10,11... | collective-permute-start | bytes 64520 | tf_op jit(solution)/shard_map/ppermute | solution.py:775
  16.7 1.5 %coarse_correct.1 = f32[6,6,21,384]{3,2,1,0:T(8,128)} custom-call(s32[1,2]{1,0:T(1,128)S(1)} %bitcast.15, f32[36,24,384]{2,1,0:T(8,128)S(1)} %get-tuple-element.24.adv, bf16[128,384]{1,0:T(8,128)(2,1)S(1)} %collective-permute-done.1.x_low.x_first, bf16[128,384]{1,0:T(8,128)(2,1)S(1)} %collective-permute-done.2.x_high.x_second, ...), custom_call_target="tpu_custom_call" | custom-call | flops 6635520 | bytes 3981312 | tf_op jit(solution)/shard_map/coarse_correct/pallas_call | solution.py:651
  18.2 0.3 %collective-permute-done.5.refs_1_ = bf16[21,512]{1,0:T(8,128)(2,1)S(1)} collective-permute-done((bf16[21,512]{1,0:T(8,128)(2,1)S(1)}, bf16[21,512]{1,0:T(8,128)(2,1)S(1)}, u32[]{:S(2)}, u32[]{:S(2)}) %collective-permute-start.5) | collective-permute-done | bytes 21536 | tf_op jit(solution)/shard_map/ppermute | solution.py:775
  18.5 0.7 %unpack.1 = bf16[21,4,512]{2,1,0:T(4,128)(2,1)} custom-call(bf16[21,512]{1,0:T(8,128)(2,1)S(1)} %get-tuple-element.38.refs_0_, bf16[21,512]{1,0:T(8,128)(2,1)S(1)} %collective-permute-done.5.refs_1_, bf16[21,512]{1,0:T(8,128)(2,1)S(1)} %collective-permute-done.6.refs_2_, bf16[21,512]{1,0:T(8,128)(2,1)S(1)} %collective-permute-done.7.refs_3_), custom_call_target="tpu_custom_call" | custom-call | tf_op jit(solution)/shard_map/unpack/pallas_call | solution.py:704
  (20 shorter events, 0.1 us)
Async XLA Ops:
  0.6 4.5 %copy-start = (f32[21,6,6,384]{3,0,2,1:T(8,128)S(1)}, f32[21,6,6,384]{3,0,2,1:T(8,128)}, u32[]{:S(2)}) copy-start(f32[21,6,6,384]{3,0,2,1:T(8,128)} %param.10) | copy-start | bytes 3483652
  2.0 8.1 %collective-permute-start = (bf16[192,384]{1,0:T(8,128)(2,1)S(1)}, bf16[192,384]{1,0:T(8,128)(2,1)S(1)}, u32[]{:S(2)}, u32[]{:S(2)}) collective-permute-start(bf16[192,384]{1,0:T(8,128)(2,1)S(1)} %get-tuple-element.22), channel_id=1, source_target_pairs={{0,1},{2,3},{1,0},{3,2},{4,5},{6,7},{5,4},{7,6},{8,9},{10,11},{9,8... | collective-permute-start | bytes 442376 | tf_op jit(solution)/shard_map/ppermute | solution.py:752
  2.5 9.9 %collective-permute-start.3 = (bf16[176,384]{1,0:T(8,128)(2,1)S(1)}, bf16[176,384]{1,0:T(8,128)(2,1)S(1)}, u32[]{:S(2)}, u32[]{:S(2)}) collective-permute-start(bf16[176,384]{1,0:T(8,128)(2,1)S(1)} %get-tuple-element.25), channel_id=1, source_target_pairs={{0,3},{2,1},{3,0},{1,2},{4,7},{6,5},{7,4},{5,6},{8,11},{10,9},{11,... | collective-permute-start | bytes 405512 | tf_op jit(solution)/shard_map/ppermute | solution.py:753
  5.1 5.0 %copy-start.2 = (f32[256,512]{1,0:T(8,128)S(1)}, f32[256,512]{1,0:T(8,128)}, u32[]{:S(2)}) copy-start(f32[256,512]{1,0:T(8,128)} %constant.8.clone.spread) | copy-start | bytes 1572868
  5.1 5.1 %copy-start.3 = (f32[128,512]{1,0:T(8,128)S(1)}, f32[128,512]{1,0:T(8,128)}, u32[]{:S(2)}) copy-start(f32[128,512]{1,0:T(8,128)} %constant.9.clone.ghost) | copy-start | bytes 786436
  5.1 5.1 %copy-start.5 = (f32[21,21]{1,0:T(8,128)S(1)}, f32[21,21]{1,0:T(8,128)}, u32[]{:S(2)}) copy-start(f32[21,21]{1,0:T(8,128)} %rate.1) | copy-start | bytes 5296
  5.1 5.1 %copy-start.6 = (s32[1,1,2]{2,1,0:T(1,128)S(1)}, s32[1,1,2]{2,1,0:T(1,128)}, u32[]{:S(2)}) copy-start(s32[1,1,2]{2,1,0:T(1,128)} %param.14) | copy-start | bytes 28
  5.1 5.1 %copy-start.7 = (f32[21]{0:T(128)S(1)}, f32[21]{0:T(128)}, u32[]{:S(2)}) copy-start(f32[21]{0:T(128)} %param.12) | copy-start | bytes 256
  5.2 7.7 %collective-permute-start.1 = (bf16[128,384]{1,0:T(8,128)(2,1)S(1)}, bf16[128,384]{1,0:T(8,128)(2,1)S(1)}, u32[]{:S(2)}, u32[]{:S(2)}) collective-permute-start(bf16[128,384]{1,0:T(8,128)(2,1)S(1)} %pack_x.2.after), channel_id=1, source_target_pairs={{0,4},{4,8},{8,12},{12,16},{16,20},{20,24},{24,28},{28,0},{1,5},{5... | collective-permute-start | bytes 294920 | tf_op jit(solution)/shard_map/ppermute | solution.py:750
  6.8 5.6 %copy-start.8 = (s32[1,1,2]{2,1,0:T(1,128)S(1)}, s32[1,1,2]{2,1,0:T(1,128)}, u32[]{:S(2)}) copy-start(s32[1,1,2]{2,1,0:T(1,128)} %param.15) | copy-start | bytes 28
  6.8 7.3 %collective-permute-start.2 = (bf16[128,384]{1,0:T(8,128)(2,1)S(1)}, bf16[128,384]{1,0:T(8,128)(2,1)S(1)}, u32[]{:S(2)}, u32[]{:S(2)}) collective-permute-start(bf16[128,384]{1,0:T(8,128)(2,1)S(1)} %pack_x.3.after), channel_id=1, source_target_pairs={{0,28},{4,0},{8,4},{12,8},{16,12},{20,16},{24,20},{28,24},{1,29},{... | collective-permute-start | bytes 294920 | tf_op jit(solution)/shard_map/ppermute | solution.py:751
  10.1 3.4 %collective-permute-start.4 = (bf16[21,512]{1,0:T(8,128)(2,1)S(1)}, bf16[21,512]{1,0:T(8,128)(2,1)S(1)}, u32[]{:S(2)}, u32[]{:S(2)}) collective-permute-start(bf16[21,512]{1,0:T(8,128)(2,1)S(1)} %relay.1.after), channel_id=1, source_target_pairs={{0,3},{2,1},{3,0},{1,2},{4,7},{6,5},{7,4},{5,6},{8,11},{10,9},{11,... | collective-permute-start | bytes 64520 | tf_op jit(solution)/shard_map/ppermute | solution.py:757
  12.4 4.3 %copy-start.4 = (f32[128,256]{1,0:T(8,128)S(1)}, f32[128,256]{1,0:T(8,128)}, u32[]{:S(2)}) copy-start(f32[128,256]{1,0:T(8,128)} %constant.11.clone.place) | copy-start | bytes 393220
  12.6 4.1 %copy-start.1 = (f32[512,256]{1,0:T(8,128)S(1)}, f32[512,256]{1,0:T(8,128)}, u32[]{:S(2)}) copy-start(f32[512,256]{1,0:T(8,128)} %constant.10.clone.average) | copy-start | bytes 1572868
  14.5 4.0 %collective-permute-start.5 = (bf16[21,512]{1,0:T(8,128)(2,1)S(1)}, bf16[21,512]{1,0:T(8,128)(2,1)S(1)}, u32[]{:S(2)}, u32[]{:S(2)}) collective-permute-start(bf16[21,512]{1,0:T(8,128)(2,1)S(1)} %get-tuple-element.39), channel_id=1, source_target_pairs={{0,2},{1,3},{2,0},{3,1},{4,6},{5,7},{6,4},{7,5},{8,10},{9,11},{10,... | collective-permute-start | bytes 64520 | tf_op jit(solution)/shard_map/ppermute | solution.py:775
  15.0 3.5 %collective-permute-start.6 = (bf16[21,512]{1,0:T(8,128)(2,1)S(1)}, bf16[21,512]{1,0:T(8,128)(2,1)S(1)}, u32[]{:S(2)}, u32[]{:S(2)}) collective-permute-start(bf16[21,512]{1,0:T(8,128)(2,1)S(1)} %get-tuple-element.40), channel_id=1, source_target_pairs={{0,3},{1,2},{2,1},{3,0},{4,7},{5,6},{6,5},{7,4},{8,11},{9,10},{10,... | collective-permute-start | bytes 64520 | tf_op jit(solution)/shard_map/ppermute | solution.py:775
  15.8 2.7 %collective-permute-start.7 = (bf16[21,512]{1,0:T(8,128)(2,1)S(1)}, bf16[21,512]{1,0:T(8,128)(2,1)S(1)}, u32[]{:S(2)}, u32[]{:S(2)}) collective-permute-start(bf16[21,512]{1,0:T(8,128)(2,1)S(1)} %get-tuple-element.41), channel_id=1, source_target_pairs={{0,1},{1,0},{2,3},{3,2},{4,5},{5,4},{6,7},{7,6},{8,9},{9,8},{10,11... | collective-permute-start | bytes 64520 | tf_op jit(solution)/shard_map/ppermute | solution.py:775

commit v6 on v4

--- a/solution.py
+++ b/solution.py
@@ -194,10 +194,12 @@
     me = lax.axis_index("yz")
     slots = pltpu.make_async_copy(fine, held, fine_sem)
     slots.start()
-    copies = []
-    for n, y in enumerate((jnp.where(me % 2 == 0, ny - 1, 0), jnp.where(me % 2 == 0, 0, ny - 1))):
-        copies.append(pltpu.make_async_copy(c.at[:, y], layer.at[n], sems.at[n]))
-        copies[-1].start()
+    ends = (jnp.where(me % 2 == 0, ny - 1, 0), jnp.where(me % 2 == 0, 0, ny - 1))
+    copies = {}
+    for n in (1, 0):
+        for r in range(nx):
+            copies[n, r] = pltpu.make_async_copy(c.at[r, ends[n]], layer.at[n, r], sems.at[n, r])
+            copies[n, r].start()
     slots.wait()
     step = rows.shape[1] // stack
     pieces = rows.shape[0]
@@ -214,7 +216,8 @@
         out[...] = jnp.concatenate(slot(lax.rem(me + 2 + k, count)), axis=1).astype(BF16)
     for n, out in enumerate((far, near)):
         n = 1 - n
-        copies[n].wait()
+        for r in range(nx):
+            copies[n, r].wait()
         pack_layer([layer[n, r] for r in range(nx)], tmp, species)
         sent = [slot(neighbour(me, count, n == 0))]
         if n == 0 and relays(count):
@@ -245,7 +248,7 @@
             pltpu.VMEM((rows, nz), F32),
             pltpu.VMEM(fine.shape, BF16),
             pltpu.VMEM((cells // 128, stack * padded(count, 8), 128), F32),
-            pltpu.SemaphoreType.DMA((2,)),
+            pltpu.SemaphoreType.DMA((2, nx)),
             pltpu.SemaphoreType.DMA,
         ],
         compiler_params=pltpu.CompilerParams(vmem_limit_bytes=LIMIT),

time: 19.2 us -> 19.4 us (1.010)
  no operation moved by 1% of the time
where the time goes in v6:
time: 19.4 us; the launch traced here: 19.2 us
  starting transfers between devices  10.3 us (53%)
  Pallas kernels  6.83 us (35%)
  waiting for transfers between devices  1.27 us (7%)
  between operations  0.79 us (4%)
    ppermute x1, starting transfers between devices, local(): lax.ppermute(x_low, 'gx', ring('gx', -1))  3.28 us
    ppermute x1, starting transfers between devices, local(): lax.ppermute(far, 'yz', mutual('yz', -1))  2.64 us
    ppermute x3, starting transfers between devices, swap(): return lax.ppermute(value, 'yz', pairs)  2.21 us
    pallas_call x1, Pallas kernels, coarse_part(): pl.pallas_call(coarse_kernel, in_specs=[vmem] * 6 + [pl.BlockSpec(memory_...  2.18 us
    ppermute x1, starting transfers between devices, local(): lax.ppermute(x_high, 'gx', ring('gx', 1))  1.54 us
    pallas_call x1, Pallas kernels, correct(): pl.pallas_call(functools.partial(correct_kernel, half=half), in_specs=[vm...  1.52 us
    pallas_call x1, Pallas kernels, pack_y(): pl.pallas_call(pack_y_kernel, in_specs=[pl.BlockSpec(memory_space=pltpu.H...  1.47 us
    ppermute x1, waiting for transfers between devices, local(): lax.ppermute(x_low, 'gx', ring('gx', -1))  0.9 us
  transfers between devices with their start and end apart: 8, of which 2 were waited for; matrix products, arithmetic and copies ran while one was open for 0% of the time, Pallas kernels for 21%

profile of v6, /device:TPU:0, one launch (start us, length us, event | category | flops | bytes accessed | tf_op | source)
XLA Modules:
  0.0 19.2 jit_solution(11557297264961485386)
XLA Ops:
  0.6 1.5 %pack_y.1 = (bf16[192,384]{1,0:T(8,128)(2,1)S(1)}, bf16[176,384]{1,0:T(8,128)(2,1)S(1)}, bf16[21,512]{1,0:T(8,128)(2,1)S(1)}) custom-call(f32[6,6,21,384]{3,2,1,0:T(8,128)} %bitcast.7, bf16[21,4,512]{2,1,0:T(4,128)(2,1)} %bitcast.22), custom_call_target="tpu_custom_call" | custom-call | tf_op jit(solution)/shard_map/pack_y/pallas_call | solution.py:241
  2.1 0.5 %collective-permute-start = (bf16[192,384]{1,0:T(8,128)(2,1)S(1)}, bf16[192,384]{1,0:T(8,128)(2,1)S(1)}, u32[]{:S(2)}, u32[]{:S(2)}) collective-permute-start(bf16[192,384]{1,0:T(8,128)(2,1)S(1)} %get-tuple-element.20), channel_id=1, source_target_pairs={{0,1},{2,3},{1,0},{3,2},{4,5},{6,7},{5,4},{7,6},{8,9},{10,11},{9,8... | collective-permute-start | bytes 442376 | tf_op jit(solution)/shard_map/ppermute | solution.py:743
  2.6 2.6 %collective-permute-start.3 = (bf16[176,384]{1,0:T(8,128)(2,1)S(1)}, bf16[176,384]{1,0:T(8,128)(2,1)S(1)}, u32[]{:S(2)}, u32[]{:S(2)}) collective-permute-start(bf16[176,384]{1,0:T(8,128)(2,1)S(1)} %get-tuple-element.23), channel_id=1, source_target_pairs={{0,3},{2,1},{3,0},{1,2},{4,7},{6,5},{7,4},{5,6},{8,11},{10,9},{11,... | collective-permute-start | bytes 405512 | tf_op jit(solution)/shard_map/ppermute | solution.py:744
  5.3 0.0 copy-start.6
  5.3 0.0 copy-start.7
  5.3 1.5 %collective-permute-start.1 = (bf16[128,384]{1,0:T(8,128)(2,1)S(1)}, bf16[128,384]{1,0:T(8,128)(2,1)S(1)}, u32[]{:S(2)}, u32[]{:S(2)}) collective-permute-start(bf16[128,384]{1,0:T(8,128)(2,1)S(1)} %pack_x.2.after), channel_id=1, source_target_pairs={{0,4},{4,8},{8,12},{12,16},{16,20},{20,24},{24,28},{28,0},{1,5},{5... | collective-permute-start | bytes 294920 | tf_op jit(solution)/shard_map/ppermute | solution.py:741
  6.9 0.0 copy-start.8
  6.9 3.3 %collective-permute-start.2 = (bf16[128,384]{1,0:T(8,128)(2,1)S(1)}, bf16[128,384]{1,0:T(8,128)(2,1)S(1)}, u32[]{:S(2)}, u32[]{:S(2)}) collective-permute-start(bf16[128,384]{1,0:T(8,128)(2,1)S(1)} %pack_x.3.after), channel_id=1, source_target_pairs={{0,28},{4,0},{8,4},{12,8},{16,12},{20,16},{24,20},{28,24},{1,29},{... | collective-permute-start | bytes 294920 | tf_op jit(solution)/shard_map/ppermute | solution.py:742
  10.2 0.0 collective-permute-done.near
  10.2 0.1 collective-permute-start.4
  10.4 2.2 %coarse_part.1 = (f32[36,24,384]{2,1,0:T(8,128)S(1)}, f32[48,256]{1,0:T(8,128)S(1)}, f32[48,256]{1,0:T(8,128)S(1)}, bf16[96,96]{1,0:T(8,128)(2,1)S(1)}, bf16[256...) custom-call(s32[1,2]{1,0:T(1,128)S(1)} %bitcast.11, f32[6,6,21,384]{3,2,1,0:T(8,128)S(1)} %bitcast.10, ...), custom_call_target="tpu_custom_call" | custom-call | flops 232243200 | bytes 3483648 | tf_op jit(solution)/shard_map/coarse_part/pallas_call | solution.py:363
  12.6 0.0 copy-start.1
  12.6 0.0 copy-start.4
  12.6 0.2 %y_faces.1 = (f32[24,128]{1,0:T(8,128)S(1)}, f32[48,512]{1,0:T(8,128)S(1)}) custom-call(s32[1,2]{1,0:T(1,128)S(1)} %bitcast.12, s32[1,2]{1,0:T(1,128)S(1)} %bitcast.18, bf16[192,384]{1,0:T(8,128)(2,1)S(1)} %collective-permute-done.near, bf16[176,384]{1,0:T(8,128)(2,1)S(1)} %collective-permute-done.3.far, bf16[21,512]{1,0:T(8,128)(2,1)S(1)} %get-tuple-element.21.after.own, ...), custom_call_target="tpu_custom_call" | custom-call | flops 1000000000 | bytes 20000000 | tf_op jit(solution)/shard_map/y_faces/pallas_call | solution.py:448
  12.8 0.9 %collective-permute-done.2.x_high.x_second = bf16[128,384]{1,0:T(8,128)(2,1)S(1)} collective-permute-done((bf16[128,384]{1,0:T(8,128)(2,1)S(1)}, bf16[128,384]{1,0:T(8,128)(2,1)S(1)}, u32[]{:S(2)}, u32[]{:S(2)}) %collective-permute-start.2) | collective-permute-done | bytes 98336 | tf_op jit(solution)/shard_map/ppermute | solution.py:742
  13.7 0.0 collective-permute-done.1.x_low.x_first
  13.7 0.0 collective-permute-done.4.refs_0_
  13.7 0.7 %fine_part.1 = (bf16[21,512]{1,0:T(8,128)(2,1)S(1)}, bf16[21,512]{1,0:T(8,128)(2,1)S(1)}, bf16[21,512]{1,0:T(8,128)(2,1)S(1)}, bf16[21,512]{1,0:T(8,128)(2,1)S(1...) custom-call(s32[1,2]{1,0:T(1,128)S(1)} %bitcast.13, s32[1,2]{1,0:T(1,128)S(1)} %bitcast.19, ...), custom_call_target="tpu_custom_call" | custom-call | tf_op jit(solution)/shard_map/fine_part/pallas_call | solution.py:553
  14.4 0.6 %collective-permute-start.5 = (bf16[21,512]{1,0:T(8,128)(2,1)S(1)}, bf16[21,512]{1,0:T(8,128)(2,1)S(1)}, u32[]{:S(2)}, u32[]{:S(2)}) collective-permute-start(bf16[21,512]{1,0:T(8,128)(2,1)S(1)} %get-tuple-element.35), channel_id=1, source_target_pairs={{0,2},{1,3},{2,0},{3,1},{4,6},{5,7},{6,4},{7,5},{8,10},{9,11},{10,... | collective-permute-start | bytes 64520 | tf_op jit(solution)/shard_map/ppermute | solution.py:765
  15.0 0.6 %collective-permute-start.6 = (bf16[21,512]{1,0:T(8,128)(2,1)S(1)}, bf16[21,512]{1,0:T(8,128)(2,1)S(1)}, u32[]{:S(2)}, u32[]{:S(2)}) collective-permute-start(bf16[21,512]{1,0:T(8,128)(2,1)S(1)} %get-tuple-element.36), channel_id=1, source_target_pairs={{0,3},{1,2},{2,1},{3,0},{4,7},{5,6},{6,5},{7,4},{8,11},{9,10},{10,... | collective-permute-start | bytes 64520 | tf_op jit(solution)/shard_map/ppermute | solution.py:765
  15.6 1.0 %collective-permute-start.7 = (bf16[21,512]{1,0:T(8,128)(2,1)S(1)}, bf16[21,512]{1,0:T(8,128)(2,1)S(1)}, u32[]{:S(2)}, u32[]{:S(2)}) collective-permute-start(bf16[21,512]{1,0:T(8,128)(2,1)S(1)} %get-tuple-element.37), channel_id=1, source_target_pairs={{0,1},{1,0},{2,3},{3,2},{4,5},{5,4},{6,7},{7,6},{8,9},{9,8},{10,11... | collective-permute-start | bytes 64520 | tf_op jit(solution)/shard_map/ppermute | solution.py:765
  16.6 1.5 %coarse_correct.1 = f32[6,6,21,384]{3,2,1,0:T(8,128)} custom-call(s32[1,2]{1,0:T(1,128)S(1)} %bitcast.14, f32[36,24,384]{2,1,0:T(8,128)S(1)} %get-tuple-element.22.adv, bf16[128,384]{1,0:T(8,128)(2,1)S(1)} %collective-permute-done.1.x_low.x_first, bf16[128,384]{1,0:T(8,128)(2,1)S(1)} %collective-permute-done.2.x_high.x_second, ...), custom_call_target="tpu_custom_call" | custom-call | flops 6635520 | bytes 3981312 | tf_op jit(solution)/shard_map/coarse_correct/pallas_call | solution.py:642
  18.1 0.4 %collective-permute-done.5.refs_1_ = bf16[21,512]{1,0:T(8,128)(2,1)S(1)} collective-permute-done((bf16[21,512]{1,0:T(8,128)(2,1)S(1)}, bf16[21,512]{1,0:T(8,128)(2,1)S(1)}, u32[]{:S(2)}, u32[]{:S(2)}) %collective-permute-start.5) | collective-permute-done | bytes 21536 | tf_op jit(solution)/shard_map/ppermute | solution.py:765
  18.5 0.7 %unpack.1 = bf16[21,4,512]{2,1,0:T(4,128)(2,1)} custom-call(bf16[21,512]{1,0:T(8,128)(2,1)S(1)} %get-tuple-element.34.refs_0_, bf16[21,512]{1,0:T(8,128)(2,1)S(1)} %collective-permute-done.5.refs_1_, bf16[21,512]{1,0:T(8,128)(2,1)S(1)} %collective-permute-done.6.refs_2_, bf16[21,512]{1,0:T(8,128)(2,1)S(1)} %collective-permute-done.7.refs_3_), custom_call_target="tpu_custom_call" | custom-call | tf_op jit(solution)/shard_map/unpack/pallas_call | solution.py:695
  (19 shorter events, 0.1 us)
Async XLA Ops:
  0.6 4.7 %copy-start = (f32[21,6,6,384]{3,0,2,1:T(8,128)S(1)}, f32[21,6,6,384]{3,0,2,1:T(8,128)}, u32[]{:S(2)}) copy-start(f32[21,6,6,384]{3,0,2,1:T(8,128)} %param.10) | copy-start | bytes 3483652
  2.1 8.1 %collective-permute-start = (bf16[192,384]{1,0:T(8,128)(2,1)S(1)}, bf16[192,384]{1,0:T(8,128)(2,1)S(1)}, u32[]{:S(2)}, u32[]{:S(2)}) collective-permute-start(bf16[192,384]{1,0:T(8,128)(2,1)S(1)} %get-tuple-element.20), channel_id=1, source_target_pairs={{0,1},{2,3},{1,0},{3,2},{4,5},{6,7},{5,4},{7,6},{8,9},{10,11},{9,8... | collective-permute-start | bytes 442376 | tf_op jit(solution)/shard_map/ppermute | solution.py:743
  2.6 9.9 %collective-permute-start.3 = (bf16[176,384]{1,0:T(8,128)(2,1)S(1)}, bf16[176,384]{1,0:T(8,128)(2,1)S(1)}, u32[]{:S(2)}, u32[]{:S(2)}) collective-permute-start(bf16[176,384]{1,0:T(8,128)(2,1)S(1)} %get-tuple-element.23), channel_id=1, source_target_pairs={{0,3},{2,1},{3,0},{1,2},{4,7},{6,5},{7,4},{5,6},{8,11},{10,9},{11,... | collective-permute-start | bytes 405512 | tf_op jit(solution)/shard_map/ppermute | solution.py:744
  5.3 5.0 %copy-start.2 = (f32[256,512]{1,0:T(8,128)S(1)}, f32[256,512]{1,0:T(8,128)}, u32[]{:S(2)}) copy-start(f32[256,512]{1,0:T(8,128)} %constant.8.clone.spread) | copy-start | bytes 1572868
  5.3 5.1 %copy-start.3 = (f32[128,512]{1,0:T(8,128)S(1)}, f32[128,512]{1,0:T(8,128)}, u32[]{:S(2)}) copy-start(f32[128,512]{1,0:T(8,128)} %constant.9.clone.ghost) | copy-start | bytes 786436
  5.3 5.1 %copy-start.5 = (f32[21,21]{1,0:T(8,128)S(1)}, f32[21,21]{1,0:T(8,128)}, u32[]{:S(2)}) copy-start(f32[21,21]{1,0:T(8,128)} %rate.1) | copy-start | bytes 5296
  5.3 5.1 %copy-start.6 = (s32[1,1,2]{2,1,0:T(1,128)S(1)}, s32[1,1,2]{2,1,0:T(1,128)}, u32[]{:S(2)}) copy-start(s32[1,1,2]{2,1,0:T(1,128)} %param.14) | copy-start | bytes 28
  5.3 5.1 %copy-start.7 = (f32[21]{0:T(128)S(1)}, f32[21]{0:T(128)}, u32[]{:S(2)}) copy-start(f32[21]{0:T(128)} %param.12) | copy-start | bytes 256
  5.3 8.4 %collective-permute-start.1 = (bf16[128,384]{1,0:T(8,128)(2,1)S(1)}, bf16[128,384]{1,0:T(8,128)(2,1)S(1)}, u32[]{:S(2)}, u32[]{:S(2)}) collective-permute-start(bf16[128,384]{1,0:T(8,128)(2,1)S(1)} %pack_x.2.after), channel_id=1, source_target_pairs={{0,4},{4,8},{8,12},{12,16},{16,20},{20,24},{24,28},{28,0},{1,5},{5... | collective-permute-start | bytes 294920 | tf_op jit(solution)/shard_map/ppermute | solution.py:741
  6.9 5.6 %copy-start.8 = (s32[1,1,2]{2,1,0:T(1,128)S(1)}, s32[1,1,2]{2,1,0:T(1,128)}, u32[]{:S(2)}) copy-start(s32[1,1,2]{2,1,0:T(1,128)} %param.15) | copy-start | bytes 28
  6.9 6.8 %collective-permute-start.2 = (bf16[128,384]{1,0:T(8,128)(2,1)S(1)}, bf16[128,384]{1,0:T(8,128)(2,1)S(1)}, u32[]{:S(2)}, u32[]{:S(2)}) collective-permute-start(bf16[128,384]{1,0:T(8,128)(2,1)S(1)} %pack_x.3.after), channel_id=1, source_target_pairs={{0,28},{4,0},{8,4},{12,8},{16,12},{20,16},{24,20},{28,24},{1,29},{... | collective-permute-start | bytes 294920 | tf_op jit(solution)/shard_map/ppermute | solution.py:742
  10.2 3.5 %collective-permute-start.4 = (bf16[21,512]{1,0:T(8,128)(2,1)S(1)}, bf16[21,512]{1,0:T(8,128)(2,1)S(1)}, u32[]{:S(2)}, u32[]{:S(2)}) collective-permute-start(bf16[21,512]{1,0:T(8,128)(2,1)S(1)} %relay.1.after), channel_id=1, source_target_pairs={{0,3},{2,1},{3,0},{1,2},{4,7},{6,5},{7,4},{5,6},{8,11},{10,9},{11,... | collective-permute-start | bytes 64520 | tf_op jit(solution)/shard_map/ppermute | solution.py:748
  12.6 4.0 %copy-start.1 = (f32[512,256]{1,0:T(8,128)S(1)}, f32[512,256]{1,0:T(8,128)}, u32[]{:S(2)}) copy-start(f32[512,256]{1,0:T(8,128)} %constant.10.clone.average) | copy-start | bytes 1572868
  12.6 4.0 %copy-start.4 = (f32[128,256]{1,0:T(8,128)S(1)}, f32[128,256]{1,0:T(8,128)}, u32[]{:S(2)}) copy-start(f32[128,256]{1,0:T(8,128)} %constant.11.clone.place) | copy-start | bytes 393220
  14.4 4.1 %collective-permute-start.5 = (bf16[21,512]{1,0:T(8,128)(2,1)S(1)}, bf16[21,512]{1,0:T(8,128)(2,1)S(1)}, u32[]{:S(2)}, u32[]{:S(2)}) collective-permute-start(bf16[21,512]{1,0:T(8,128)(2,1)S(1)} %get-tuple-element.35), channel_id=1, source_target_pairs={{0,2},{1,3},{2,0},{3,1},{4,6},{5,7},{6,4},{7,5},{8,10},{9,11},{10,... | collective-permute-start | bytes 64520 | tf_op jit(solution)/shard_map/ppermute | solution.py:765
  15.0 3.5 %collective-permute-start.6 = (bf16[21,512]{1,0:T(8,128)(2,1)S(1)}, bf16[21,512]{1,0:T(8,128)(2,1)S(1)}, u32[]{:S(2)}, u32[]{:S(2)}) collective-permute-start(bf16[21,512]{1,0:T(8,128)(2,1)S(1)} %get-tuple-element.36), channel_id=1, source_target_pairs={{0,3},{1,2},{2,1},{3,0},{4,7},{5,6},{6,5},{7,4},{8,11},{9,10},{10,... | collective-permute-start | bytes 64520 | tf_op jit(solution)/shard_map/ppermute | solution.py:765
  15.6 2.9 %collective-permute-start.7 = (bf16[21,512]{1,0:T(8,128)(2,1)S(1)}, bf16[21,512]{1,0:T(8,128)(2,1)S(1)}, u32[]{:S(2)}, u32[]{:S(2)}) collective-permute-start(bf16[21,512]{1,0:T(8,128)(2,1)S(1)} %get-tuple-element.37), channel_id=1, source_target_pairs={{0,1},{1,0},{2,3},{3,2},{4,5},{5,4},{6,7},{7,6},{8,9},{9,8},{10,11... | collective-permute-start | bytes 64520 | tf_op jit(solution)/shard_map/ppermute | solution.py:765

commit v7 on v4

--- a/solution.py
+++ b/solution.py
@@ -409,7 +409,7 @@
     return total
 
 
-def y_faces_kernel(pos, owner, near, far, own, after, from_y, start, wide):
+def y_faces_kernel(pos, owner, near, far, own, old, new, spread, from_y, start, ghosts, wide):
     stack = from_y.shape[0]
     species, cells = own.shape
     nz = near.shape[1]
@@ -423,6 +423,8 @@
     zero = jnp.zeros(from_y.shape, F32)
     layers = (wide.at[0], wide.at[1])
     from_y[...] = gather_faces(pos, layers, (3 - odd, 2 + odd), half, stack, species, nz, zero)
+    old_v = old[...]
+    ghosts[...] = rows_dot(jnp.concatenate([old_v, old_v + new[...]], axis=0), spread[...])
     direct = own[...].astype(F32)
     places = blocks_of(width, species, nz, cells // 128)
     edge = species // 8 * 8
@@ -438,30 +440,31 @@
             start[at : at + species, q * 128 : (q + 1) * 128] = part
 
 
-def y_faces(pos, owner, near, far, own, after, half, stack):
+def y_faces(pos, owner, near, far, own, old, new, spread, half, stack):
     vmem = pl.BlockSpec(memory_space=pltpu.VMEM)
     boxes = pos.shape[1]
     lanes = padded(boxes * 4 * half * half, 128)
     return pl.pallas_call(
         y_faces_kernel,
-        in_specs=[vmem] * 5 + [pl.BlockSpec(memory_space=pl.ANY)],
-        out_specs=[vmem] * 2,
+        in_specs=[vmem] * 8,
+        out_specs=[vmem] * 3,
         out_shape=[
             jax.ShapeDtypeStruct((stack, lanes), F32),
             jax.ShapeDtypeStruct((boxes * stack, own.shape[1]), F32),
+            jax.ShapeDtypeStruct((2 * boxes * stack, own.shape[1]), F32),
         ],
         scratch_shapes=[pltpu.VMEM((2, *near.shape), F32)],
         compiler_params=pltpu.CompilerParams(vmem_limit_bytes=LIMIT),
         cost_estimate=pl.CostEstimate(flops=10**9, bytes_accessed=ORDER, transcendentals=0),
         name="y_faces",
-    )(pos, owner, near, far, own, after)
+    )(pos, owner, near, far, own, old, new, spread)
 
 
 def fine_kernel(pos, owner, x_low, x_high, start, *refs, count, edge):
     others, refs = refs[: count - 3], refs[count - 3 :]
-    old, new, mix, coef, spread, ghost, from_y = refs[:7]
-    packets = refs[7 : 7 + count]
-    fix, kept, final, field, wide = refs[7 + count :]
+    mix, coef, ghosts, ghost, from_y = refs[:5]
+    packets = refs[5 : 5 + count]
+    mid, kept, final, field, wide = refs[5 + count :]
     species = packets[0].shape[0]
     stack = from_y.shape[0]
     boxes = final.shape[0] // stack
@@ -487,11 +490,7 @@
             value = jnp.where(back == k + 2, sent[k], value)
         field[at : at + species] = value
     diff = jnp.concatenate([column(coef, stack)] * boxes, axis=0)
-    old_v, new_v = old[...], new[...]
-    sums = old_v + new_v
-    spread_v = spread[...]
-    both = rows_dot(jnp.concatenate([old_v, sums], axis=0), spread_v)
-    ghost0, ghost1 = both[: boxes * stack], both[boxes * stack :]
+    ghost0, ghost1 = ghosts[: boxes * stack], ghosts[boxes * stack :]
     index = lax.broadcasted_iota(jnp.int32, (1, cells), 1)
     at = (index // (edge * edge), index // edge % edge, index % edge)
     step = (edge * edge, edge, 1)
@@ -520,28 +519,10 @@
         for i in range(boxes):
             packet = jnp.where(owner[0, i] == dest, value[i * stack : i * stack + species], packet)
         out[...] = packet.astype(BF16)
-    pooled = lax.dot_general(
-        parts(first + second), spread_v, (((1,), (1,)), ((), ())), preferred_element_type=F32
-    )
-    pooled = 0.25 * (pooled[: boxes * stack] + pooled[boxes * stack :])
-    width = edge // 2 + 2
-    lanes = old.shape[1]
-    lane = lax.broadcasted_iota(jnp.int32, (1, lanes), 1)
-    at = (lane // (width * width), lane // width % width, lane % width)
-    step = (width * width, width, 1)
-    inner = [(a >= 1) & (a <= width - 2) for a in at]
-    rest = pooled - 0.5 * sums
-    result = jnp.zeros_like(old_v)
-    for axis in range(3):
-        sides = inner[(axis + 1) % 3] & inner[(axis + 2) % 3]
-        for edge_at, shift in ((0, lanes - step[axis]), (width - 1, step[axis])):
-            mask = sides & (at[axis] == edge_at)
-            fixed = rest - pltpu.roll(old_v, shift, 1)
-            result = jnp.where(mask, fixed, result)
-    fix[...] = diff * result
-
-
-def fine_part(pos, owner, low, high, start, others, old, new, mix, coef, spread, ghost, from_y, edge):
+    mid[...] = first + second
+
+
+def fine_part(pos, owner, low, high, start, others, mix, coef, ghosts, ghost, from_y, edge):
     boxes = owner.shape[1]
     count = len(others) + 3
     stack = from_y.shape[0]
@@ -549,11 +530,11 @@
     vmem = pl.BlockSpec(memory_space=pltpu.VMEM)
     return pl.pallas_call(
         functools.partial(fine_kernel, count=count, edge=edge),
-        in_specs=[vmem] * (count + 9),
+        in_specs=[vmem] * (count + 7),
         out_specs=[vmem] * (count + 3),
         out_shape=[jax.ShapeDtypeStruct((coef.shape[1], cells), BF16)] * count
         + [
-            jax.ShapeDtypeStruct((boxes * stack, old.shape[1]), F32),
+            jax.ShapeDtypeStruct((boxes * stack, cells), F32),
             jax.ShapeDtypeStruct(from_y.shape, F32),
             jax.ShapeDtypeStruct((boxes * stack, cells), F32),
         ],
@@ -563,25 +544,65 @@
         ],
         compiler_params=pltpu.CompilerParams(vmem_limit_bytes=LIMIT),
         name="fine_part",
-    )(pos, owner, low, high, start, *others, old, new, mix, coef, spread, ghost, from_y)
-
-
-def delta_of(field, kept, fix, coef, average, place, half, stack):
+    )(pos, owner, low, high, start, *others, mix, coef, ghosts, ghost, from_y)
+
+
+def fix_of(mid, old, new, spread, diffs, width):
+    old_v = old[...]
+    size = old_v.shape[0]
+    pooled = lax.dot_general(
+        parts(mid[...]), spread[...], (((1,), (1,)), ((), ())), preferred_element_type=F32
+    )
+    rest = 0.25 * (pooled[:size] + pooled[size:]) - 0.5 * (old_v + new[...])
+    lanes = old_v.shape[1]
+    lane = lax.broadcasted_iota(jnp.int32, (1, lanes), 1)
+    at = (lane // (width * width), lane // width % width, lane % width)
+    step = (width * width, width, 1)
+    inner = [(a >= 1) & (a <= width - 2) for a in at]
+    result = jnp.zeros_like(old_v)
+    for axis in range(3):
+        sides = inner[(axis + 1) % 3] & inner[(axis + 2) % 3]
+        for edge_at, shift in ((0, lanes - step[axis]), (width - 1, step[axis])):
+            mask = sides & (at[axis] == edge_at)
+            result = jnp.where(mask, rest - pltpu.roll(old_v, shift, 1), result)
+    return diffs * result
+
+
+def delta_of(field, kept, mid, old, new, spread, coef, average, place, half, stack):
     boxes = field.shape[0] // stack
     diffs = jnp.concatenate([column(coef, stack)] * boxes, axis=0)
-    stacked = by_box(kept[...], boxes, half).astype(BF16)
-    halo = dot(stacked, place[...].astype(BF16))
+    halo = dot(by_box(kept[...], boxes, half).astype(BF16), place[...].astype(BF16))
     means = rows_dot(field[...], average[...].astype(BF16))
-    return fix[...] - 0.5 * diffs * diffs * halo + means
+    fix = fix_of(mid, old, new, spread, diffs, half + 2)
+    return fix - 0.5 * diffs * diffs * halo + means
 
 
 def correct_kernel(
-    pos, adv, x_first, x_second, near, far, coef, field, kept, fix, average, place, out, block, wide, sems, half
+    pos,
+    adv,
+    x_first,
+    x_second,
+    near,
+    far,
+    coef,
+    field,
+    kept,
+    mid,
+    old,
+    new,
+    spread,
+    average,
+    place,
+    out,
+    block,
+    wide,
+    sems,
+    half,
 ):
     count, stack, nz = adv.shape
     species = block.shape[2]
     width = half + 2
-    delta = delta_of(field, kept, fix, coef, average, place, half, stack)
+    delta = delta_of(field, kept, mid, old, new, spread, coef, average, place, half, stack)
     diff = column(coef, stack)
     even = lax.axis_index("yz") % 2 == 0
     rows = x_first.shape[0]
@@ -631,14 +652,14 @@
         copy.wait()
 
 
-def correct(pos, adv, halos, coef, field, kept, fix, table, half):
+def correct(pos, adv, halos, coef, field, kept, mid, old, new, spread, table, half):
     _, stack, nz = adv.shape
     width = half + 2
     species = coef.shape[1]
     vmem = pl.BlockSpec(memory_space=pltpu.VMEM)
     return pl.pallas_call(
         functools.partial(correct_kernel, half=half),
-        in_specs=[vmem] * 12,
+        in_specs=[vmem] * 15,
         out_specs=pl.BlockSpec(memory_space=pltpu.HBM),
         out_shape=jax.ShapeDtypeStruct((width, width, species, nz), F32),
         scratch_shapes=[
@@ -658,7 +679,10 @@
         coef,
         field,
         kept,
-        fix,
+        mid,
+        old,
+        new,
+        spread,
         jnp.asarray(table["average"]),
         jnp.asarray(table["place"]),
     )
@@ -750,11 +774,11 @@
     adv, old, new, mix, spread, ghost = coarse_part(
         pos, c, rate, coef, table, stack, after
     )
-    from_y, start = y_faces(pos, owner, *halos[2:], own, old, half, stack)
+    from_y, start, ghosts = y_faces(pos, owner, *halos[2:], own, old, new, spread, half, stack)
     made = fine_part(
-        pos, owner, *halos[:2], start, others, old, new, mix, coef, spread, ghost, from_y, 2 * half
+        pos, owner, *halos[:2], start, others, mix, coef, ghosts, ghost, from_y, 2 * half
     )
-    packets, (fix, kept, field) = made[:count], made[count:]
+    packets, (mid, kept, field) = made[:count], made[count:]
 
     def swap(value, k):
         even = count & (count - 1) == 0
@@ -762,7 +786,7 @@
         return lax.ppermute(value, "yz", pairs)
 
     back = [packets[0]] + [swap(packets[k], k) for k in range(1, count)]
-    coarse_next = correct(pos, adv, halos, coef, field, kept, fix, table, half)
+    coarse_next = correct(pos, adv, halos, coef, field, kept, mid, old, new, spread, table, half)
 
     fine_next = jnp.transpose(unpack(back), (1, 0, 2))
     return jnp.transpose(coarse_next, (2, 0, 1, 3)), fine_next

time: 19.2 us -> 19.1 us (level)
  transfers between devices with their start and end apart: 8 -> 8, of which waited for: 2 -> 2; matrix products, arithmetic and copies ran while one was open for 0% -> 0% of each run, Pallas kernels for 21% -> 22%
where the time goes in v7:
time: 19.1 us; the launch traced here: 19 us
  starting transfers between devices  10.3 us (54%)
  Pallas kernels  6.79 us (36%)
  waiting for transfers between devices  1.1 us (6%)
  between operations  0.8 us (4%)
    ppermute x1, starting transfers between devices, local(): lax.ppermute(x_low, 'gx', ring('gx', -1))  3.28 us
    ppermute x1, starting transfers between devices, local(): lax.ppermute(far, 'yz', mutual('yz', -1))  2.64 us
    ppermute x3, starting transfers between devices, swap(): return lax.ppermute(value, 'yz', pairs)  2.21 us
    pallas_call x1, Pallas kernels, coarse_part(): pl.pallas_call(coarse_kernel, in_specs=[vmem] * 6 + [pl.BlockSpec(memory_...  2.17 us
    pallas_call x1, Pallas kernels, correct(): pl.pallas_call(functools.partial(correct_kernel, half=half), in_specs=[vm...  1.66 us
    ppermute x1, starting transfers between devices, local(): lax.ppermute(x_high, 'gx', ring('gx', 1))  1.54 us
    pallas_call x1, Pallas kernels, pack_y(): pl.pallas_call(pack_y_kernel, in_specs=[pl.BlockSpec(memory_space=pltpu.H...  1.31 us
    ppermute x1, waiting for transfers between devices, local(): lax.ppermute(x_low, 'gx', ring('gx', -1))  0.87 us
  transfers between devices with their start and end apart: 8, of which 2 were waited for; matrix products, arithmetic and copies ran while one was open for 0% of the time, Pallas kernels for 22%

profile of v7, /device:TPU:0, one launch (start us, length us, event | category | flops | bytes accessed | tf_op | source)
XLA Modules:
  0.0 19.0 jit_solution(11438113229682756280)
XLA Ops:
  0.6 1.3 %pack_y.1 = (bf16[192,384]{1,0:T(8,128)(2,1)S(1)}, bf16[176,384]{1,0:T(8,128)(2,1)S(1)}, bf16[21,512]{1,0:T(8,128)(2,1)S(1)}) custom-call(f32[6,6,21,384]{3,2,1,0:T(8,128)} %bitcast.7, bf16[21,4,512]{2,1,0:T(4,128)(2,1)} %bitcast.22), custom_call_target="tpu_custom_call" | custom-call | tf_op jit(solution)/shard_map/pack_y/pallas_call | solution.py:238
  2.0 0.5 %collective-permute-start = (bf16[192,384]{1,0:T(8,128)(2,1)S(1)}, bf16[192,384]{1,0:T(8,128)(2,1)S(1)}, u32[]{:S(2)}, u32[]{:S(2)}) collective-permute-start(bf16[192,384]{1,0:T(8,128)(2,1)S(1)} %get-tuple-element.21), channel_id=1, source_target_pairs={{0,1},{2,3},{1,0},{3,2},{4,5},{6,7},{5,4},{7,6},{8,9},{10,11},{9,8... | collective-permute-start | bytes 442376 | tf_op jit(solution)/shard_map/ppermute | solution.py:764
  2.5 2.6 %collective-permute-start.3 = (bf16[176,384]{1,0:T(8,128)(2,1)S(1)}, bf16[176,384]{1,0:T(8,128)(2,1)S(1)}, u32[]{:S(2)}, u32[]{:S(2)}) collective-permute-start(bf16[176,384]{1,0:T(8,128)(2,1)S(1)} %get-tuple-element.24), channel_id=1, source_target_pairs={{0,3},{2,1},{3,0},{1,2},{4,7},{6,5},{7,4},{5,6},{8,11},{10,9},{11,... | collective-permute-start | bytes 405512 | tf_op jit(solution)/shard_map/ppermute | solution.py:765
  5.1 0.0 copy-start.6
  5.1 0.0 copy-start.7
  5.2 1.5 %collective-permute-start.1 = (bf16[128,384]{1,0:T(8,128)(2,1)S(1)}, bf16[128,384]{1,0:T(8,128)(2,1)S(1)}, u32[]{:S(2)}, u32[]{:S(2)}) collective-permute-start(bf16[128,384]{1,0:T(8,128)(2,1)S(1)} %pack_x.2.after), channel_id=1, source_target_pairs={{0,4},{4,8},{8,12},{12,16},{16,20},{20,24},{24,28},{28,0},{1,5},{5... | collective-permute-start | bytes 294920 | tf_op jit(solution)/shard_map/ppermute | solution.py:762
  6.8 0.0 copy-start.8
  6.8 3.3 %collective-permute-start.2 = (bf16[128,384]{1,0:T(8,128)(2,1)S(1)}, bf16[128,384]{1,0:T(8,128)(2,1)S(1)}, u32[]{:S(2)}, u32[]{:S(2)}) collective-permute-start(bf16[128,384]{1,0:T(8,128)(2,1)S(1)} %pack_x.3.after), channel_id=1, source_target_pairs={{0,28},{4,0},{8,4},{12,8},{16,12},{20,16},{24,20},{28,24},{1,29},{... | collective-permute-start | bytes 294920 | tf_op jit(solution)/shard_map/ppermute | solution.py:763
  10.1 0.0 collective-permute-done.near
  10.1 0.1 collective-permute-start.4
  10.2 2.2 %coarse_part.1 = (f32[36,24,384]{2,1,0:T(8,128)S(1)}, f32[48,256]{1,0:T(8,128)S(1)}, f32[48,256]{1,0:T(8,128)S(1)}, bf16[96,96]{1,0:T(8,128)(2,1)S(1)}, bf16[256...) custom-call(s32[1,2]{1,0:T(1,128)S(1)} %bitcast.11, f32[6,6,21,384]{3,2,1,0:T(8,128)S(1)} %bitcast.10, ...), custom_call_target="tpu_custom_call" | custom-call | flops 232243200 | bytes 3483648 | tf_op jit(solution)/shard_map/coarse_part/pallas_call | solution.py:360
  12.4 0.0 collective-permute-done.3.far
  12.4 0.0 copy-start.1
  12.4 0.0 copy-start.4
  12.4 0.2 %y_faces.1 = (f32[24,128]{1,0:T(8,128)S(1)}, f32[48,512]{1,0:T(8,128)S(1)}, f32[96,512]{1,0:T(8,128)S(1)}) custom-call(s32[1,2]{1,0:T(1,128)S(1)} %bitcast.12, s32[1,2]{1,0:T(1,128)S(1)} %bitcast.18, bf16[192,384]{1,0:T(8,128)(2,1)S(1)} %collective-permute-done.near, bf16[176,384]{1,0:T(8,128)(2,1)S(1)} %collective-permute-done.3.far, ...), custom_call_target="tpu_custom_call" | custom-call | flops 1000000000 | bytes 20000000 | tf_op jit(solution)/shard_map/y_faces/pallas_call | solution.py:447
  12.7 0.9 %collective-permute-done.2.x_high.x_second = bf16[128,384]{1,0:T(8,128)(2,1)S(1)} collective-permute-done((bf16[128,384]{1,0:T(8,128)(2,1)S(1)}, bf16[128,384]{1,0:T(8,128)(2,1)S(1)}, u32[]{:S(2)}, u32[]{:S(2)}) %collective-permute-start.2) | collective-permute-done | bytes 98336 | tf_op jit(solution)/shard_map/ppermute | solution.py:763
  13.6 0.0 collective-permute-done.1.x_low.x_first
  13.6 0.6 %fine_part.1 = (bf16[21,512]{1,0:T(8,128)(2,1)S(1)}, bf16[21,512]{1,0:T(8,128)(2,1)S(1)}, bf16[21,512]{1,0:T(8,128)(2,1)S(1)}, bf16[21,512]{1,0:T(8,128)(2,1)S(1...) custom-call(s32[1,2]{1,0:T(1,128)S(1)} %bitcast.13, s32[1,2]{1,0:T(1,128)S(1)} %bitcast.19, ...), custom_call_target="tpu_custom_call" | custom-call | tf_op jit(solution)/shard_map/fine_part/pallas_call | solution.py:531
  14.2 0.6 %collective-permute-start.5 = (bf16[21,512]{1,0:T(8,128)(2,1)S(1)}, bf16[21,512]{1,0:T(8,128)(2,1)S(1)}, u32[]{:S(2)}, u32[]{:S(2)}) collective-permute-start(bf16[21,512]{1,0:T(8,128)(2,1)S(1)} %get-tuple-element.37), channel_id=1, source_target_pairs={{0,2},{1,3},{2,0},{3,1},{4,6},{5,7},{6,4},{7,5},{8,10},{9,11},{10,... | collective-permute-start | bytes 64520 | tf_op jit(solution)/shard_map/ppermute | solution.py:786
  14.8 0.6 %collective-permute-start.6 = (bf16[21,512]{1,0:T(8,128)(2,1)S(1)}, bf16[21,512]{1,0:T(8,128)(2,1)S(1)}, u32[]{:S(2)}, u32[]{:S(2)}) collective-permute-start(bf16[21,512]{1,0:T(8,128)(2,1)S(1)} %get-tuple-element.38), channel_id=1, source_target_pairs={{0,3},{1,2},{2,1},{3,0},{4,7},{5,6},{6,5},{7,4},{8,11},{9,10},{10,... | collective-permute-start | bytes 64520 | tf_op jit(solution)/shard_map/ppermute | solution.py:786
  15.4 1.0 %collective-permute-start.7 = (bf16[21,512]{1,0:T(8,128)(2,1)S(1)}, bf16[21,512]{1,0:T(8,128)(2,1)S(1)}, u32[]{:S(2)}, u32[]{:S(2)}) collective-permute-start(bf16[21,512]{1,0:T(8,128)(2,1)S(1)} %get-tuple-element.39), channel_id=1, source_target_pairs={{0,1},{1,0},{2,3},{3,2},{4,5},{5,4},{6,7},{7,6},{8,9},{9,8},{10,11... | collective-permute-start | bytes 64520 | tf_op jit(solution)/shard_map/ppermute | solution.py:786
  16.4 1.7 %coarse_correct.1 = f32[6,6,21,384]{3,2,1,0:T(8,128)} custom-call(s32[1,2]{1,0:T(1,128)S(1)} %bitcast.14, f32[36,24,384]{2,1,0:T(8,128)S(1)} %get-tuple-element.23.adv, bf16[128,384]{1,0:T(8,128)(2,1)S(1)} %collective-permute-done.1.x_low.x_first, bf16[128,384]{1,0:T(8,128)(2,1)S(1)} %collective-permute-done.2.x_high.x_second, ...), custom_call_target="tpu_custom_call" | custom-call | flops 6635520 | bytes 3981312 | tf_op jit(solution)/shard_map/coarse_correct/pallas_call | solution.py:660
  18.1 0.2 %collective-permute-done.5.refs_1_ = bf16[21,512]{1,0:T(8,128)(2,1)S(1)} collective-permute-done((bf16[21,512]{1,0:T(8,128)(2,1)S(1)}, bf16[21,512]{1,0:T(8,128)(2,1)S(1)}, u32[]{:S(2)}, u32[]{:S(2)}) %collective-permute-start.5) | collective-permute-done | bytes 21536 | tf_op jit(solution)/shard_map/ppermute | solution.py:786
  18.3 0.7 %unpack.1 = bf16[21,4,512]{2,1,0:T(4,128)(2,1)} custom-call(bf16[21,512]{1,0:T(8,128)(2,1)S(1)} %get-tuple-element.36.refs_0_, bf16[21,512]{1,0:T(8,128)(2,1)S(1)} %collective-permute-done.5.refs_1_, bf16[21,512]{1,0:T(8,128)(2,1)S(1)} %collective-permute-done.6.refs_2_, bf16[21,512]{1,0:T(8,128)(2,1)S(1)} %collective-permute-done.7.refs_3_), custom_call_target="tpu_custom_call" | custom-call | tf_op jit(solution)/shard_map/unpack/pallas_call | solution.py:716
  (19 shorter events, 0.1 us)
Async XLA Ops:
  0.6 4.5 %copy-start = (f32[21,6,6,384]{3,0,2,1:T(8,128)S(1)}, f32[21,6,6,384]{3,0,2,1:T(8,128)}, u32[]{:S(2)}) copy-start(f32[21,6,6,384]{3,0,2,1:T(8,128)} %param.10) | copy-start | bytes 3483652
  2.0 8.1 %collective-permute-start = (bf16[192,384]{1,0:T(8,128)(2,1)S(1)}, bf16[192,384]{1,0:T(8,128)(2,1)S(1)}, u32[]{:S(2)}, u32[]{:S(2)}) collective-permute-start(bf16[192,384]{1,0:T(8,128)(2,1)S(1)} %get-tuple-element.21), channel_id=1, source_target_pairs={{0,1},{2,3},{1,0},{3,2},{4,5},{6,7},{5,4},{7,6},{8,9},{10,11},{9,8... | collective-permute-start | bytes 442376 | tf_op jit(solution)/shard_map/ppermute | solution.py:764
  2.5 9.9 %collective-permute-start.3 = (bf16[176,384]{1,0:T(8,128)(2,1)S(1)}, bf16[176,384]{1,0:T(8,128)(2,1)S(1)}, u32[]{:S(2)}, u32[]{:S(2)}) collective-permute-start(bf16[176,384]{1,0:T(8,128)(2,1)S(1)} %get-tuple-element.24), channel_id=1, source_target_pairs={{0,3},{2,1},{3,0},{1,2},{4,7},{6,5},{7,4},{5,6},{8,11},{10,9},{11,... | collective-permute-start | bytes 405512 | tf_op jit(solution)/shard_map/ppermute | solution.py:765
  5.1 5.0 %copy-start.2 = (f32[256,512]{1,0:T(8,128)S(1)}, f32[256,512]{1,0:T(8,128)}, u32[]{:S(2)}) copy-start(f32[256,512]{1,0:T(8,128)} %constant.8.clone.spread) | copy-start | bytes 1572868
  5.1 5.1 %copy-start.3 = (f32[128,512]{1,0:T(8,128)S(1)}, f32[128,512]{1,0:T(8,128)}, u32[]{:S(2)}) copy-start(f32[128,512]{1,0:T(8,128)} %constant.9.clone.ghost) | copy-start | bytes 786436
  5.1 5.1 %copy-start.5 = (f32[21,21]{1,0:T(8,128)S(1)}, f32[21,21]{1,0:T(8,128)}, u32[]{:S(2)}) copy-start(f32[21,21]{1,0:T(8,128)} %rate.1) | copy-start | bytes 5296
  5.1 5.1 %copy-start.6 = (s32[1,1,2]{2,1,0:T(1,128)S(1)}, s32[1,1,2]{2,1,0:T(1,128)}, u32[]{:S(2)}) copy-start(s32[1,1,2]{2,1,0:T(1,128)} %param.14) | copy-start | bytes 28
  5.1 5.1 %copy-start.7 = (f32[21]{0:T(128)S(1)}, f32[21]{0:T(128)}, u32[]{:S(2)}) copy-start(f32[21]{0:T(128)} %param.12) | copy-start | bytes 256
  5.2 8.4 %collective-permute-start.1 = (bf16[128,384]{1,0:T(8,128)(2,1)S(1)}, bf16[128,384]{1,0:T(8,128)(2,1)S(1)}, u32[]{:S(2)}, u32[]{:S(2)}) collective-permute-start(bf16[128,384]{1,0:T(8,128)(2,1)S(1)} %pack_x.2.after), channel_id=1, source_target_pairs={{0,4},{4,8},{8,12},{12,16},{16,20},{20,24},{24,28},{28,0},{1,5},{5... | collective-permute-start | bytes 294920 | tf_op jit(solution)/shard_map/ppermute | solution.py:762
  6.8 5.6 %copy-start.8 = (s32[1,1,2]{2,1,0:T(1,128)S(1)}, s32[1,1,2]{2,1,0:T(1,128)}, u32[]{:S(2)}) copy-start(s32[1,1,2]{2,1,0:T(1,128)} %param.15) | copy-start | bytes 28
  6.8 6.8 %collective-permute-start.2 = (bf16[128,384]{1,0:T(8,128)(2,1)S(1)}, bf16[128,384]{1,0:T(8,128)(2,1)S(1)}, u32[]{:S(2)}, u32[]{:S(2)}) collective-permute-start(bf16[128,384]{1,0:T(8,128)(2,1)S(1)} %pack_x.3.after), channel_id=1, source_target_pairs={{0,28},{4,0},{8,4},{12,8},{16,12},{20,16},{24,20},{28,24},{1,29},{... | collective-permute-start | bytes 294920 | tf_op jit(solution)/shard_map/ppermute | solution.py:763
  10.1 3.5 %collective-permute-start.4 = (bf16[21,512]{1,0:T(8,128)(2,1)S(1)}, bf16[21,512]{1,0:T(8,128)(2,1)S(1)}, u32[]{:S(2)}, u32[]{:S(2)}) collective-permute-start(bf16[21,512]{1,0:T(8,128)(2,1)S(1)} %relay.1.after), channel_id=1, source_target_pairs={{0,3},{2,1},{3,0},{1,2},{4,7},{6,5},{7,4},{5,6},{8,11},{10,9},{11,... | collective-permute-start | bytes 64520 | tf_op jit(solution)/shard_map/ppermute | solution.py:769
  12.4 4.0 %copy-start.1 = (f32[512,256]{1,0:T(8,128)S(1)}, f32[512,256]{1,0:T(8,128)}, u32[]{:S(2)}) copy-start(f32[512,256]{1,0:T(8,128)} %constant.10.clone.average) | copy-start | bytes 1572868
  12.4 4.0 %copy-start.4 = (f32[128,256]{1,0:T(8,128)S(1)}, f32[128,256]{1,0:T(8,128)}, u32[]{:S(2)}) copy-start(f32[128,256]{1,0:T(8,128)} %constant.11.clone.place) | copy-start | bytes 393220
  14.2 4.1 %collective-permute-start.5 = (bf16[21,512]{1,0:T(8,128)(2,1)S(1)}, bf16[21,512]{1,0:T(8,128)(2,1)S(1)}, u32[]{:S(2)}, u32[]{:S(2)}) collective-permute-start(bf16[21,512]{1,0:T(8,128)(2,1)S(1)} %get-tuple-element.37), channel_id=1, source_target_pairs={{0,2},{1,3},{2,0},{3,1},{4,6},{5,7},{6,4},{7,5},{8,10},{9,11},{10,... | collective-permute-start | bytes 64520 | tf_op jit(solution)/shard_map/ppermute | solution.py:786
  14.8 3.5 %collective-permute-start.6 = (bf16[21,512]{1,0:T(8,128)(2,1)S(1)}, bf16[21,512]{1,0:T(8,128)(2,1)S(1)}, u32[]{:S(2)}, u32[]{:S(2)}) collective-permute-start(bf16[21,512]{1,0:T(8,128)(2,1)S(1)} %get-tuple-element.38), channel_id=1, source_target_pairs={{0,3},{1,2},{2,1},{3,0},{4,7},{5,6},{6,5},{7,4},{8,11},{9,10},{10,... | collective-permute-start | bytes 64520 | tf_op jit(solution)/shard_map/ppermute | solution.py:786
  15.4 2.9 %collective-permute-start.7 = (bf16[21,512]{1,0:T(8,128)(2,1)S(1)}, bf16[21,512]{1,0:T(8,128)(2,1)S(1)}, u32[]{:S(2)}, u32[]{:S(2)}) collective-permute-start(bf16[21,512]{1,0:T(8,128)(2,1)S(1)} %get-tuple-element.39), channel_id=1, source_target_pairs={{0,1},{1,0},{2,3},{3,2},{4,5},{5,4},{6,7},{7,6},{8,9},{9,8},{10,11... | collective-permute-start | bytes 64520 | tf_op jit(solution)/shard_map/ppermute | solution.py:786

commit v8 on v7

--- a/solution.py
+++ b/solution.py
@@ -409,7 +409,9 @@
     return total
 
 
-def y_faces_kernel(pos, owner, near, far, own, old, new, spread, from_y, start, ghosts, wide):
+def y_faces_kernel(
+    pos, owner, near, far, x_low, own, old, new, spread, from_y, start, ghosts, wide, x_wide
+):
     stack = from_y.shape[0]
     species, cells = own.shape
     nz = near.shape[1]
@@ -418,11 +420,13 @@
     half = width - 2
     wide[0] = near[...].astype(F32)
     wide[1, : far.shape[0]] = far[...].astype(F32)
+    x_wide[...] = x_low[...].astype(F32)
     me, count = lax.axis_index("yz"), lax.axis_size("yz")
     odd = me % 2
     zero = jnp.zeros(from_y.shape, F32)
-    layers = (wide.at[0], wide.at[1])
-    from_y[...] = gather_faces(pos, layers, (3 - odd, 2 + odd), half, stack, species, nz, zero)
+    layers = (wide.at[0], wide.at[1], x_wide)
+    faces = (3 - odd, 2 + odd, 0)
+    from_y[...] = gather_faces(pos, layers, faces, half, stack, species, nz, zero)
     old_v = old[...]
     ghosts[...] = rows_dot(jnp.concatenate([old_v, old_v + new[...]], axis=0), spread[...])
     direct = own[...].astype(F32)
@@ -440,27 +444,27 @@
             start[at : at + species, q * 128 : (q + 1) * 128] = part
 
 
-def y_faces(pos, owner, near, far, own, old, new, spread, half, stack):
+def y_faces(pos, owner, near, far, x_low, own, old, new, spread, half, stack):
     vmem = pl.BlockSpec(memory_space=pltpu.VMEM)
     boxes = pos.shape[1]
     lanes = padded(boxes * 4 * half * half, 128)
     return pl.pallas_call(
         y_faces_kernel,
-        in_specs=[vmem] * 8,
+        in_specs=[vmem] * 9,
         out_specs=[vmem] * 3,
         out_shape=[
             jax.ShapeDtypeStruct((stack, lanes), F32),
             jax.ShapeDtypeStruct((boxes * stack, own.shape[1]), F32),
             jax.ShapeDtypeStruct((2 * boxes * stack, own.shape[1]), F32),
         ],
-        scratch_shapes=[pltpu.VMEM((2, *near.shape), F32)],
+        scratch_shapes=[pltpu.VMEM((2, *near.shape), F32), pltpu.VMEM(x_low.shape, F32)],
         compiler_params=pltpu.CompilerParams(vmem_limit_bytes=LIMIT),
         cost_estimate=pl.CostEstimate(flops=10**9, bytes_accessed=ORDER, transcendentals=0),
         name="y_faces",
-    )(pos, owner, near, far, own, old, new, spread)
-
-
-def fine_kernel(pos, owner, x_low, x_high, start, *refs, count, edge):
+    )(pos, owner, near, far, x_low, own, old, new, spread)
+
+
+def fine_kernel(pos, owner, x_high, start, *refs, count, edge):
     others, refs = refs[: count - 3], refs[count - 3 :]
     mix, coef, ghosts, ghost, from_y = refs[:5]
     packets = refs[5 : 5 + count]
@@ -476,10 +480,9 @@
         pairs = [value[at : at + 2 * stack] for at in range(0, boxes * stack, 2 * stack)]
         return jnp.concatenate([react(mixed, pair) for pair in pairs], axis=0)
 
-    nz = x_low.shape[1]
+    nz = x_high.shape[1]
     half = edge // 2
-    wide[0, : x_low.shape[0]] = x_low[...].astype(F32)
-    wide[1, : x_high.shape[0]] = x_high[...].astype(F32)
+    wide[...] = x_high[...].astype(F32)
     sent = [ref[...].astype(F32) for ref in others]
     for i in range(boxes):
         at = i * stack
@@ -507,8 +510,7 @@
     first = field[...]
     second = first + 2.0 * diff * (inside(first) + ghost0) + 0.5 * reaction(first)
     base = second + diff * (2.0 * inside(second) + ghost1) + 0.5 * reaction(second)
-    layers = (wide.at[0], wide.at[1])
-    total = gather_faces(pos, layers, (0, 1), half, stack, species, nz, from_y[...])
+    total = gather_faces(pos, [wide], [1], half, stack, species, nz, from_y[...])
     kept[...] = total
     stacked = by_box(total, boxes, half).astype(BF16)
     value = base + diff * diff * dot(stacked, ghost[...])
@@ -522,7 +524,7 @@
     mid[...] = first + second
 
 
-def fine_part(pos, owner, low, high, start, others, mix, coef, ghosts, ghost, from_y, edge):
+def fine_part(pos, owner, high, start, others, mix, coef, ghosts, ghost, from_y, edge):
     boxes = owner.shape[1]
     count = len(others) + 3
     stack = from_y.shape[0]
@@ -530,7 +532,7 @@
     vmem = pl.BlockSpec(memory_space=pltpu.VMEM)
     return pl.pallas_call(
         functools.partial(fine_kernel, count=count, edge=edge),
-        in_specs=[vmem] * (count + 7),
+        in_specs=[vmem] * (count + 6),
         out_specs=[vmem] * (count + 3),
         out_shape=[jax.ShapeDtypeStruct((coef.shape[1], cells), BF16)] * count
         + [
@@ -540,11 +542,11 @@
         ],
         scratch_shapes=[
             pltpu.VMEM((boxes * stack, cells), F32),
-            pltpu.VMEM((2, *low.shape), F32),
+            pltpu.VMEM(high.shape, F32),
         ],
         compiler_params=pltpu.CompilerParams(vmem_limit_bytes=LIMIT),
         name="fine_part",
-    )(pos, owner, low, high, start, *others, mix, coef, ghosts, ghost, from_y)
+    )(pos, owner, high, start, *others, mix, coef, ghosts, ghost, from_y)
 
 
 def fix_of(mid, old, new, spread, diffs, width):
@@ -774,9 +776,11 @@
     adv, old, new, mix, spread, ghost = coarse_part(
         pos, c, rate, coef, table, stack, after
     )
-    from_y, start, ghosts = y_faces(pos, owner, *halos[2:], own, old, new, spread, half, stack)
+    from_y, start, ghosts = y_faces(
+        pos, owner, *halos[2:], halos[0], own, old, new, spread, half, stack
+    )
     made = fine_part(
-        pos, owner, *halos[:2], start, others, mix, coef, ghosts, ghost, from_y, 2 * half
+        pos, owner, halos[1], start, others, mix, coef, ghosts, ghost, from_y, 2 * half
     )
     packets, (mid, kept, field) = made[:count], made[count:]
 

time: 19.1 us -> 19.1 us (level)
    ppermute x1, waiting for transfers between devices: 0.87 us -> 0.37 us  [local(): lax.ppermute(x_low, 'gx', ring('gx', -1))]
    ppermute x1, waiting for transfers between devices: 0.01 us -> 0.51 us  [local(): lax.ppermute(x_high, 'gx', ring('gx', 1))]
  transfers between devices with their start and end apart: 8 -> 8, of which waited for: 2 -> 3; matrix products, arithmetic and copies ran while one was open for 0% -> 0% of each run, Pallas kernels for 22% -> 22%
where the time goes in v8:
time: 19.1 us; the launch traced here: 18.9 us
  starting transfers between devices  10.3 us (54%)
  Pallas kernels  6.76 us (35%)
  waiting for transfers between devices  1.09 us (6%)
  between operations  0.78 us (4%)
    ppermute x1, starting transfers between devices, local(): lax.ppermute(x_low, 'gx', ring('gx', -1))  3.28 us
    ppermute x1, starting transfers between devices, local(): lax.ppermute(far, 'yz', mutual('yz', -1))  2.64 us
    ppermute x3, starting transfers between devices, swap(): return lax.ppermute(value, 'yz', pairs)  2.21 us
    pallas_call x1, Pallas kernels, coarse_part(): pl.pallas_call(coarse_kernel, in_specs=[vmem] * 6 + [pl.BlockSpec(memory_...  2.18 us
    pallas_call x1, Pallas kernels, correct(): pl.pallas_call(functools.partial(correct_kernel, half=half), in_specs=[vm...  1.66 us
    ppermute x1, starting transfers between devices, local(): lax.ppermute(x_high, 'gx', ring('gx', 1))  1.54 us
    pallas_call x1, Pallas kernels, pack_y(): pl.pallas_call(pack_y_kernel, in_specs=[pl.BlockSpec(memory_space=pltpu.H...  1.31 us
    pallas_call x1, Pallas kernels, unpack(): pl.pallas_call(unpack_kernel, in_specs=[vmem] * count, out_specs=vmem, ou...  0.71 us
  transfers between devices with their start and end apart: 8, of which 3 were waited for; matrix products, arithmetic and copies ran while one was open for 0% of the time, Pallas kernels for 22%

profile of v8, /device:TPU:0, one launch (start us, length us, event | category | flops | bytes accessed | tf_op | source)
XLA Modules:
  0.0 18.9 jit_solution(107407578675802184)
XLA Ops:
  0.6 1.3 %pack_y.1 = (bf16[192,384]{1,0:T(8,128)(2,1)S(1)}, bf16[176,384]{1,0:T(8,128)(2,1)S(1)}, bf16[21,512]{1,0:T(8,128)(2,1)S(1)}) custom-call(f32[6,6,21,384]{3,2,1,0:T(8,128)} %bitcast.7, bf16[21,4,512]{2,1,0:T(4,128)(2,1)} %bitcast.22), custom_call_target="tpu_custom_call" | custom-call | tf_op jit(solution)/shard_map/pack_y/pallas_call | solution.py:238
  2.0 0.5 %collective-permute-start = (bf16[192,384]{1,0:T(8,128)(2,1)S(1)}, bf16[192,384]{1,0:T(8,128)(2,1)S(1)}, u32[]{:S(2)}, u32[]{:S(2)}) collective-permute-start(bf16[192,384]{1,0:T(8,128)(2,1)S(1)} %get-tuple-element.21), channel_id=1, source_target_pairs={{0,1},{2,3},{1,0},{3,2},{4,5},{6,7},{5,4},{7,6},{8,9},{10,11},{9,8... | collective-permute-start | bytes 442376 | tf_op jit(solution)/shard_map/ppermute | solution.py:766
  2.5 2.6 %collective-permute-start.3 = (bf16[176,384]{1,0:T(8,128)(2,1)S(1)}, bf16[176,384]{1,0:T(8,128)(2,1)S(1)}, u32[]{:S(2)}, u32[]{:S(2)}) collective-permute-start(bf16[176,384]{1,0:T(8,128)(2,1)S(1)} %get-tuple-element.24), channel_id=1, source_target_pairs={{0,3},{2,1},{3,0},{1,2},{4,7},{6,5},{7,4},{5,6},{8,11},{10,9},{11,... | collective-permute-start | bytes 405512 | tf_op jit(solution)/shard_map/ppermute | solution.py:767
  5.1 0.0 copy-start.6
  5.1 0.0 copy-start.7
  5.2 1.5 %collective-permute-start.1 = (bf16[128,384]{1,0:T(8,128)(2,1)S(1)}, bf16[128,384]{1,0:T(8,128)(2,1)S(1)}, u32[]{:S(2)}, u32[]{:S(2)}) collective-permute-start(bf16[128,384]{1,0:T(8,128)(2,1)S(1)} %pack_x.2.after), channel_id=1, source_target_pairs={{0,4},{4,8},{8,12},{12,16},{16,20},{20,24},{24,28},{28,0},{1,5},{5... | collective-permute-start | bytes 294920 | tf_op jit(solution)/shard_map/ppermute | solution.py:764
  6.8 0.0 copy-start.8
  6.8 3.3 %collective-permute-start.2 = (bf16[128,384]{1,0:T(8,128)(2,1)S(1)}, bf16[128,384]{1,0:T(8,128)(2,1)S(1)}, u32[]{:S(2)}, u32[]{:S(2)}) collective-permute-start(bf16[128,384]{1,0:T(8,128)(2,1)S(1)} %pack_x.3.after), channel_id=1, source_target_pairs={{0,28},{4,0},{8,4},{12,8},{16,12},{20,16},{24,20},{28,24},{1,29},{... | collective-permute-start | bytes 294920 | tf_op jit(solution)/shard_map/ppermute | solution.py:765
  10.1 0.0 collective-permute-done.near
  10.1 0.1 collective-permute-start.4
  10.2 2.2 %coarse_part.1 = (f32[36,24,384]{2,1,0:T(8,128)S(1)}, f32[48,256]{1,0:T(8,128)S(1)}, f32[48,256]{1,0:T(8,128)S(1)}, bf16[96,96]{1,0:T(8,128)(2,1)S(1)}, bf16[256...) custom-call(s32[1,2]{1,0:T(1,128)S(1)} %bitcast.11, f32[6,6,21,384]{3,2,1,0:T(8,128)S(1)} %bitcast.10, ...), custom_call_target="tpu_custom_call" | custom-call | flops 232243200 | bytes 3483648 | tf_op jit(solution)/shard_map/coarse_part/pallas_call | solution.py:360
  12.4 0.5 %collective-permute-done.1.x_low.x_first = bf16[128,384]{1,0:T(8,128)(2,1)S(1)} collective-permute-done((bf16[128,384]{1,0:T(8,128)(2,1)S(1)}, bf16[128,384]{1,0:T(8,128)(2,1)S(1)}, u32[]{:S(2)}, u32[]{:S(2)}) %collective-permute-start.1) | collective-permute-done | bytes 98336 | tf_op jit(solution)/shard_map/ppermute | solution.py:764
  12.9 0.0 collective-permute-done.3.far
  12.9 0.0 copy-start.4
  12.9 0.3 %y_faces.1 = (f32[24,128]{1,0:T(8,128)S(1)}, f32[48,512]{1,0:T(8,128)S(1)}, f32[96,512]{1,0:T(8,128)S(1)}) custom-call(s32[1,2]{1,0:T(1,128)S(1)} %bitcast.12, s32[1,2]{1,0:T(1,128)S(1)} %bitcast.18, bf16[192,384]{1,0:T(8,128)(2,1)S(1)} %collective-permute-done.near, bf16[176,384]{1,0:T(8,128)(2,1)S(1)} %collective-permute-done.3.far, ...), custom_call_target="tpu_custom_call" | custom-call | flops 1000000000 | bytes 20000000 | tf_op jit(solution)/shard_map/y_faces/pallas_call | solution.py:451
  13.2 0.4 %collective-permute-done.2.x_high.x_second = bf16[128,384]{1,0:T(8,128)(2,1)S(1)} collective-permute-done((bf16[128,384]{1,0:T(8,128)(2,1)S(1)}, bf16[128,384]{1,0:T(8,128)(2,1)S(1)}, u32[]{:S(2)}, u32[]{:S(2)}) %collective-permute-start.2) | collective-permute-done | bytes 98336 | tf_op jit(solution)/shard_map/ppermute | solution.py:765
  13.6 0.0 collective-permute-done.4.refs_0_
  13.6 0.6 %fine_part.1 = (bf16[21,512]{1,0:T(8,128)(2,1)S(1)}, bf16[21,512]{1,0:T(8,128)(2,1)S(1)}, bf16[21,512]{1,0:T(8,128)(2,1)S(1)}, bf16[21,512]{1,0:T(8,128)(2,1)S(1...) custom-call(s32[1,2]{1,0:T(1,128)S(1)} %bitcast.13, s32[1,2]{1,0:T(1,128)S(1)} %bitcast.19, ...), custom_call_target="tpu_custom_call" | custom-call | tf_op jit(solution)/shard_map/fine_part/pallas_call | solution.py:533
  14.1 0.6 %collective-permute-start.5 = (bf16[21,512]{1,0:T(8,128)(2,1)S(1)}, bf16[21,512]{1,0:T(8,128)(2,1)S(1)}, u32[]{:S(2)}, u32[]{:S(2)}) collective-permute-start(bf16[21,512]{1,0:T(8,128)(2,1)S(1)} %get-tuple-element.37), channel_id=1, source_target_pairs={{0,2},{1,3},{2,0},{3,1},{4,6},{5,7},{6,4},{7,5},{8,10},{9,11},{10,... | collective-permute-start | bytes 64520 | tf_op jit(solution)/shard_map/ppermute | solution.py:790
  14.7 0.6 %collective-permute-start.6 = (bf16[21,512]{1,0:T(8,128)(2,1)S(1)}, bf16[21,512]{1,0:T(8,128)(2,1)S(1)}, u32[]{:S(2)}, u32[]{:S(2)}) collective-permute-start(bf16[21,512]{1,0:T(8,128)(2,1)S(1)} %get-tuple-element.38), channel_id=1, source_target_pairs={{0,3},{1,2},{2,1},{3,0},{4,7},{5,6},{6,5},{7,4},{8,11},{9,10},{10,... | collective-permute-start | bytes 64520 | tf_op jit(solution)/shard_map/ppermute | solution.py:790
  15.4 1.0 %collective-permute-start.7 = (bf16[21,512]{1,0:T(8,128)(2,1)S(1)}, bf16[21,512]{1,0:T(8,128)(2,1)S(1)}, u32[]{:S(2)}, u32[]{:S(2)}) collective-permute-start(bf16[21,512]{1,0:T(8,128)(2,1)S(1)} %get-tuple-element.39), channel_id=1, source_target_pairs={{0,1},{1,0},{2,3},{3,2},{4,5},{5,4},{6,7},{7,6},{8,9},{9,8},{10,11... | collective-permute-start | bytes 64520 | tf_op jit(solution)/shard_map/ppermute | solution.py:790
  16.4 1.7 %coarse_correct.1 = f32[6,6,21,384]{3,2,1,0:T(8,128)} custom-call(s32[1,2]{1,0:T(1,128)S(1)} %bitcast.14, f32[36,24,384]{2,1,0:T(8,128)S(1)} %get-tuple-element.23.adv, bf16[128,384]{1,0:T(8,128)(2,1)S(1)} %collective-permute-done.1.x_low.x_first, bf16[128,384]{1,0:T(8,128)(2,1)S(1)} %collective-permute-done.2.x_high.x_second, ...), custom_call_target="tpu_custom_call" | custom-call | flops 6635520 | bytes 3981312 | tf_op jit(solution)/shard_map/coarse_correct/pallas_call | solution.py:662
  18.0 0.2 %collective-permute-done.5.refs_1_ = bf16[21,512]{1,0:T(8,128)(2,1)S(1)} collective-permute-done((bf16[21,512]{1,0:T(8,128)(2,1)S(1)}, bf16[21,512]{1,0:T(8,128)(2,1)S(1)}, u32[]{:S(2)}, u32[]{:S(2)}) %collective-permute-start.5) | collective-permute-done | bytes 21536 | tf_op jit(solution)/shard_map/ppermute | solution.py:790
  18.2 0.7 %unpack.1 = bf16[21,4,512]{2,1,0:T(4,128)(2,1)} custom-call(bf16[21,512]{1,0:T(8,128)(2,1)S(1)} %get-tuple-element.36.refs_0_, bf16[21,512]{1,0:T(8,128)(2,1)S(1)} %collective-permute-done.5.refs_1_, bf16[21,512]{1,0:T(8,128)(2,1)S(1)} %collective-permute-done.6.refs_2_, bf16[21,512]{1,0:T(8,128)(2,1)S(1)} %collective-permute-done.7.refs_3_), custom_call_target="tpu_custom_call" | custom-call | tf_op jit(solution)/shard_map/unpack/pallas_call | solution.py:718
  (19 shorter events, 0.1 us)
Async XLA Ops:
  0.6 4.5 %copy-start = (f32[21,6,6,384]{3,0,2,1:T(8,128)S(1)}, f32[21,6,6,384]{3,0,2,1:T(8,128)}, u32[]{:S(2)}) copy-start(f32[21,6,6,384]{3,0,2,1:T(8,128)} %param.10) | copy-start | bytes 3483652
  2.0 8.1 %collective-permute-start = (bf16[192,384]{1,0:T(8,128)(2,1)S(1)}, bf16[192,384]{1,0:T(8,128)(2,1)S(1)}, u32[]{:S(2)}, u32[]{:S(2)}) collective-permute-start(bf16[192,384]{1,0:T(8,128)(2,1)S(1)} %get-tuple-element.21), channel_id=1, source_target_pairs={{0,1},{2,3},{1,0},{3,2},{4,5},{6,7},{5,4},{7,6},{8,9},{10,11},{9,8... | collective-permute-start | bytes 442376 | tf_op jit(solution)/shard_map/ppermute | solution.py:766
  2.5 10.4 %collective-permute-start.3 = (bf16[176,384]{1,0:T(8,128)(2,1)S(1)}, bf16[176,384]{1,0:T(8,128)(2,1)S(1)}, u32[]{:S(2)}, u32[]{:S(2)}) collective-permute-start(bf16[176,384]{1,0:T(8,128)(2,1)S(1)} %get-tuple-element.24), channel_id=1, source_target_pairs={{0,3},{2,1},{3,0},{1,2},{4,7},{6,5},{7,4},{5,6},{8,11},{10,9},{11,... | collective-permute-start | bytes 405512 | tf_op jit(solution)/shard_map/ppermute | solution.py:767
  5.1 5.0 %copy-start.2 = (f32[256,512]{1,0:T(8,128)S(1)}, f32[256,512]{1,0:T(8,128)}, u32[]{:S(2)}) copy-start(f32[256,512]{1,0:T(8,128)} %constant.8.clone.spread) | copy-start | bytes 1572868
  5.1 5.1 %copy-start.3 = (f32[128,512]{1,0:T(8,128)S(1)}, f32[128,512]{1,0:T(8,128)}, u32[]{:S(2)}) copy-start(f32[128,512]{1,0:T(8,128)} %constant.9.clone.ghost) | copy-start | bytes 786436
  5.1 5.1 %copy-start.5 = (f32[21,21]{1,0:T(8,128)S(1)}, f32[21,21]{1,0:T(8,128)}, u32[]{:S(2)}) copy-start(f32[21,21]{1,0:T(8,128)} %rate.1) | copy-start | bytes 5296
  5.1 5.1 %copy-start.6 = (s32[1,1,2]{2,1,0:T(1,128)S(1)}, s32[1,1,2]{2,1,0:T(1,128)}, u32[]{:S(2)}) copy-start(s32[1,1,2]{2,1,0:T(1,128)} %param.14) | copy-start | bytes 28
  5.1 5.1 %copy-start.7 = (f32[21]{0:T(128)S(1)}, f32[21]{0:T(128)}, u32[]{:S(2)}) copy-start(f32[21]{0:T(128)} %param.12) | copy-start | bytes 256
  5.2 7.7 %collective-permute-start.1 = (bf16[128,384]{1,0:T(8,128)(2,1)S(1)}, bf16[128,384]{1,0:T(8,128)(2,1)S(1)}, u32[]{:S(2)}, u32[]{:S(2)}) collective-permute-start(bf16[128,384]{1,0:T(8,128)(2,1)S(1)} %pack_x.2.after), channel_id=1, source_target_pairs={{0,4},{4,8},{8,12},{12,16},{16,20},{20,24},{24,28},{28,0},{1,5},{5... | collective-permute-start | bytes 294920 | tf_op jit(solution)/shard_map/ppermute | solution.py:764
  6.8 6.1 %copy-start.8 = (s32[1,1,2]{2,1,0:T(1,128)S(1)}, s32[1,1,2]{2,1,0:T(1,128)}, u32[]{:S(2)}) copy-start(s32[1,1,2]{2,1,0:T(1,128)} %param.15) | copy-start | bytes 28
  6.8 6.8 %collective-permute-start.2 = (bf16[128,384]{1,0:T(8,128)(2,1)S(1)}, bf16[128,384]{1,0:T(8,128)(2,1)S(1)}, u32[]{:S(2)}, u32[]{:S(2)}) collective-permute-start(bf16[128,384]{1,0:T(8,128)(2,1)S(1)} %pack_x.3.after), channel_id=1, source_target_pairs={{0,28},{4,0},{8,4},{12,8},{16,12},{20,16},{24,20},{28,24},{1,29},{... | collective-permute-start | bytes 294920 | tf_op jit(solution)/shard_map/ppermute | solution.py:765
  10.1 3.5 %collective-permute-start.4 = (bf16[21,512]{1,0:T(8,128)(2,1)S(1)}, bf16[21,512]{1,0:T(8,128)(2,1)S(1)}, u32[]{:S(2)}, u32[]{:S(2)}) collective-permute-start(bf16[21,512]{1,0:T(8,128)(2,1)S(1)} %relay.1.after), channel_id=1, source_target_pairs={{0,3},{2,1},{3,0},{1,2},{4,7},{6,5},{7,4},{5,6},{8,11},{10,9},{11,... | collective-permute-start | bytes 64520 | tf_op jit(solution)/shard_map/ppermute | solution.py:771
  12.9 3.4 %copy-start.1 = (f32[512,256]{1,0:T(8,128)S(1)}, f32[512,256]{1,0:T(8,128)}, u32[]{:S(2)}) copy-start(f32[512,256]{1,0:T(8,128)} %constant.10.clone.average) | copy-start | bytes 1572868
  12.9 3.4 %copy-start.4 = (f32[128,256]{1,0:T(8,128)S(1)}, f32[128,256]{1,0:T(8,128)}, u32[]{:S(2)}) copy-start(f32[128,256]{1,0:T(8,128)} %constant.11.clone.place) | copy-start | bytes 393220
  14.1 4.1 %collective-permute-start.5 = (bf16[21,512]{1,0:T(8,128)(2,1)S(1)}, bf16[21,512]{1,0:T(8,128)(2,1)S(1)}, u32[]{:S(2)}, u32[]{:S(2)}) collective-permute-start(bf16[21,512]{1,0:T(8,128)(2,1)S(1)} %get-tuple-element.37), channel_id=1, source_target_pairs={{0,2},{1,3},{2,0},{3,1},{4,6},{5,7},{6,4},{7,5},{8,10},{9,11},{10,... | collective-permute-start | bytes 64520 | tf_op jit(solution)/shard_map/ppermute | solution.py:790
  14.7 3.5 %collective-permute-start.6 = (bf16[21,512]{1,0:T(8,128)(2,1)S(1)}, bf16[21,512]{1,0:T(8,128)(2,1)S(1)}, u32[]{:S(2)}, u32[]{:S(2)}) collective-permute-start(bf16[21,512]{1,0:T(8,128)(2,1)S(1)} %get-tuple-element.38), channel_id=1, source_target_pairs={{0,3},{1,2},{2,1},{3,0},{4,7},{5,6},{6,5},{7,4},{8,11},{9,10},{10,... | collective-permute-start | bytes 64520 | tf_op jit(solution)/shard_map/ppermute | solution.py:790
  15.4 2.9 %collective-permute-start.7 = (bf16[21,512]{1,0:T(8,128)(2,1)S(1)}, bf16[21,512]{1,0:T(8,128)(2,1)S(1)}, u32[]{:S(2)}, u32[]{:S(2)}) collective-permute-start(bf16[21,512]{1,0:T(8,128)(2,1)S(1)} %get-tuple-element.39), channel_id=1, source_target_pairs={{0,1},{1,0},{2,3},{3,2},{4,5},{5,4},{6,7},{7,6},{8,9},{9,8},{10,11... | collective-permute-start | bytes 64520 | tf_op jit(solution)/shard_map/ppermute | solution.py:790

commit v9 on v7

--- a/solution.py
+++ b/solution.py
@@ -689,7 +689,7 @@
 
 
 def return_order(count):
-    return [0, 2, 3, 1] if count == 4 else list(range(count))
+    return [0, 2, 1, 3] if count == 4 else list(range(count))
 
 
 def unpack_kernel(*refs):

time: 19.1 us -> 19.4 us (1.016)
  waiting for transfers between devices: 1.1 us -> 1.36 us
    ppermute x3, waiting for transfers between devices: 0.21 us -> 0.48 us  [swap(): return lax.ppermute(value, 'yz', pairs)]
where the time goes in v9:
time: 19.4 us; the launch traced here: 19.3 us
  starting transfers between devices  10.3 us (53%)
  Pallas kernels  6.8 us (35%)
  waiting for transfers between devices  1.36 us (7%)
  between operations  0.8 us (4%)
    ppermute x1, starting transfers between devices, local(): lax.ppermute(x_low, 'gx', ring('gx', -1))  3.28 us
    ppermute x1, starting transfers between devices, local(): lax.ppermute(far, 'yz', mutual('yz', -1))  2.64 us
    ppermute x3, starting transfers between devices, swap(): return lax.ppermute(value, 'yz', pairs)  2.21 us
    pallas_call x1, Pallas kernels, coarse_part(): pl.pallas_call(coarse_kernel, in_specs=[vmem] * 6 + [pl.BlockSpec(memory_...  2.18 us
    pallas_call x1, Pallas kernels, correct(): pl.pallas_call(functools.partial(correct_kernel, half=half), in_specs=[vm...  1.66 us
    ppermute x1, starting transfers between devices, local(): lax.ppermute(x_high, 'gx', ring('gx', 1))  1.54 us
    pallas_call x1, Pallas kernels, pack_y(): pl.pallas_call(pack_y_kernel, in_specs=[pl.BlockSpec(memory_space=pltpu.H...  1.31 us
    ppermute x1, waiting for transfers between devices, local(): lax.ppermute(x_low, 'gx', ring('gx', -1))  0.86 us
  transfers between devices with their start and end apart: 8, of which 2 were waited for; matrix products, arithmetic and copies ran while one was open for 0% of the time, Pallas kernels for 22%

profile of v9, /device:TPU:0, one launch (start us, length us, event | category | flops | bytes accessed | tf_op | source)
XLA Modules:
  0.0 19.3 jit_solution(10945309456401483258)
XLA Ops:
  0.6 1.3 %pack_y.1 = (bf16[192,384]{1,0:T(8,128)(2,1)S(1)}, bf16[176,384]{1,0:T(8,128)(2,1)S(1)}, bf16[21,512]{1,0:T(8,128)(2,1)S(1)}) custom-call(f32[6,6,21,384]{3,2,1,0:T(8,128)} %bitcast.7, bf16[21,4,512]{2,1,0:T(4,128)(2,1)} %bitcast.22), custom_call_target="tpu_custom_call" | custom-call | tf_op jit(solution)/shard_map/pack_y/pallas_call | solution.py:238
  2.0 0.5 %collective-permute-start = (bf16[192,384]{1,0:T(8,128)(2,1)S(1)}, bf16[192,384]{1,0:T(8,128)(2,1)S(1)}, u32[]{:S(2)}, u32[]{:S(2)}) collective-permute-start(bf16[192,384]{1,0:T(8,128)(2,1)S(1)} %get-tuple-element.21), channel_id=1, source_target_pairs={{0,1},{2,3},{1,0},{3,2},{4,5},{6,7},{5,4},{7,6},{8,9},{10,11},{9,8... | collective-permute-start | bytes 442376 | tf_op jit(solution)/shard_map/ppermute | solution.py:764
  2.5 2.6 %collective-permute-start.3 = (bf16[176,384]{1,0:T(8,128)(2,1)S(1)}, bf16[176,384]{1,0:T(8,128)(2,1)S(1)}, u32[]{:S(2)}, u32[]{:S(2)}) collective-permute-start(bf16[176,384]{1,0:T(8,128)(2,1)S(1)} %get-tuple-element.24), channel_id=1, source_target_pairs={{0,3},{2,1},{3,0},{1,2},{4,7},{6,5},{7,4},{5,6},{8,11},{10,9},{11,... | collective-permute-start | bytes 405512 | tf_op jit(solution)/shard_map/ppermute | solution.py:765
  5.1 0.0 copy-start.6
  5.1 0.0 copy-start.7
  5.2 1.5 %collective-permute-start.1 = (bf16[128,384]{1,0:T(8,128)(2,1)S(1)}, bf16[128,384]{1,0:T(8,128)(2,1)S(1)}, u32[]{:S(2)}, u32[]{:S(2)}) collective-permute-start(bf16[128,384]{1,0:T(8,128)(2,1)S(1)} %pack_x.2.after), channel_id=1, source_target_pairs={{0,4},{4,8},{8,12},{12,16},{16,20},{20,24},{24,28},{28,0},{1,5},{5... | collective-permute-start | bytes 294920 | tf_op jit(solution)/shard_map/ppermute | solution.py:762
  6.8 0.0 copy-start.8
  6.8 3.3 %collective-permute-start.2 = (bf16[128,384]{1,0:T(8,128)(2,1)S(1)}, bf16[128,384]{1,0:T(8,128)(2,1)S(1)}, u32[]{:S(2)}, u32[]{:S(2)}) collective-permute-start(bf16[128,384]{1,0:T(8,128)(2,1)S(1)} %pack_x.3.after), channel_id=1, source_target_pairs={{0,28},{4,0},{8,4},{12,8},{16,12},{20,16},{24,20},{28,24},{1,29},{... | collective-permute-start | bytes 294920 | tf_op jit(solution)/shard_map/ppermute | solution.py:763
  10.1 0.0 collective-permute-done.near
  10.1 0.1 collective-permute-start.4
  10.2 2.2 %coarse_part.1 = (f32[36,24,384]{2,1,0:T(8,128)S(1)}, f32[48,256]{1,0:T(8,128)S(1)}, f32[48,256]{1,0:T(8,128)S(1)}, bf16[96,96]{1,0:T(8,128)(2,1)S(1)}, bf16[256...) custom-call(s32[1,2]{1,0:T(1,128)S(1)} %bitcast.11, f32[6,6,21,384]{3,2,1,0:T(8,128)S(1)} %bitcast.10, ...), custom_call_target="tpu_custom_call" | custom-call | flops 232243200 | bytes 3483648 | tf_op jit(solution)/shard_map/coarse_part/pallas_call | solution.py:360
  12.4 0.0 copy-start.1
  12.4 0.0 copy-start.4
  12.4 0.2 %y_faces.1 = (f32[24,128]{1,0:T(8,128)S(1)}, f32[48,512]{1,0:T(8,128)S(1)}, f32[96,512]{1,0:T(8,128)S(1)}) custom-call(s32[1,2]{1,0:T(1,128)S(1)} %bitcast.12, s32[1,2]{1,0:T(1,128)S(1)} %bitcast.18, bf16[192,384]{1,0:T(8,128)(2,1)S(1)} %collective-permute-done.near, bf16[176,384]{1,0:T(8,128)(2,1)S(1)} %collective-permute-done.3.far, ...), custom_call_target="tpu_custom_call" | custom-call | flops 1000000000 | bytes 20000000 | tf_op jit(solution)/shard_map/y_faces/pallas_call | solution.py:447
  12.7 0.9 %collective-permute-done.2.x_high.x_second = bf16[128,384]{1,0:T(8,128)(2,1)S(1)} collective-permute-done((bf16[128,384]{1,0:T(8,128)(2,1)S(1)}, bf16[128,384]{1,0:T(8,128)(2,1)S(1)}, u32[]{:S(2)}, u32[]{:S(2)}) %collective-permute-start.2) | collective-permute-done | bytes 98336 | tf_op jit(solution)/shard_map/ppermute | solution.py:763
  13.6 0.6 %fine_part.1 = (bf16[21,512]{1,0:T(8,128)(2,1)S(1)}, bf16[21,512]{1,0:T(8,128)(2,1)S(1)}, bf16[21,512]{1,0:T(8,128)(2,1)S(1)}, bf16[21,512]{1,0:T(8,128)(2,1)S(1...) custom-call(s32[1,2]{1,0:T(1,128)S(1)} %bitcast.13, s32[1,2]{1,0:T(1,128)S(1)} %bitcast.19, ...), custom_call_target="tpu_custom_call" | custom-call | tf_op jit(solution)/shard_map/fine_part/pallas_call | solution.py:531
  14.2 0.6 %collective-permute-start.5 = (bf16[21,512]{1,0:T(8,128)(2,1)S(1)}, bf16[21,512]{1,0:T(8,128)(2,1)S(1)}, u32[]{:S(2)}, u32[]{:S(2)}) collective-permute-start(bf16[21,512]{1,0:T(8,128)(2,1)S(1)} %get-tuple-element.37), channel_id=1, source_target_pairs={{0,2},{1,3},{2,0},{3,1},{4,6},{5,7},{6,4},{7,5},{8,10},{9,11},{10,... | collective-permute-start | bytes 64520 | tf_op jit(solution)/shard_map/ppermute | solution.py:786
  14.8 0.5 %collective-permute-start.6 = (bf16[21,512]{1,0:T(8,128)(2,1)S(1)}, bf16[21,512]{1,0:T(8,128)(2,1)S(1)}, u32[]{:S(2)}, u32[]{:S(2)}) collective-permute-start(bf16[21,512]{1,0:T(8,128)(2,1)S(1)} %get-tuple-element.38), channel_id=1, source_target_pairs={{0,1},{1,0},{2,3},{3,2},{4,5},{5,4},{6,7},{7,6},{8,9},{9,8},{10,11... | collective-permute-start | bytes 64520 | tf_op jit(solution)/shard_map/ppermute | solution.py:786
  15.2 1.2 %collective-permute-start.7 = (bf16[21,512]{1,0:T(8,128)(2,1)S(1)}, bf16[21,512]{1,0:T(8,128)(2,1)S(1)}, u32[]{:S(2)}, u32[]{:S(2)}) collective-permute-start(bf16[21,512]{1,0:T(8,128)(2,1)S(1)} %get-tuple-element.39), channel_id=1, source_target_pairs={{0,3},{1,2},{2,1},{3,0},{4,7},{5,6},{6,5},{7,4},{8,11},{9,10},{10,... | collective-permute-start | bytes 64520 | tf_op jit(solution)/shard_map/ppermute | solution.py:786
  16.4 1.7 %coarse_correct.1 = f32[6,6,21,384]{3,2,1,0:T(8,128)} custom-call(s32[1,2]{1,0:T(1,128)S(1)} %bitcast.14, f32[36,24,384]{2,1,0:T(8,128)S(1)} %get-tuple-element.23.adv, bf16[128,384]{1,0:T(8,128)(2,1)S(1)} %collective-permute-done.1.x_low.x_first, bf16[128,384]{1,0:T(8,128)(2,1)S(1)} %collective-permute-done.2.x_high.x_second, ...), custom_call_target="tpu_custom_call" | custom-call | flops 6635520 | bytes 3981312 | tf_op jit(solution)/shard_map/coarse_correct/pallas_call | solution.py:660
  18.1 0.0 collective-permute-done.5.refs_1_
  18.1 0.0 collective-permute-done.6.refs_2_
  18.1 0.5 %collective-permute-done.7.refs_3_ = bf16[21,512]{1,0:T(8,128)(2,1)S(1)} collective-permute-done((bf16[21,512]{1,0:T(8,128)(2,1)S(1)}, bf16[21,512]{1,0:T(8,128)(2,1)S(1)}, u32[]{:S(2)}, u32[]{:S(2)}) %collective-permute-start.7) | collective-permute-done | bytes 21536 | tf_op jit(solution)/shard_map/ppermute | solution.py:786
  18.6 0.7 %unpack.1 = bf16[21,4,512]{2,1,0:T(4,128)(2,1)} custom-call(bf16[21,512]{1,0:T(8,128)(2,1)S(1)} %get-tuple-element.36.refs_0_, bf16[21,512]{1,0:T(8,128)(2,1)S(1)} %collective-permute-done.5.refs_1_, bf16[21,512]{1,0:T(8,128)(2,1)S(1)} %collective-permute-done.6.refs_2_, bf16[21,512]{1,0:T(8,128)(2,1)S(1)} %collective-permute-done.7.refs_3_), custom_call_target="tpu_custom_call" | custom-call | tf_op jit(solution)/shard_map/unpack/pallas_call | solution.py:716
  (19 shorter events, 0.1 us)
Async XLA Ops:
  0.6 4.5 %copy-start = (f32[21,6,6,384]{3,0,2,1:T(8,128)S(1)}, f32[21,6,6,384]{3,0,2,1:T(8,128)}, u32[]{:S(2)}) copy-start(f32[21,6,6,384]{3,0,2,1:T(8,128)} %param.10) | copy-start | bytes 3483652
  2.0 8.1 %collective-permute-start = (bf16[192,384]{1,0:T(8,128)(2,1)S(1)}, bf16[192,384]{1,0:T(8,128)(2,1)S(1)}, u32[]{:S(2)}, u32[]{:S(2)}) collective-permute-start(bf16[192,384]{1,0:T(8,128)(2,1)S(1)} %get-tuple-element.21), channel_id=1, source_target_pairs={{0,1},{2,3},{1,0},{3,2},{4,5},{6,7},{5,4},{7,6},{8,9},{10,11},{9,8... | collective-permute-start | bytes 442376 | tf_op jit(solution)/shard_map/ppermute | solution.py:764
  2.5 9.9 %collective-permute-start.3 = (bf16[176,384]{1,0:T(8,128)(2,1)S(1)}, bf16[176,384]{1,0:T(8,128)(2,1)S(1)}, u32[]{:S(2)}, u32[]{:S(2)}) collective-permute-start(bf16[176,384]{1,0:T(8,128)(2,1)S(1)} %get-tuple-element.24), channel_id=1, source_target_pairs={{0,3},{2,1},{3,0},{1,2},{4,7},{6,5},{7,4},{5,6},{8,11},{10,9},{11,... | collective-permute-start | bytes 405512 | tf_op jit(solution)/shard_map/ppermute | solution.py:765
  5.1 5.0 %copy-start.2 = (f32[256,512]{1,0:T(8,128)S(1)}, f32[256,512]{1,0:T(8,128)}, u32[]{:S(2)}) copy-start(f32[256,512]{1,0:T(8,128)} %constant.8.clone.spread) | copy-start | bytes 1572868
  5.1 5.1 %copy-start.3 = (f32[128,512]{1,0:T(8,128)S(1)}, f32[128,512]{1,0:T(8,128)}, u32[]{:S(2)}) copy-start(f32[128,512]{1,0:T(8,128)} %constant.9.clone.ghost) | copy-start | bytes 786436
  5.1 5.1 %copy-start.5 = (f32[21,21]{1,0:T(8,128)S(1)}, f32[21,21]{1,0:T(8,128)}, u32[]{:S(2)}) copy-start(f32[21,21]{1,0:T(8,128)} %rate.1) | copy-start | bytes 5296
  5.1 5.1 %copy-start.6 = (s32[1,1,2]{2,1,0:T(1,128)S(1)}, s32[1,1,2]{2,1,0:T(1,128)}, u32[]{:S(2)}) copy-start(s32[1,1,2]{2,1,0:T(1,128)} %param.14) | copy-start | bytes 28
  5.1 5.1 %copy-start.7 = (f32[21]{0:T(128)S(1)}, f32[21]{0:T(128)}, u32[]{:S(2)}) copy-start(f32[21]{0:T(128)} %param.12) | copy-start | bytes 256
  5.2 8.4 %collective-permute-start.1 = (bf16[128,384]{1,0:T(8,128)(2,1)S(1)}, bf16[128,384]{1,0:T(8,128)(2,1)S(1)}, u32[]{:S(2)}, u32[]{:S(2)}) collective-permute-start(bf16[128,384]{1,0:T(8,128)(2,1)S(1)} %pack_x.2.after), channel_id=1, source_target_pairs={{0,4},{4,8},{8,12},{12,16},{16,20},{20,24},{24,28},{28,0},{1,5},{5... | collective-permute-start | bytes 294920 | tf_op jit(solution)/shard_map/ppermute | solution.py:762
  6.8 5.6 %copy-start.8 = (s32[1,1,2]{2,1,0:T(1,128)S(1)}, s32[1,1,2]{2,1,0:T(1,128)}, u32[]{:S(2)}) copy-start(s32[1,1,2]{2,1,0:T(1,128)} %param.15) | copy-start | bytes 28
  6.8 6.8 %collective-permute-start.2 = (bf16[128,384]{1,0:T(8,128)(2,1)S(1)}, bf16[128,384]{1,0:T(8,128)(2,1)S(1)}, u32[]{:S(2)}, u32[]{:S(2)}) collective-permute-start(bf16[128,384]{1,0:T(8,128)(2,1)S(1)} %pack_x.3.after), channel_id=1, source_target_pairs={{0,28},{4,0},{8,4},{12,8},{16,12},{20,16},{24,20},{28,24},{1,29},{... | collective-permute-start | bytes 294920 | tf_op jit(solution)/shard_map/ppermute | solution.py:763
  10.1 3.5 %collective-permute-start.4 = (bf16[21,512]{1,0:T(8,128)(2,1)S(1)}, bf16[21,512]{1,0:T(8,128)(2,1)S(1)}, u32[]{:S(2)}, u32[]{:S(2)}) collective-permute-start(bf16[21,512]{1,0:T(8,128)(2,1)S(1)} %relay.1.after), channel_id=1, source_target_pairs={{0,3},{2,1},{3,0},{1,2},{4,7},{6,5},{7,4},{5,6},{8,11},{10,9},{11,... | collective-permute-start | bytes 64520 | tf_op jit(solution)/shard_map/ppermute | solution.py:769
  12.4 4.0 %copy-start.1 = (f32[512,256]{1,0:T(8,128)S(1)}, f32[512,256]{1,0:T(8,128)}, u32[]{:S(2)}) copy-start(f32[512,256]{1,0:T(8,128)} %constant.10.clone.average) | copy-start | bytes 1572868
  12.4 4.0 %copy-start.4 = (f32[128,256]{1,0:T(8,128)S(1)}, f32[128,256]{1,0:T(8,128)}, u32[]{:S(2)}) copy-start(f32[128,256]{1,0:T(8,128)} %constant.11.clone.place) | copy-start | bytes 393220
  14.2 3.9 %collective-permute-start.5 = (bf16[21,512]{1,0:T(8,128)(2,1)S(1)}, bf16[21,512]{1,0:T(8,128)(2,1)S(1)}, u32[]{:S(2)}, u32[]{:S(2)}) collective-permute-start(bf16[21,512]{1,0:T(8,128)(2,1)S(1)} %get-tuple-element.37), channel_id=1, source_target_pairs={{0,2},{1,3},{2,0},{3,1},{4,6},{5,7},{6,4},{7,5},{8,10},{9,11},{10,... | collective-permute-start | bytes 64520 | tf_op jit(solution)/shard_map/ppermute | solution.py:786
  14.8 3.3 %collective-permute-start.6 = (bf16[21,512]{1,0:T(8,128)(2,1)S(1)}, bf16[21,512]{1,0:T(8,128)(2,1)S(1)}, u32[]{:S(2)}, u32[]{:S(2)}) collective-permute-start(bf16[21,512]{1,0:T(8,128)(2,1)S(1)} %get-tuple-element.38), channel_id=1, source_target_pairs={{0,1},{1,0},{2,3},{3,2},{4,5},{5,4},{6,7},{7,6},{8,9},{9,8},{10,11... | collective-permute-start | bytes 64520 | tf_op jit(solution)/shard_map/ppermute | solution.py:786
  15.2 3.3 %collective-permute-start.7 = (bf16[21,512]{1,0:T(8,128)(2,1)S(1)}, bf16[21,512]{1,0:T(8,128)(2,1)S(1)}, u32[]{:S(2)}, u32[]{:S(2)}) collective-permute-start(bf16[21,512]{1,0:T(8,128)(2,1)S(1)} %get-tuple-element.39), channel_id=1, source_target_pairs={{0,3},{1,2},{2,1},{3,0},{4,7},{5,6},{6,5},{7,4},{8,11},{9,10},{10,... | collective-permute-start | bytes 64520 | tf_op jit(solution)/shard_map/ppermute | solution.py:786
